TPU v7x, 32 devices: a whole 2x2x4 slice. The times are simulated.
32 devices in a mesh: seq: 2 (over y), ctx: 16 (over z, x, core).
Axes of the slice: x: 2, y: 2, z: 4, core: 2. Of those that a mesh axis runs over, the one named last changes fastest.
Arguments:
- hidden_in: bfloat16 [2, 2048, 768], P('seq', 'ctx'), may hold values from -6 to 6
- w_qkv: bfloat16 [768, 2304], P(('seq', 'ctx')), may hold values from -0.21875 to 0.21875
- q_bias: bfloat16 [768], P(('seq', 'ctx')), may hold values from -3 to 3
- v_bias: bfloat16 [768], P(('seq', 'ctx')), may hold values from -3 to 3
- w_out: bfloat16 [768, 768], P(('seq', 'ctx')), may hold values from -0.875 to 0.875
- out_bias: bfloat16 [768], P(('seq', 'ctx')), may hold values from -2 to 2
- w_up: bfloat16 [768, 3072], P(('seq', 'ctx')), may hold values from -0.21875 to 0.21875
- up_bias: bfloat16 [3072], P(('seq', 'ctx')), may hold values from -2 to 2
- w_down: bfloat16 [3072, 768], P(('seq', 'ctx')), may hold values from -0.15625 to 0.15625
- down_bias: bfloat16 [768], P(('seq', 'ctx')), may hold values from -2 to 2
- ln1_gain: bfloat16 [768], P(('seq', 'ctx')), may hold values from 0.5 to 1.5
- ln1_bias: bfloat16 [768], P(('seq', 'ctx')), may hold values from -2 to 2
- ln2_gain: bfloat16 [768], P(('seq', 'ctx')), may hold values from 0.5 to 1.5
- ln2_bias: bfloat16 [768], P(('seq', 'ctx')), may hold values from -2 to 2
- segment_ids: int32 [2, 2048], P('seq', 'ctx'), may hold values from 0 to 4, as said below
- padding_mask: int32 [2, 2048], P('seq', 'ctx'), may hold values from 0 to 1, as said below
- teacher: bfloat16 [2, 2048, 768], P('seq', 'ctx'), may hold values from -6 to 6
- cotangent: bfloat16 [2, 2048, 768], P('seq', 'ctx'), may hold values from -6 to 6
Outputs:
- layer_out: bfloat16 [2, 2048, 768], P('seq', 'ctx')
- loss: float32 [], replicated
- input_grad: float32 [2, 2048, 768], P('seq', 'ctx')
- grad_w_qkv: float32 [768, 2304], P(('seq', 'ctx'))
- grad_q_bias: float32 [768], P(('seq', 'ctx'))
- grad_v_bias: float32 [768], P(('seq', 'ctx'))
- grad_w_out: float32 [768, 768], P(('seq', 'ctx'))
- grad_out_bias: float32 [768], P(('seq', 'ctx'))
- grad_w_up: float32 [768, 3072], P(('seq', 'ctx'))
- grad_up_bias: float32 [3072], P(('seq', 'ctx'))
- grad_w_down: float32 [3072, 768], P(('seq', 'ctx'))
- grad_down_bias: float32 [768], P(('seq', 'ctx'))
- grad_ln1_gain: float32 [768], P(('seq', 'ctx'))
- grad_ln1_bias: float32 [768], P(('seq', 'ctx'))
- grad_ln2_gain: float32 [768], P(('seq', 'ctx'))
- grad_ln2_bias: float32 [768], P(('seq', 'ctx'))
Inputs may be any that keep to these rules, and one draw needn't show every extreme that they name: `segment_ids`: in each sequence the ids never fall and each of the 5 documents holds one token or more; document 2 begins within the first 128 tokens and ends within the last 128 tokens. `padding_mask`: in each sequence the tokens with 1 come first, the padding after them.
All inputs are finite; a program needn't handle non-finite values.
Results may differ from a plain program's by a relative error of at most 0.014.
Values may be sent and summed in bfloat16 or wider, within the bound.
No kernel may reach another device: no remote copies, remote signals or barrier semaphores. Data moves between devices by JAX's collectives and lax.ppermute only.
A program may use at most 192 MiB of HBM per device.

v0:
```python
import functools

import jax
import jax.numpy as jnp
from jax import lax
from jax.experimental import pallas as pl
from jax.experimental.pallas import tpu as pltpu
from jax.sharding import Mesh
from jax.sharding import PartitionSpec as P

HEADS = 12
HEAD_DIM = 64
ZS = 4
BF = jnp.bfloat16
F32 = jnp.float32
NEG = -1e30
LANES = 128


def shift(value, axis, step):
    size = lax.axis_size(axis)
    return lax.ppermute(value, axis, [(a, (a + step) % size) for a in range(size)])


def gather(value, axis, dim, after=()):
    size = lax.axis_size(axis)
    return arrange([value] + [shift(value, axis, d) for d in range(1, size)], lax.axis_index(axis), dim, after)


def scatter_sum(value, axis, dim, last=BF, after=()):
    size = lax.axis_size(axis)
    place = lax.axis_index(axis)

    def cut(d):
        return lax.dynamic_slice_in_dim(value, lax.rem(place + d, size), 1, dim)

    came = [shift(cut(d), axis, d) for d in range(1, size)]

    def body(place_ref, value_ref, *refs):
        index = (slice(None),) * dim + (pl.ds(place_ref[0], 1),)
        total = value_ref[index].astype(F32)
        for ref in refs[:size - 1]:
            total = total + ref[...].astype(F32)
        refs[-1][...] = total.astype(last)

    vmem = pl.BlockSpec(memory_space=pltpu.VMEM)
    return pl.pallas_call(
        body,
        in_specs=[pl.BlockSpec(memory_space=pltpu.SMEM)] + [vmem] * size + [pl.BlockSpec(memory_space=pl.ANY)] * len(after),
        out_shape=jax.ShapeDtypeStruct(came[0].shape, last),
        compiler_params=params(),
        cost_estimate=SMALL,
        name="scatter_sum",
    )(place.astype(jnp.int32).reshape(1), value, *came, *after)


def spread_tokens(value):
    some = [value] + [shift(value, "x", d) for d in range(1, lax.axis_size("x"))]
    return some + [shift(member, "core", 1) for member in some]


def fold_tokens(kept, sent, after=()):
    came = shift(sent, "core", 1)
    size = kept.shape[0]
    shape = kept.shape[1:]

    def body(kept_ref, came_ref, *outs):
        for d in range(size):
            outs[d][...] = (kept_ref[d] + came_ref[d].astype(F32)).astype(outs[d].dtype)

    terms = call(body, (kept, came), [(shape, BF if d else F32) for d in range(size)], "fold_tokens", 0, after)
    return [terms[0]] + [shift(terms[d], "x", -d) for d in range(1, size)]


def dot(a, b):
    return jnp.dot(a, b, preferred_element_type=F32)


def dot_nt(a, b):
    return lax.dot_general(a, b, (((1,), (1,)), ((), ())), preferred_element_type=F32)


def dot_tn(a, b):
    return lax.dot_general(a, b, (((0,), (0,)), ((), ())), preferred_element_type=F32)


SMALL = pl.CostEstimate(flops=1, bytes_accessed=1, transcendentals=0)


def params(mib=6):
    return pltpu.CompilerParams(vmem_limit_bytes=mib * 1024 * 1024)


def pack_one(w_qkv, flat, seg, mask):
    rows, width = w_qkv.shape[0], w_qkv.shape[1] // 3
    group = width // ZS
    hd = HEAD_DIM
    upc = flat.shape[0] - 8

    def body(qkv_ref, flat_ref, seg_ref, mask_ref, one_ref, vec):
        vec[...] = jnp.zeros_like(vec)
        vec[0:8 + upc, 0:rows] = flat_ref[...].astype(F32)
        count = jnp.sum(mask_ref[...].astype(F32), -1, keepdims=True)
        lane = lax.broadcasted_iota(jnp.int32, (LANES, LANES), 1)
        vec[...] = jnp.where(lane == 8 + upc, count, vec[...].T)
        ids = seg_ref[...].astype(F32)
        vec[0:1, hd:] = ids[:, 0:hd]
        vec[1:2, hd:] = ids[:, hd:]
        cols = vec[0:rows, :].astype(BF)
        for g in range(ZS):
            k = width + g * group
            v = 2 * width + g * group
            one_ref[g, :, 0:3 * hd] = qkv_ref[:, k:k + 3 * hd]
            one_ref[g, :, 3 * hd:4 * hd] = qkv_ref[:, v + 2 * hd:v + 3 * hd]
            one_ref[g, :, 4 * hd:6 * hd] = qkv_ref[:, v:v + 2 * hd]
            one_ref[g, :, 6 * hd:9 * hd] = qkv_ref[:, g * group:g * group + 3 * hd]
            one_ref[g, :, 9 * hd:11 * hd] = cols

    specs = [pl.BlockSpec(a.shape, lambda i: (0, 0)) for a in (w_qkv, flat, seg, mask)]
    return pl.pallas_call(
        body,
        grid=(1,),
        in_specs=specs,
        out_specs=pl.BlockSpec((ZS, rows, 11 * hd), lambda i: (0, 0, 0)),
        out_shape=jax.ShapeDtypeStruct((ZS, rows, 11 * hd), BF),
        scratch_shapes=[pltpu.VMEM((LANES, LANES), F32)],
        compiler_params=params(),
        cost_estimate=SMALL,
        name="pack_one",
    )(w_qkv, flat, seg, mask)


def pack_up(w_up, w_out, ffd, sx):
    rows, width = w_out.shape
    blocks = w_up.shape[1] // (2 * sx * ffd)
    ff = blocks * ffd

    def body(up_ref, out_ref, to_ref):
        for c in range(2):
            for x in range(sx):
                for b in range(blocks):
                    at = ((b * sx + x) * 2 + c) * ffd
                    to_ref[c, x, :, b * ffd:(b + 1) * ffd] = up_ref[:, at:at + ffd]
                to_ref[c, x, :, ff:] = out_ref[...]

    return call(body, (w_up, w_out), [((2, sx, rows, ff + width), BF)], "pack_up")[0]


def held(value, after):
    def body(value_ref, *rest):
        rest[-1][...] = value_ref[...]

    return pl.pallas_call(
        body,
        in_specs=[pl.BlockSpec(memory_space=pltpu.VMEM)] + [pl.BlockSpec(memory_space=pl.ANY)] * len(after),
        out_shape=jax.ShapeDtypeStruct(value.shape, value.dtype),
        compiler_params=params(),
        cost_estimate=SMALL,
        name="held",
    )(value, *after)


def arrange(pieces, place, dim, after=()):
    size = len(pieces)
    shape = list(pieces[0].shape)
    shape[dim] = size

    def body(place_ref, *refs):
        out = refs[-1]
        for d in range(size):
            spot = lax.rem(place_ref[0] + size - d, size)
            index = (slice(None),) * dim + (pl.ds(spot, 1),)
            out[index] = refs[d][...]

    return pl.pallas_call(
        body,
        in_specs=[pl.BlockSpec(memory_space=pltpu.SMEM)] + [pl.BlockSpec(memory_space=pltpu.VMEM)] * size + [pl.BlockSpec(memory_space=pl.ANY)] * len(after),
        out_shape=jax.ShapeDtypeStruct(tuple(shape), pieces[0].dtype),
        compiler_params=params(),
        cost_estimate=SMALL,
        name="arrange",
    )(place.astype(jnp.int32).reshape(1), *pieces, *after)


def project_kernel(place, h0, h1, h2, h3, w_ref, gain_ref, shift_ref, bkv_ref, bq_ref, n1_ref, q_ref, kv_ref):
    rows = h0.shape[0]
    hd = HEAD_DIM
    for d, piece in enumerate((h0, h1, h2, h3)):
        spot = pl.ds(pl.multiple_of(lax.rem(place[0] + ZS - d, ZS) * rows, rows), rows)
        values = piece[...].astype(F32)
        centered = values - jnp.mean(values, -1, keepdims=True)
        rstd = lax.rsqrt(jnp.mean(centered * centered, -1, keepdims=True) + 1e-05)
        n1 = (centered * rstd * gain_ref[...] + shift_ref[...]).astype(BF)
        n1_ref[spot, :] = n1
        joined = dot(n1, w_ref[:, 0:9 * hd])
        kv_ref[spot, :] = (joined[:, 0:6 * hd] + bkv_ref[...]).astype(BF)
        q = (joined[:, 6 * hd:9 * hd] + bq_ref[...]).astype(BF).astype(F32) * 0.125
        q_ref[spot, 0:3 * hd] = q.astype(BF)
        q_ref[spot, 3 * hd:4 * hd] = jnp.zeros((rows, hd), BF)


def project(place, pieces, w, gain, shift_row, bkv, bq):
    total, width = ZS * pieces[0].shape[0], pieces[0].shape[1]
    outs = [((total, width), BF), ((total, 4 * HEAD_DIM), BF), ((total, 6 * HEAD_DIM), BF)]
    return call(project_kernel, (place, *pieces, w, gain, shift_row, bkv, bq), outs, "project", 1)


def fill_keys(kv_refs, keys, rows):
    for j, ref in enumerate(kv_refs):
        for z in range(ZS):
            at = (z * len(kv_refs) + j) * rows
            keys[at:at + rows, :] = ref[z * rows:(z + 1) * rows, :]


def turn_segments(order, seg_ref, turned, count):
    turned[...] = jnp.zeros_like(turned)
    for z in range(ZS):
        for j in range(count):
            turned[z * count + j:z * count + j + 1, :] = seg_ref[pl.ds(z * count + order[j], 1), :]
    queries = jnp.concatenate([turned[z * count:z * count + 1, :] for z in range(ZS)], 1)
    turned[...] = turned[...].T
    return queries


def fill_bias(order, queries, turned, bias, z, count, rows):
    for j in range(count):
        same = turned[:, z * count + j:z * count + j + 1] == queries[:, z * rows:]
        bias[j * rows:(j + 1) * rows, z * rows:] = jnp.where(same, 0.0, NEG)
        key = lax.broadcasted_iota(jnp.int32, (rows, rows), 0) + order[j] * rows
        query = lax.broadcasted_iota(jnp.int32, (rows, rows), 1) + order[0] * rows
        ok = same[:, 0:rows] & (key <= query)
        bias[j * rows:(j + 1) * rows, z * rows:(z + 1) * rows] = jnp.where(ok, 0.0, NEG)


def head_parts(q_ref, keys, z, span, lower_q, lower_k):
    at = slice(z * span, (z + 1) * span)
    k01, kv2, v01 = (keys[at, i * LANES:(i + 1) * LANES] for i in range(3))
    one = jnp.ones_like(k01)
    return (k01, k01, kv2), (jnp.where(lower_k, v01, one), jnp.where(lower_k, one, v01), jnp.where(lower_k, one, kv2))


def attend_kernel(order, q_ref, seg_ref, *rest):
    count = len(rest) - 10
    kv_refs, low_refs, (ctx_ref, tot_ref), (keys, bias, acc, turned) = rest[:count], rest[count:count + 4], rest[count + 4:count + 6], rest[count + 6:]
    total = q_ref.shape[0]
    rows = total // ZS
    span = count * rows
    fill_keys(kv_refs, keys, rows)
    queries = turn_segments(order, seg_ref, turned, count)
    lower_q = lax.broadcasted_iota(jnp.int32, (total, LANES), 1) < HEAD_DIM
    lower_k = lax.broadcasted_iota(jnp.int32, (span, LANES), 1) < HEAD_DIM
    q01, q2 = q_ref[:, 0:LANES], q_ref[:, LANES:2 * LANES]
    none = jnp.zeros_like(q01)
    qs = (jnp.where(lower_q, q01, none), jnp.where(lower_q, none, q01), q2)
    for z in range(ZS):
        fill_bias(order, queries, turned, bias, z, count, rows)
        ks, vs = head_parts(q_ref, keys, z, span, lower_q, lower_k)
        for h in range(3):
            scores = dot_nt(ks[h], qs[h][z * rows:, :]) + bias[:, z * rows:]
            expo = jnp.exp(scores).astype(BF)
            part = dot_tn(vs[h], expo)
            if z == 0:
                acc[h] = part
            else:
                acc[h, :, z * rows:] += part
    u0, u1, u2 = (acc[h].T for h in range(3))
    unnormed = jnp.where(lower_q, u0, u1)
    totals = jnp.where(lower_q, pltpu.roll(u0, HEAD_DIM, 1), pltpu.roll(u1, HEAD_DIM, 1))
    ctx = unnormed / totals
    tot_ref[:, 0:LANES] = totals
    ctx_ref[:, 0:LANES] = ctx
    ctx = pltpu.roll(u2, HEAD_DIM, 1) / u2
    tot_ref[:, LANES:] = u2
    ctx_ref[:, LANES:] = ctx
    for d in range(ZS):
        spot = pl.ds(pl.multiple_of(lax.rem(order[count] + d, ZS) * rows, rows), rows)
        low_refs[d][...] = ctx_ref[spot, 0:3 * HEAD_DIM].astype(BF)


def attend(order, q, seg, kvs, after=()):
    total = q.shape[0]
    span = len(kvs) * total // ZS
    outs = [((total // ZS, 3 * HEAD_DIM), BF)] * ZS + [((total, 2 * LANES), F32)] * 2
    scratch = [pltpu.VMEM((ZS * span, 3 * LANES), BF), pltpu.VMEM((span, total), F32), pltpu.VMEM((3, LANES, total), F32), pltpu.VMEM((LANES, LANES), F32)]
    return call(attend_kernel, (order, q, seg, *kvs), outs, "attend", 1, after, scratch, 28)


def attend_back_kernel(order, q_ref, gc0, gc1, gc2, gc3, ctx_ref, tot_ref, seg_ref, *rest):
    count = len(rest) - 9
    kv_refs, (dq_ref, kept_ref, sent_ref), (keys, bias, ge, acc, gctx_ref, turned) = rest[:count], rest[count:count + 3], rest[count + 3:]
    total = q_ref.shape[0]
    rows = total // ZS
    for d, ref in enumerate((gc0, gc1, gc2, gc3)):
        spot = pl.ds(pl.multiple_of(lax.rem(order[count] + ZS - d, ZS) * rows, rows), rows)
        gctx_ref[spot, :] = ref[...].astype(F32)
    span = count * rows
    fill_keys(kv_refs, keys, rows)
    queries = turn_segments(order, seg_ref, turned, count)
    lane = lax.broadcasted_iota(jnp.int32, (total, LANES), 1)
    lower_q = lane < HEAD_DIM
    lower_k = lax.broadcasted_iota(jnp.int32, (span, LANES), 1) < HEAD_DIM
    q01, q2 = q_ref[:, 0:LANES], q_ref[:, LANES:2 * LANES]
    none = jnp.zeros_like(q01)
    qs = (jnp.where(lower_q, q01, none), jnp.where(lower_q, none, q01), q2)
    gs = []
    g01 = gctx_ref[:, 0:LANES]
    g2 = jnp.concatenate([jnp.zeros((total, HEAD_DIM), F32), gctx_ref[:, LANES:]], 1)
    c2 = pltpu.roll(ctx_ref[:, LANES:], HEAD_DIM, 1)
    t2 = tot_ref[:, LANES:]
    t2 = jnp.where(lower_q, 1.0, pltpu.roll(t2, HEAD_DIM, 1))
    for h in range(3):
        grad = g2 if h == 2 else g01
        tot = t2 if h == 2 else tot_ref[:, 0:LANES]
        ctx = c2 if h == 2 else ctx_ref[:, 0:LANES]
        mine = lower_q if h == 0 else jnp.logical_not(lower_q)
        gu = jnp.where(mine, grad / tot, 0.0).astype(BF)
        gtot = -jnp.sum(jnp.where(mine, grad * ctx / tot, 0.0), -1, keepdims=True)
        high = gtot.astype(BF)
        low = (gtot - high.astype(F32)).astype(BF)
        first = HEAD_DIM if h == 0 else 0
        ge[h] = jnp.where(lane == first, high, jnp.where(lane == first + 1, low, gu))
        gs.append(gu)
    for z in range(ZS):
        fill_bias(order, queries, turned, bias, z, count, rows)
        ks, vs = head_parts(q_ref, keys, z, span, lower_q, lower_k)
        dk, dv = [], []
        for h in range(3):
            qz = qs[h][z * rows:, :]
            expo = jnp.exp(dot_nt(ks[h], qz) + bias[:, z * rows:])
            gprob = dot_nt(vs[h], ge[h, z * rows:, :])
            gscore = (expo * gprob).astype(BF)
            dv.append(dot(expo.astype(BF), gs[h][z * rows:, :]))
            dk.append(dot(gscore, qz))
            part = dot_tn(ks[h], gscore)
            if z == 0:
                acc[h] = part
            else:
                acc[h, :, z * rows:] += part
        parts = (dk[0] + dk[1], dk[2] + dv[2], dv[0] + dv[1])
        for j in range(count):
            to = kept_ref if j < count // 2 else sent_ref
            for i in range(3):
                to[j % (count // 2), z * rows:(z + 1) * rows, i * LANES:(i + 1) * LANES] = parts[i][j * rows:(j + 1) * rows, :].astype(to.dtype)
    upper = lax.broadcasted_iota(jnp.int32, (LANES, total), 0) >= HEAD_DIM
    dq_ref[:, 0:LANES] = (0.125 * jnp.where(upper, acc[1], acc[0])).T.astype(BF)
    dq_ref[:, LANES:] = (0.125 * acc[2]).T[:, 0:HEAD_DIM].astype(BF)


def attend_back(order, q, gctx, ctx, tot, seg, kvs, after=()):
    total = q.shape[0]
    count = len(kvs)
    span = count * total // ZS
    outs = [((total, 3 * HEAD_DIM), BF), ((count // 2, total, 6 * HEAD_DIM), F32), ((count // 2, total, 6 * HEAD_DIM), BF)]
    scratch = [
        pltpu.VMEM((ZS * span, 3 * LANES), BF),
        pltpu.VMEM((span, total), F32),
        pltpu.VMEM((3, total, LANES), BF),
        pltpu.VMEM((3, LANES, total), F32),
        pltpu.VMEM((total, 3 * HEAD_DIM), F32),
        pltpu.VMEM((LANES, LANES), F32),
    ]
    return call(attend_back_kernel, (order, q, *gctx, ctx, tot, seg, *kvs), outs, "attend_back", 1, after, scratch, 32)


def norm_parts(values):
    mean = jnp.mean(values, -1, keepdims=True)
    centered = values - mean
    rstd = lax.rsqrt(jnp.mean(centered * centered, -1, keepdims=True) + 1e-05)
    return centered * rstd, rstd


def norm_back(normed, rstd, grad, gain):
    q = grad * gain
    return rstd * (q - jnp.mean(q, -1, keepdims=True) - normed * jnp.mean(q * normed, -1, keepdims=True))


GC = 0.7978845608028654


def call(body, args, outs, name, smem=0, after=(), scratch=(), mib=16, keep=()):
    large = [i for i in keep]
    specs = [pl.BlockSpec(memory_space=pltpu.SMEM if i < smem else pl.ANY if i in large else pltpu.VMEM) for i in range(len(args))]
    count = len(args)
    fetched = [pltpu.VMEM(args[i].shape, args[i].dtype) for i in large]

    def whole(*refs):
        ins, rest = list(refs[:count]), refs[count + len(after):]
        if large:
            rest, slots, sems = rest[:-len(large) - 1], rest[-len(large) - 1:-1], rest[-1]
            copies = [pltpu.make_async_copy(ins[i], slot, sems.at[n]) for n, (i, slot) in enumerate(zip(large, slots))]
            for copy in copies:
                copy.start()
            for copy in copies:
                copy.wait()
            for i, slot in zip(large, slots):
                ins[i] = slot
        body(*ins, *rest)

    return pl.pallas_call(
        whole,
        in_specs=specs + [pl.BlockSpec(memory_space=pl.ANY)] * len(after),
        out_shape=[jax.ShapeDtypeStruct(*out) for out in outs],
        scratch_shapes=list(scratch) + fetched + ([pltpu.SemaphoreType.DMA((len(large),))] if large else []),
        compiler_params=params(mib),
        cost_estimate=SMALL,
        name=name,
    )(*args, *after)


def fold(own, came, place, dim, size, name="fold"):
    shape = list(own.shape)
    shape[dim] //= size
    part = shape[dim]

    def body(place_ref, own_ref, *refs):
        for d in range(size):
            spot = lax.rem(place_ref[0] + d, size) * part
            index = (slice(None),) * dim + (pl.ds(spot, part),)
            total = own_ref[index].astype(F32)
            for ref in refs[:len(came)]:
                total = total + ref[index].astype(F32)
            refs[len(came) + d][...] = total.astype(F32 if d == 0 else BF)

    outs = [(tuple(shape), BF if d else F32) for d in range(size)]
    return call(body, (place.astype(jnp.int32).reshape(1), own, *came), outs, name, 1)


def passed(pieces, axis):
    return [shift(pieces[d], axis, d) for d in range(1, len(pieces))]


def out_project(place, pieces, w_out, bias, hidden, gain, shift_row, at, after):
    rows, group = pieces[0].shape
    width = hidden.shape[1]

    def body(place_ref, p0, p1, p2, p3, w_ref, bias_ref, hidden_ref, gain_ref, shift_ref, res_ref, n2_ref):
        total = hidden_ref[...].astype(F32) + bias_ref[...]
        for d, piece in enumerate((p0, p1, p2, p3)):
            spot = pl.ds(pl.multiple_of(lax.rem(place_ref[0] + ZS - d, ZS) * group, group), group)
            total = total + dot(piece[...], w_ref[spot, at:at + width])
        res_ref[...] = total
        n2, _ = norm_parts(total)
        n2_ref[...] = (n2 * gain_ref[...] + shift_ref[...]).astype(BF)

    return call(body, (place, *pieces, w_out, bias, hidden, gain, shift_row), [((rows, width), F32), ((rows, width), BF)], "out_project", 1, after)


def mlp_up(blocks, weights, bias):
    rows, width = blocks[0].shape
    count = len(blocks)
    half = count // 2
    ff = bias.shape[1]

    def body(*refs):
        n2_refs, (bias_ref, w_ref), (kept_ref, sent_ref, act_ref, slope_ref) = refs[:count], refs[count:count + 2], refs[-4:]
        down_ref = refs[count + 2] if len(weights) == 2 else w_ref.at[:, ff + width:]
        for j in range(count):
            pre = dot(n2_refs[j][...], w_ref[:, 0:ff]) + bias_ref[...]
            square = pre * pre
            tanh = jnp.tanh(GC * pre * (1.0 + 0.044715 * square))
            half_one = 0.5 * (1.0 + tanh)
            act = (pre * half_one).astype(BF)
            slope_ref[j] = half_one + 0.5 * pre * (1.0 - tanh * tanh) * (GC + GC * 0.134145 * square)
            act_ref[j * rows:(j + 1) * rows, :] = act
            part = dot(act, down_ref[...])
            if j < half:
                kept_ref[j] = part
            else:
                sent_ref[j - half] = part.astype(BF)

    outs = [((half, rows, width), F32), ((half, rows, width), BF), ((count * rows, ff), BF), ((count, rows, ff), F32)]
    return call(body, (*blocks, bias, *weights), outs, "mlp_up")


def finish(terms, residual, bias, teacher, cotangent, mask, scale):
    rows, width = residual.shape
    size = len(terms)

    def body(scale_ref, *refs):
        res_ref, bias_ref, teacher_ref, cot_ref, mask_ref, out_ref, err_ref, gfin_ref, gmlp_ref = refs[size:]
        valid = jnp.broadcast_to(mask_ref[...].astype(F32), (LANES, rows)).T[:, 0:1]
        final = res_ref[...] + bias_ref[...]
        for ref in refs[:size]:
            final = final + ref[...].astype(F32)
        out_ref[...] = final.astype(BF)
        deviation = final - teacher_ref[...].astype(F32)
        err_ref[...] = jnp.sum(valid * deviation * deviation, 0, keepdims=True)
        grad = valid * (cot_ref[...].astype(F32) + deviation * scale_ref[0])
        gfin_ref[...] = grad
        gmlp_ref[...] = grad.astype(BF)

    outs = [((rows, width), BF), ((1, width), F32), ((rows, width), F32), ((rows, width), BF)]
    return call(body, (scale, *terms, residual, bias, teacher, cotangent, mask), outs, "finish", 1)


def mlp_back(grads, weights, slope):
    rows, width = grads[0].shape
    count = len(grads)
    half = count // 2
    ff = slope.shape[2]

    def body(*refs):
        g_refs, (slope_ref, w_ref), (kept_ref, sent_ref, gpre_ref) = refs[:count], refs[count:count + 2], refs[-3:]
        down_ref = refs[count + 2] if len(weights) == 2 else w_ref.at[:, ff + width:]
        for j in range(count):
            gpre = (dot_nt(g_refs[j][...], down_ref[...]) * slope_ref[j]).astype(BF)
            gpre_ref[j * rows:(j + 1) * rows, :] = gpre
            part = dot_nt(gpre, w_ref[:, 0:ff])
            if j < half:
                kept_ref[j] = part
            else:
                sent_ref[j - half] = part.astype(BF)

    outs = [((half, rows, width), F32), ((half, rows, width), BF), ((count * rows, ff), BF)]
    return call(body, (*grads, slope, *weights), outs, "mlp_back")


def mlp_weights(grads, act, blocks, gpre):
    rows, width = grads[0].shape
    count = len(grads)
    ff = act.shape[1]

    def body(*refs):
        g_refs, act_ref, n_refs, gpre_ref, outs, (g_all, n_all) = refs[:count], refs[count], refs[count + 1:2 * count + 1], refs[2 * count + 1], refs[2 * count + 2:-2], refs[-2:]
        down_ref, up_ref = (outs[0].at[:, 0:width], outs[0].at[:, width:]) if ff == width else outs[:2]
        for j in range(count):
            g_all[j * rows:(j + 1) * rows, :] = g_refs[j][...]
            n_all[j * rows:(j + 1) * rows, :] = n_refs[j][...]
        down_ref[...] = dot_tn(act_ref[...], g_all[...]).astype(BF)
        up_ref[...] = dot_tn(n_all[...], gpre_ref[...]).astype(BF)
        outs[-1][...] = jnp.sum(gpre_ref[...].astype(F32), 0, keepdims=True)

    outs = [((width, 2 * width), BF)] if ff == width else [((ff, width), BF), ((width, ff), BF)]
    scratch = [pltpu.VMEM((count * rows, width), BF)] * 2
    *grads, sums = call(body, (*grads, act, *blocks, gpre), outs + [((1, ff), F32)], "mlp_weights", scratch=scratch)
    return grads, sums


def out_back(place, terms, residual, gain, gfin, pieces, w_out, gmlp, at, after):
    rows, width = residual.shape
    group = pieces[0].shape[1]
    size = len(terms)

    def body(place_ref, *refs):
        res_ref, gain_ref, gfin_ref = refs[size:size + 3]
        p_refs, (w_ref, gmlp_ref), gres_ref, gctx_refs, (gw_ref, sums_ref) = refs[size + 3:size + 7], refs[size + 7:size + 9], refs[size + 9], refs[size + 10:size + 14], refs[size + 14:]
        gn2 = refs[0][...]
        for ref in refs[1:size]:
            gn2 = gn2 + ref[...].astype(F32)
        n2, rstd = norm_parts(res_ref[...])
        gres = gfin_ref[...] + norm_back(n2, rstd, gn2, gain_ref[...])
        gres_ref[...] = gres
        branch = gres.astype(BF)
        for d in range(ZS):
            spot = pl.ds(pl.multiple_of(lax.rem(place_ref[0] + d, ZS) * group, group), group)
            gctx_refs[d][...] = dot_nt(branch, w_ref[spot, at:at + width]).astype(BF)
        for d in range(ZS):
            spot = pl.ds(pl.multiple_of(lax.rem(place_ref[0] + ZS - d, ZS) * group, group), group)
            gw_ref[spot, :] = dot_tn(p_refs[d][...], branch).astype(BF)
        rowsum = lambda v: jnp.sum(v, 0, keepdims=True)
        sums_ref[0:1, :] = rowsum(branch.astype(F32))
        sums_ref[1:2, :] = rowsum(gmlp_ref[...].astype(F32))
        sums_ref[2:3, :] = rowsum(gn2 * n2)
        sums_ref[3:4, :] = rowsum(gn2)

    outs = [((rows, width), F32)] + [((rows, group), BF)] * ZS + [((width, width), BF), ((4, width), F32)]
    return call(body, (place, *terms, residual, gain, gfin, *pieces, w_out, gmlp), outs, "out_back", 1, after)


def join_back(place, terms, dq, w):
    total, group = dq.shape
    width = w.shape[0]
    rows = total // ZS
    size = len(terms)
    cols = 3 * group

    def body(place_ref, *refs):
        dq_ref, w_ref, gj_ref, gn1_ref = refs[size:size + 4]
        out_refs = refs[size + 4:]
        dkv = refs[0][...]
        for ref in refs[1:size]:
            dkv = dkv + ref[...].astype(F32)
        gj_ref[:, 0:2 * group] = dkv.astype(BF)
        gj_ref[:, 2 * group:] = dq_ref[...]
        gn1_ref[...] = dot_nt(gj_ref[...], w_ref[:, 0:cols])
        for d in range(ZS):
            spot = pl.ds(pl.multiple_of(lax.rem(place_ref[0] + d, ZS) * rows, rows), rows)
            out_refs[d][...] = gn1_ref[spot, :].astype(out_refs[d].dtype)

    outs = [((total, cols), BF), ((total, width), F32)] + [((rows, width), BF if d else F32) for d in range(ZS)]
    return call(body, (place, *terms, dq, w), outs, "join_back", 1)


def weights_back(place, n1, grad_joined, gn1, pieces, out_sums, up_rows, marks, gw_out, wr):
    total, cols = grad_joined.shape
    width = n1.shape[1]
    rows = total // ZS
    group = cols // 3
    upc = up_rows.shape[0]
    markc = marks.shape[0]
    chips = width // (2 * wr)
    wide = cols + LANES + width

    def body(place_ref, n1_ref, gj_ref, gn1_ref, h0, h1, h2, h3, sums_ref, up_ref, marks_ref, gw_ref, kept_ref, sent_ref, vec, full):
        gain_sum = jnp.zeros((1, width), F32)
        for d, piece in enumerate((h0, h1, h2, h3)):
            spot = pl.ds(pl.multiple_of(lax.rem(place_ref[0] + ZS - d, ZS) * rows, rows), rows)
            normed, _ = norm_parts(piece[...].astype(F32))
            gain_sum = gain_sum + jnp.sum(gn1_ref[spot, :] * normed, 0, keepdims=True)
        joined_sums = jnp.sum(gj_ref[...].astype(F32), 0, keepdims=True)
        vec[...] = jnp.zeros_like(vec)
        hd = HEAD_DIM
        for g in range(ZS):
            here = place_ref[0] == g
            at = g * group
            vec[0:1, at:at + group] = jnp.where(here, joined_sums[:, 2 * group:], 0.0)
            vec[1:2, at:at + 2 * hd] = jnp.where(here, joined_sums[:, 4 * hd:6 * hd], 0.0)
            vec[1:2, at + 2 * hd:at + 3 * hd] = jnp.where(here, joined_sums[:, 3 * hd:4 * hd], 0.0)
        vec[2:4, :] = sums_ref[0:2, :]
        vec[4:5, :] = gain_sum
        vec[5:6, :] = jnp.sum(gn1_ref[...], 0, keepdims=True)
        vec[6:8, :] = sums_ref[2:4, :]
        vec[8:8 + upc, :] = up_ref[...]
        vec[16:16 + markc, :] = marks_ref[...]
        full[:, 0:cols] = dot_tn(n1_ref[...], gj_ref[...])
        full[:, cols:cols + LANES] = vec[...].T
        full[:, cols + LANES:] = gw_ref[...].astype(F32)
        for c in range(2):
            @pl.when(place_ref[1] == c)
            def _():
                for chip in range(chips):
                    at = chip * 2 * wr
                    kept_ref[chip] = full[at + c * wr:at + (c + 1) * wr, :].astype(BF)
                    sent_ref[chip] = full[at + (1 - c) * wr:at + (2 - c) * wr, :].astype(BF)

    outs = [((chips, wr, wide), BF)] * 2
    scratch = [pltpu.VMEM((LANES, width), F32), pltpu.VMEM((width, wide), F32)]
    return call(body, (place, n1, grad_joined, gn1, *pieces, out_sums, up_rows, marks, gw_out), outs, "weights_back", 1, scratch=scratch, mib=28)


def input_back(terms, hidden, gain, grad_res):
    rows, width = hidden.shape

    def body(t0, t1, t2, t3, hidden_ref, gain_ref, gres_ref, out_ref):
        back = t0[...] + t1[...].astype(F32) + t2[...].astype(F32) + t3[...].astype(F32)
        normed, rstd = norm_parts(hidden_ref[...].astype(F32))
        out_ref[...] = gres_ref[...] + norm_back(normed, rstd, back, gain_ref[...])

    return call(body, (*terms, hidden, gain, grad_res), [((rows, width), F32)], "input_back")[0]


def unpack_one(place, pieces):
    rows, wide = pieces[0].shape[-2:]
    hd = HEAD_DIM
    group = 3 * hd
    width = ZS * group

    def body(place_ref, p0, p1, p2, p3, qkv_ref, vec_ref, out_ref, held_ref):
        for d, piece in enumerate((p0, p1, p2, p3)):
            held_ref[pl.ds(lax.rem(place_ref[0] + ZS - d, ZS), 1)] = piece[...].reshape(1, rows, wide).astype(F32)
        total = jnp.zeros((rows, LANES + width), F32)
        for g in range(ZS):
            k = width + g * group
            v = 2 * width + g * group
            qkv_ref[:, k:k + 3 * hd] = held_ref[g, :, 0:3 * hd]
            qkv_ref[:, v + 2 * hd:v + 3 * hd] = held_ref[g, :, 3 * hd:4 * hd]
            qkv_ref[:, v:v + 2 * hd] = held_ref[g, :, 4 * hd:6 * hd]
            qkv_ref[:, g * group:g * group + 3 * hd] = held_ref[g, :, 6 * hd:9 * hd]
            total = total + held_ref[g, :, 9 * hd:]
        vec_ref[...] = total[:, 0:LANES]
        out_ref[...] = total[:, LANES:]

    outs = [((rows, 3 * width), F32), ((rows, LANES), F32), ((rows, width), F32)]
    return call(body, (place, *pieces), outs, "unpack_one", 1, scratch=[pltpu.VMEM((ZS, rows, wide), F32)])


def per_device(hidden_in, w_qkv, q_bias, v_bias, w_out, out_bias, w_up, up_bias, w_down, down_bias, ln1_gain, ln1_bias, ln2_gain, ln2_bias, segment_ids, padding_mask, teacher, cotangent):
    sy, sz, sx = (lax.axis_size(a) for a in ("y", "z", "x"))
    iy, iz, ix, core = (lax.axis_index(a) for a in ("y", "z", "x", "core"))
    device = ((iy * sz + iz) * sx + ix) * 2 + core
    devices = sy * sz * sx * 2
    rows, width = hidden_in.shape[1:]
    wr = w_qkv.shape[0]
    ffd = w_down.shape[0]
    ff = sy * sz * ffd
    upc = ffd // wr
    wcols = 9 * HEAD_DIM
    group = width // sz
    place = iz.astype(jnp.int32).reshape(1)

    def from_z(value):
        return [value] + [shift(value, "z", d) for d in range(1, sz)]

    def to_z(pieces):
        return [pieces[0]] + [shift(pieces[d], "z", d) for d in range(1, sz)]

    def cut_z(value):
        return [lax.dynamic_slice_in_dim(value, lax.rem(iz + d, sz), 1, 0) for d in range(sz)]

    flat = jnp.concatenate([jnp.stack([q_bias, v_bias, out_bias, down_bias, ln1_gain, ln1_bias, ln2_gain, ln2_bias]), up_bias.reshape(upc, wr)])
    one_z = to_z(cut_z(pack_one(w_qkv, flat, segment_ids, padding_mask)))
    hidden = hidden_in[0]
    pieces = from_z(hidden)
    one = arrange(one_z, iz, 0)
    one = gather(one[None, :, None], "x", 2)
    one = gather(one, "y", 0)[:, :, :, None]
    one = gather(one, "core", 3).reshape(width, -1)

    mid = pack_up(w_up, w_out, ffd, sx)
    mid = arrange([lax.dynamic_slice_in_dim(mid, core, 1, 0), shift(lax.dynamic_slice_in_dim(mid, 1 - core, 1, 0), "core", 1)], core, 0)
    mid_x = [lax.dynamic_slice_in_dim(mid, lax.rem(ix + d, sx), 1, 1) for d in range(sx)]
    mid = arrange([mid_x[0]] + [shift(mid_x[d], "x", d) for d in range(1, sx)], ix, 1)
    weights = [mid.transpose(1, 0, 2, 3).reshape(2 * sx * wr, ff + width), w_down]
    if ff == width:
        weights = [jnp.concatenate(weights, 1)]
    weights = [lax.all_gather(member, ("y", "z"), axis=0, tiled=True) for member in weights]
    mid = weights[0]

    vec = one[:, wcols:wcols + LANES]
    vec_rows = vec[:, :16].T.astype(F32)
    qb, vb, ob, db, g1, b1, g2, b2 = (vec_rows[i][None] for i in range(8))
    ub = vec_rows[8:8 + upc].reshape(upc, sy * sz, sx * 2, wr)
    ub = lax.dynamic_index_in_dim(ub, ix * 2 + core, 2, keepdims=False).transpose(1, 0, 2).reshape(1, ff)
    count = jnp.sum(vec_rows[8 + upc]) / wr
    seg = lax.dynamic_index_in_dim(vec.reshape(sy, sz * sx * 2, wr, LANES), iy, 0, keepdims=False)[:, :2, HEAD_DIM:].astype(F32).reshape(sz * sx * 2, rows)
    qb_g = lax.dynamic_slice_in_dim(qb, iz * group, group, 1)
    vb_g = lax.dynamic_slice_in_dim(vb, iz * group, group, 1)
    bkv = jnp.concatenate([jnp.zeros((1, group), F32), vb_g[:, 2 * HEAD_DIM:], vb_g[:, :2 * HEAD_DIM]], 1)
    spots = [(lax.rem(ix + sx - d, sx), core) for d in range(sx)]
    spots = spots + [(at, 1 - core) for at, _ in spots]
    order = jnp.stack([at * 2 + c for at, c in spots] + [iz]).astype(jnp.int32)
    yplace = iy.astype(jnp.int32).reshape(1)

    n1_low, q, kv = project(place, pieces, one, g1, b1, bkv, qb_g)
    kvs = spread_tokens(kv)
    *ctx_parts, ctx, tot = attend(order, q, seg, kvs)
    ctx_parts = to_z(ctx_parts)
    residual, n2_low = out_project(place, ctx_parts, mid, ob, hidden, g2, b2, ff, after=[ub])
    n2_all = spread_tokens(n2_low)
    kept, sent, act, slope = mlp_up(n2_all, weights, ub)
    layer_out, errors, grad_final, grad_mlp = finish(fold_tokens(kept, sent), residual, db, teacher[0], cotangent[0], padding_mask, (2.0 / (count * width)).reshape(1))

    grads = spread_tokens(grad_mlp)
    kept, sent, grad_pre = mlp_back(grads, weights, slope)
    gn2_terms = fold_tokens(kept, sent)
    gw_mlp, up_sums = mlp_weights(grads, act, n2_all, grad_pre)
    gw_sums = [lax.psum_scatter(member, ("y", "z"), scatter_dimension=0, tiled=True) for member in gw_mlp]
    grad_res, *gctx, gw_out, out_sums = out_back(place, gn2_terms, residual, g2, grad_final, ctx_parts, mid, grad_mlp, ff, after=gw_mlp)
    dq, dkv_kept, dkv_sent = attend_back(order, q, to_z(gctx), ctx, tot, seg, kvs)
    dkv_terms = fold_tokens(dkv_kept, dkv_sent)
    grad_joined, gn1, *gn1_parts = join_back(place, dkv_terms, dq, one)
    input_grad = input_back(to_z(gn1_parts), hidden, g1, grad_res)

    up_rows = jnp.zeros((upc, sy * sz, sx * 2, wr), F32)
    up_rows = lax.dynamic_update_slice_in_dim(up_rows, up_sums.reshape(sy * sz, upc, wr).transpose(1, 0, 2)[:, :, None], ix * 2 + core, 2).reshape(upc, width)
    slots = -(-devices // wr)
    error = jnp.sum(errors)
    high = error.astype(BF).astype(F32)
    turn = lax.broadcasted_iota(jnp.int32, (slots, width), 1) % wr
    at = turn + wr * lax.broadcasted_iota(jnp.int32, (slots, width), 0)
    marks = jnp.concatenate([jnp.where(at == device, high, 0.0), jnp.where(turn[:1] == 0, error - high, 0.0)])
    at_zc = jnp.stack([iz, core]).astype(jnp.int32)
    kept, sent = weights_back(at_zc, n1_low, grad_joined, gn1, pieces, out_sums, up_rows, marks, gw_out, wr)
    grid = (sy, sz, sx, wr, kept.shape[-1])
    third = fold(kept.reshape(grid), [shift(sent, "core", 1).reshape(grid)], iy, 0, sy, "fold_core")
    third = fold(third[0], passed(third, "y"), ix, 2, sx, "fold_y")
    third = fold(third[0], passed(third, "x"), iz, 1, sz, "fold_x")
    third = [third[0]] + passed(third, "z")
    grad_w_qkv, sums, gw_out = unpack_one(place, third)
    sums = sums.T
    loss = jnp.sum(sums[16:17 + slots]) / (count * width)

    gw_down = gw_sums[0][:, :width].astype(F32)
    gw_up = gw_sums[-1][:, -ff:]
    gw_up = gw_up.reshape(1, 1, sx, 2, wr, ff)
    up_x = [lax.dynamic_slice_in_dim(gw_up, lax.rem(ix + d, sx), 1, 2) for d in range(sx)]
    gw_up = arrange([up_x[0]] + [shift(up_x[d], "x", d) for d in range(1, sx)], ix, 2)
    gw_up = arrange([lax.dynamic_slice_in_dim(gw_up, core, 1, 3), shift(lax.dynamic_slice_in_dim(gw_up, 1 - core, 1, 3), "core", 1)], core, 3)
    gw_up = gw_up.reshape(sx, 2, wr, sy * sz, ffd).transpose(2, 3, 0, 1, 4).reshape(wr, -1).astype(F32)
    return (
        layer_out[None], loss, input_grad[None], grad_w_qkv, sums[0], sums[1], gw_out, sums[2],
        gw_up, sums[8:8 + upc].reshape(-1), gw_down, sums[3], sums[4], sums[5], sums[6], sums[7],
    )


def solution(mesh):
    seq, ctx = mesh.shape["seq"], mesh.shape["ctx"]
    grid = Mesh(mesh.devices.reshape(seq, ZS, ctx // (2 * ZS), 2), ("y", "z", "x", "core"))
    every = ("y", "z", "x", "core")
    matrix, vector = P(every, None), P(every)
    tokens = P("y", ("z", "x", "core"), None)
    marks = P("y", ("z", "x", "core"))
    return jax.shard_map(
        per_device,
        mesh=grid,
        in_specs=(tokens, matrix, vector, vector, matrix, vector, matrix, vector, matrix, vector, vector, vector, vector, vector, marks, marks, tokens, tokens),
        out_specs=(tokens, P(), tokens, matrix, vector, vector, matrix, vector, matrix, vector, matrix, vector, vector, vector, vector, vector),
        check_vma=False,
    )
```

profile of v0, /device:TPU:0, one launch (start us, length us, event | category | flops | bytes accessed | tf_op | source)
XLA Modules:
  0.0 284.5 jit_solution(2511712100802362058)
XLA Ops:
  10.7 2.9 %collective-permute-start.16 = (bf16[2,1,24,1536]{3,2,1,0:T(8,128)(2,1)S(1)}, bf16[2,1,24,1536]{3,2,1,0:T(8,128)(2,1)S(1)}, u32[]{:S(2)}, u32[]{:S(2)}) collective-permute-start(bf16[2,1,24,1536]{3,2,1,0:T(8,128)(2,1)S(1)} %get-tuple-element.146), channel_id=1, source_target_pairs={{0,2},{2,0},{1,3},{3,1},{4,6},{6,4},{5,7},{7,5},{8,10},{10,8},{9,1... | collective-permute-start | bytes 442376 | tf_op jit(solution)/shard_map/ppermute | solution.py:22
  13.6 4.2 %collective-permute-done.16.refs_1_ = bf16[2,1,24,1536]{3,2,1,0:T(8,128)(2,1)S(1)} collective-permute-done((bf16[2,1,24,1536]{3,2,1,0:T(8,128)(2,1)S(1)}, bf16[2,1,24,1536]{3,2,1,0:T(8,128)(2,1)S(1)}, u32[]{:S(2)}, u32[]{:S(2)}) %collective-permute-start.16) | collective-permute-done | bytes 147488 | tf_op jit(solution)/shard_map/ppermute | solution.py:22
  19.3 1.9 collective-permute-start
  21.2 2.6 collective-permute-start.1
  27.7 1.6 collective-permute-start.3
  29.3 3.7 %collective-permute-done.3.refs_1_ = bf16[1,4,1,24,704]{4,3,2,1,0:T(8,128)(2,1)S(1)} collective-permute-done((bf16[1,4,1,24,704]{4,3,2,1,0:T(8,128)(2,1)S(1)}, bf16[1,4,1,24,704]{4,3,2,1,0:T(8,128)(2,1)S(1)}, u32[]{:S(2)}, u32[]{:S(2)}) %collective-permute-start.3) | collective-permute-done | bytes 135200 | tf_op jit(solution)/shard_map/ppermute | solution.py:22
  33.0 1.6 collective-permute-start.4
  34.6 7.7 %collective-permute-done.4.refs_1_ = bf16[1,4,2,24,704]{4,3,2,1,0:T(8,128)(2,1)S(1)} collective-permute-done((bf16[1,4,2,24,704]{4,3,2,1,0:T(8,128)(2,1)S(1)}, bf16[1,4,2,24,704]{4,3,2,1,0:T(8,128)(2,1)S(1)}, u32[]{:S(2)}, u32[]{:S(2)}) %collective-permute-start.4) | collective-permute-done | bytes 270368 | tf_op jit(solution)/shard_map/ppermute | solution.py:22
  42.4 1.5 collective-permute-start.6
  44.0 2.4 collective-permute-start.7
  49.4 3.9 %collective-permute-done.6.refs_2_.refs_5_ = bf16[128,768]{1,0:T(8,128)(2,1)S(1)} collective-permute-done((bf16[128,768]{1,0:T(8,128)(2,1)S(1)}, bf16[128,768]{1,0:T(8,128)(2,1)S(1)}, u32[]{:S(2)}, u32[]{:S(2)}) %collective-permute-start.6) | collective-permute-done | bytes 196640 | tf_op jit(solution)/shard_map/ppermute | solution.py:22
  53.3 8.3 %collective-permute-done.7.refs_3_.refs_6_ = bf16[128,768]{1,0:T(8,128)(2,1)S(1)} collective-permute-done((bf16[128,768]{1,0:T(8,128)(2,1)S(1)}, bf16[128,768]{1,0:T(8,128)(2,1)S(1)}, u32[]{:S(2)}, u32[]{:S(2)}) %collective-permute-start.7) | collective-permute-done | bytes 196640 | tf_op jit(solution)/shard_map/ppermute | solution.py:22
  65.1 9.6 %collective-permute-done.9.refs_4_.refs_10_ = bf16[512,384]{1,0:T(8,128)(2,1)S(1)} collective-permute-done((bf16[512,384]{1,0:T(8,128)(2,1)S(1)}, bf16[512,384]{1,0:T(8,128)(2,1)S(1)}, u32[]{:S(2)}, u32[]{:S(2)}) %collective-permute-start.9) | collective-permute-done | bytes 393248 | tf_op jit(solution)/shard_map/ppermute | solution.py:22
  76.4 4.3 %attend.1 = (bf16[128,192]{1,0:T(8,128)(2,1)S(1)}, bf16[128,192]{1,0:T(8,128)(2,1)S(1)}, bf16[128,192]{1,0:T(8,128)(2,1)S(1)}, bf16[128,192]{1,0:T(8,128)(2,1)S(...) custom-call(s32[5]{0:T(128)S(1)} %stack.57.refs_0_, bf16[512,256]{1,0:T(8,128)(2,1)S(1)} %get-tuple-element.75.refs_1_, ...), custom_call_target="tpu_custom_call" | custom-call | flops 1 | bytes 1 | tf_op jit(solution)/shard_map/attend/pallas_call | solution.py:399
  83.1 8.5 %collective-permute-start.12 = (bf16[128,192]{1,0:T(8,128)(2,1)S(1)}, bf16[128,192]{1,0:T(8,128)(2,1)S(1)}, u32[]{:S(2)}, u32[]{:S(2)}) collective-permute-start(bf16[128,192]{1,0:T(8,128)(2,1)S(1)} %get-tuple-element.78), channel_id=1, source_target_pairs={{0,4},{4,8},{8,12},{12,0},{1,5},{5,9},{9,13},{13,1},{2,6},{6,10},{... | collective-permute-start | bytes 147464 | tf_op jit(solution)/shard_map/ppermute | solution.py:22
  91.6 2.4 collective-permute-start.14
  95.3 4.5 %collective-permute-done.13.refs_3_.refs_8_ = bf16[128,192]{1,0:T(8,128)(2,1)S(1)} collective-permute-done((bf16[128,192]{1,0:T(8,128)(2,1)S(1)}, bf16[128,192]{1,0:T(8,128)(2,1)S(1)}, u32[]{:S(2)}, u32[]{:S(2)}) %collective-permute-start.13) | collective-permute-done | bytes 49184 | tf_op jit(solution)/shard_map/ppermute | solution.py:22
  101.0 2.0 copy-done
  112.1 5.3 %collective-permute-done.17.refs_1_.refs_6_ = bf16[128,768]{1,0:T(8,128)(2,1)S(1)} collective-permute-done((bf16[128,768]{1,0:T(8,128)(2,1)S(1)}, bf16[128,768]{1,0:T(8,128)(2,1)S(1)}, u32[]{:S(2)}, u32[]{:S(2)}) %collective-permute-start.17) | collective-permute-done | bytes 196640 | tf_op jit(solution)/shard_map/ppermute | solution.py:22
  118.9 2.3 mlp_up.1
  123.3 1.6 collective-permute-done.20.refs_1_
  126.4 1.5 collective-permute-start.21
  128.6 5.1 %collective-permute-done.21.refs_2_ = bf16[128,768]{1,0:T(8,128)(2,1)} collective-permute-done((bf16[128,768]{1,0:T(8,128)(2,1)}, bf16[128,768]{1,0:T(8,128)(2,1)}, u32[]{:S(2)}, u32[]{:S(2)}) %collective-permute-start.21) | collective-permute-done | bytes 196640 | tf_op jit(solution)/shard_map/ppermute | solution.py:22
  138.9 1.8 finish.1
  142.1 1.5 collective-permute-start.22
  143.6 4.6 %collective-permute-done.22.refs_1_ = bf16[128,768]{1,0:T(8,128)(2,1)S(1)} collective-permute-done((bf16[128,768]{1,0:T(8,128)(2,1)S(1)}, bf16[128,768]{1,0:T(8,128)(2,1)S(1)}, u32[]{:S(2)}, u32[]{:S(2)}) %collective-permute-start.22) | collective-permute-done | bytes 196640 | tf_op jit(solution)/shard_map/ppermute | solution.py:22
  151.1 2.8 %mlp_back.1 = (f32[2,128,768]{2,1,0:T(8,128)S(1)}, bf16[2,128,768]{2,1,0:T(8,128)(2,1)S(1)}, bf16[512,768]{1,0:T(8,128)(2,1)S(1)}) custom-call(bf16[128,768]{1,0:T(8,128)(2,1)S(1)} %get-tuple-element.89.refs_0_.refs_11_, bf16[128,768]{1,0:T(8,128)(2,1)S(1)} %collective-permute-done.22.refs_1_, bf16[128,768]{1,0:T(8,128)(2,1)S(1)} %collective-permute-done.23.refs_2_, ...), custom_call_target="tpu_custom_call" | custom-call | flops 1 | bytes 1 | tf_op jit(solution)/shard_map/mlp_back/pallas_call | solution.py:399
  159.3 1.8 collective-permute-done.25.refs_1_
  162.3 1.6 collective-permute-start.26
  163.9 5.5 %collective-permute-done.26.refs_2_ = bf16[128,768]{1,0:T(8,128)(2,1)S(1)} collective-permute-done((bf16[128,768]{1,0:T(8,128)(2,1)S(1)}, bf16[128,768]{1,0:T(8,128)(2,1)S(1)}, u32[]{:S(2)}, u32[]{:S(2)}) %collective-permute-start.26) | collective-permute-done | bytes 196640 | tf_op jit(solution)/shard_map/ppermute | solution.py:22
  169.4 1.7 copy-done.5
  176.8 2.0 collective-permute-start.28
  179.3 4.3 %collective-permute-done.27.refs_3_ = bf16[128,192]{1,0:T(8,128)(2,1)S(1)} collective-permute-done((bf16[128,192]{1,0:T(8,128)(2,1)S(1)}, bf16[128,192]{1,0:T(8,128)(2,1)S(1)}, u32[]{:S(2)}, u32[]{:S(2)}) %collective-permute-start.27) | collective-permute-done | bytes 49184 | tf_op jit(solution)/shard_map/ppermute | solution.py:22
  183.6 4.0 %collective-permute-done.28.refs_4_ = bf16[128,192]{1,0:T(8,128)(2,1)S(1)} collective-permute-done((bf16[128,192]{1,0:T(8,128)(2,1)S(1)}, bf16[128,192]{1,0:T(8,128)(2,1)S(1)}, u32[]{:S(2)}, u32[]{:S(2)}) %collective-permute-start.28) | collective-permute-done | bytes 49184 | tf_op jit(solution)/shard_map/ppermute | solution.py:22
  187.7 7.4 %attend_back.1 = (bf16[512,192]{1,0:T(8,128)(2,1)S(1)}, f32[2,512,384]{2,1,0:T(8,128)S(1)}, bf16[2,512,384]{2,1,0:T(8,128)(2,1)}) custom-call(s32[5]{0:T(128)S(1)} %copy-done.88, bf16[512,256]{1,0:T(8,128)(2,1)S(1)} %copy-done.27, bf16[128,192]{1,0:T(8,128)(2,1)S(1)} %get-tuple-element.99.refs_2_, bf16[128,192]{1,0:T(8,128)(2,1)S(1)} %collective-permute-done.27.refs_3_, ...), custom_call_target="tpu_custom_call" | custom-call | flops 1 | bytes 1 | tf_op jit(solution)/shard_map/attend_back/pallas_call | solution.py:399
  204.4 9.2 %collective-permute-done.31.refs_2_ = bf16[512,384]{1,0:T(8,128)(2,1)S(1)} collective-permute-done((bf16[512,384]{1,0:T(8,128)(2,1)}, bf16[512,384]{1,0:T(8,128)(2,1)S(1)}, u32[]{:S(2)}, u32[]{:S(2)}) %collective-permute-start.31) | collective-permute-done | bytes 393248 | tf_op jit(solution)/shard_map/ppermute | solution.py:22
  217.9 2.5 weights_back.1
  220.4 2.8 collective-permute-done.32
  223.6 15.4 %collective-permute-done.33.refs_2_ = bf16[1,4,2,24,1472]{4,3,2,1,0:T(8,128)(2,1)S(1)} collective-permute-done((bf16[1,4,2,24,1472]{4,3,2,1,0:T(8,128)(2,1)S(1)}, bf16[1,4,2,24,1472]{4,3,2,1,0:T(8,128)(2,1)S(1)}, u32[]{:S(2)}, u32[]{:S(2)}) %collective-permute-start.33) | collective-permute-done | bytes 565280 | tf_op jit(solution)/shard_map/ppermute | solution.py:22
  239.1 1.6 collective-permute-start.34
  240.7 3.9 %collective-permute-start.38 = (bf16[128,768]{1,0:T(8,128)(2,1)S(1)}, bf16[128,768]{1,0:T(8,128)(2,1)S(1)}, u32[]{:S(2)}, u32[]{:S(2)}) collective-permute-start(bf16[128,768]{1,0:T(8,128)(2,1)S(1)} %get-tuple-element.128), channel_id=1, source_target_pairs={{0,4},{4,8},{8,12},{12,0},{1,5},{5,9},{9,13},{13,1},{2,6},{6,10},{... | collective-permute-start | bytes 589832 | tf_op jit(solution)/shard_map/ppermute | solution.py:22
  245.2 1.7 collective-permute-start.40
  247.4 3.9 %collective-permute-start.35 = (bf16[1,1,1,24,1472]{4,3,2,1,0:T(8,128)(2,1)S(1)}, bf16[1,1,1,24,1472]{4,3,2,1,0:T(8,128)(2,1)S(1)}, u32[]{:S(2)}, u32[]{:S(2)}) collective-permute-start(bf16[1,1,1,24,1472]{4,3,2,1,0:T(8,128)(2,1)S(1)} %get-tuple-element.123), channel_id=1, source_target_pairs={{0,4},{4,8},{8,12},{12,0},{1,5},{5,9},{9,13},{13,1},{2,6},{6,10},{... | collective-permute-start | bytes 211976 | tf_op jit(solution)/shard_map/ppermute | solution.py:22
  251.9 1.9 collective-permute-start.37
  253.8 5.0 %collective-permute-done.39.refs_2_ = bf16[128,768]{1,0:T(8,128)(2,1)S(1)} collective-permute-done((bf16[128,768]{1,0:T(8,128)(2,1)S(1)}, bf16[128,768]{1,0:T(8,128)(2,1)S(1)}, u32[]{:S(2)}, u32[]{:S(2)}) %collective-permute-start.39) | collective-permute-done | bytes 196640 | tf_op jit(solution)/shard_map/ppermute | solution.py:22
  260.3 5.9 %collective-permute-done.36.refs_3_ = bf16[1,1,1,24,1472]{4,3,2,1,0:T(8,128)(2,1)S(1)} collective-permute-done((bf16[1,1,1,24,1472]{4,3,2,1,0:T(8,128)(2,1)S(1)}, bf16[1,1,1,24,1472]{4,3,2,1,0:T(8,128)(2,1)S(1)}, u32[]{:S(2)}, u32[]{:S(2)}) %collective-permute-start.36) | collective-permute-done | bytes 70688 | tf_op jit(solution)/shard_map/ppermute | solution.py:22
  267.2 1.7 slice_convert_fusion
  271.4 1.9 collective-permute-done.41.refs_1_
  (345 shorter events, 80.1 us)
Async XLA Ops:
  7.2 93.8 %all-gather.2.cloned.1.call-start = ((), (), s32[]{:S(2)}) async-start(), calls=%async_computation.1 | async-start | bytes 3981312 | tf_op jit(solution)/shard_map/all_gather | solution.py:716
  9.1 1.5 collective-permute-start.15
  10.7 7.1 %collective-permute-start.16 = (bf16[2,1,24,1536]{3,2,1,0:T(8,128)(2,1)S(1)}, bf16[2,1,24,1536]{3,2,1,0:T(8,128)(2,1)S(1)}, u32[]{:S(2)}, u32[]{:S(2)}) collective-permute-start(bf16[2,1,24,1536]{3,2,1,0:T(8,128)(2,1)S(1)} %get-tuple-element.146), channel_id=1, source_target_pairs={{0,2},{2,0},{1,3},{3,1},{4,6},{6,4},{5,7},{7,5},{8,10},{10,8},{9,1... | collective-permute-start | bytes 442376 | tf_op jit(solution)/shard_map/ppermute | solution.py:22
  18.8 248.4 %reduce-scatter.2.cloned.1.call-start = ((), (), s32[]{:S(2)}) async-start(), calls=%async_computation.2 | async-start | bytes 2654208 | tf_op jit(solution)/shard_map/reduce_scatter | solution.py:747
  19.3 6.4 %collective-permute-start = (bf16[1,24,704]{2,1,0:T(8,128)(2,1)S(1)}, bf16[1,24,704]{2,1,0:T(8,128)(2,1)S(1)}, u32[]{:S(2)}, u32[]{:S(2)}) collective-permute-start(bf16[1,24,704]{2,1,0:T(8,128)(2,1)S(1)} %get-tuple-element.156), channel_id=1, source_target_pairs={{0,4},{4,8},{8,12},{12,0},{1,5},{5,9},{9,13},{13,1},{2,6},{6,10},{... | collective-permute-start | bytes 101384 | tf_op jit(solution)/shard_map/ppermute | solution.py:22
  21.2 5.1 %collective-permute-start.1 = (bf16[1,24,704]{2,1,0:T(8,128)(2,1)S(1)}, bf16[1,24,704]{2,1,0:T(8,128)(2,1)S(1)}, u32[]{:S(2)}, u32[]{:S(2)}) collective-permute-start(bf16[1,24,704]{2,1,0:T(8,128)(2,1)S(1)} %get-tuple-element.155), channel_id=1, source_target_pairs={{0,8},{4,12},{8,0},{12,4},{1,9},{5,13},{9,1},{13,5},{2,10},{6,14},... | collective-permute-start | bytes 101384 | tf_op jit(solution)/shard_map/ppermute | solution.py:22
  23.8 4.0 %collective-permute-start.2 = (bf16[1,24,704]{2,1,0:T(8,128)(2,1)S(1)}, bf16[1,24,704]{2,1,0:T(8,128)(2,1)S(1)}, u32[]{:S(2)}, u32[]{:S(2)}) collective-permute-start(bf16[1,24,704]{2,1,0:T(8,128)(2,1)S(1)} %get-tuple-element.154), channel_id=1, source_target_pairs={{0,12},{4,0},{8,4},{12,8},{1,13},{5,1},{9,5},{13,9},{2,14},{6,2},{... | collective-permute-start | bytes 101384 | tf_op jit(solution)/shard_map/ppermute | solution.py:22
  27.7 5.2 %collective-permute-start.3 = (bf16[1,4,1,24,704]{4,3,2,1,0:T(8,128)(2,1)S(1)}, bf16[1,4,1,24,704]{4,3,2,1,0:T(8,128)(2,1)S(1)}, u32[]{:S(2)}, u32[]{:S(2)}) collective-permute-start(bf16[1,4,1,24,704]{4,3,2,1,0:T(8,128)(2,1)S(1)} %bitcast.66), channel_id=1, source_target_pairs={{0,2},{2,0},{1,3},{3,1},{4,6},{6,4},{5,7},{7,5},{8,10},{10,8},{9,1... | collective-permute-start | bytes 405512 | tf_op jit(solution)/shard_map/ppermute | solution.py:22
  33.0 9.3 %collective-permute-start.4 = (bf16[1,4,2,24,704]{4,3,2,1,0:T(8,128)(2,1)S(1)}, bf16[1,4,2,24,704]{4,3,2,1,0:T(8,128)(2,1)S(1)}, u32[]{:S(2)}, u32[]{:S(2)}) collective-permute-start(bf16[1,4,2,24,704]{4,3,2,1,0:T(8,128)(2,1)S(1)} %arrange.9.refs_0_), channel_id=1, source_target_pairs={{0,16},{16,0},{1,17},{17,1},{2,18},{18,2},{3,19},{19,3},{4,20},{20... | collective-permute-start | bytes 811016 | tf_op jit(solution)/shard_map/ppermute | solution.py:22
  42.3 5.1 %collective-permute-start.5 = (bf16[2,4,2,1,24,704]{5,4,3,2,1,0:T(8,128)(2,1)S(1)}, bf16[2,4,2,1,24,704]{5,4,3,2,1,0:T(8,128)(2,1)S(1)}, u32[]{:S(2)}, u32[]{:S(2)}) collective-permute-start(bf16[2,4,2,1,24,704]{5,4,3,2,1,0:T(8,128)(2,1)S(1)} %bitcast.58), channel_id=1, source_target_pairs={{0,1},{1,0},{2,3},{3,2},{4,5},{5,4},{6,7},{7,6},{8,9},{9,8},{10,11... | collective-permute-start | bytes 1622024 | tf_op jit(solution)/shard_map/ppermute | solution.py:22
  42.4 10.9 %collective-permute-start.6 = (bf16[128,768]{1,0:T(8,128)(2,1)S(1)}, bf16[128,768]{1,0:T(8,128)(2,1)S(1)}, u32[]{:S(2)}, u32[]{:S(2)}) collective-permute-start(bf16[128,768]{1,0:T(8,128)(2,1)S(1)} %bitcast.51), channel_id=1, source_target_pairs={{0,4},{4,8},{8,12},{12,0},{1,5},{5,9},{9,13},{13,1},{2,6},{6,10},{... | collective-permute-start | bytes 589832 | tf_op jit(solution)/shard_map/ppermute | solution.py:22
  44.0 17.7 %collective-permute-start.7 = (bf16[128,768]{1,0:T(8,128)(2,1)S(1)}, bf16[128,768]{1,0:T(8,128)(2,1)S(1)}, u32[]{:S(2)}, u32[]{:S(2)}) collective-permute-start(bf16[128,768]{1,0:T(8,128)(2,1)S(1)} %bitcast.52), channel_id=1, source_target_pairs={{0,8},{4,12},{8,0},{12,4},{1,9},{5,13},{9,1},{13,5},{2,10},{6,14},... | collective-permute-start | bytes 589832 | tf_op jit(solution)/shard_map/ppermute | solution.py:22
  46.4 15.3 %collective-permute-start.8 = (bf16[128,768]{1,0:T(8,128)(2,1)S(1)}, bf16[128,768]{1,0:T(8,128)(2,1)S(1)}, u32[]{:S(2)}, u32[]{:S(2)}) collective-permute-start(bf16[128,768]{1,0:T(8,128)(2,1)S(1)} %bitcast.53), channel_id=1, source_target_pairs={{0,12},{4,0},{8,4},{12,8},{1,13},{5,1},{9,5},{13,9},{2,14},{6,2},{... | collective-permute-start | bytes 589832 | tf_op jit(solution)/shard_map/ppermute | solution.py:22
  47.6 27.2 %copy-start.2 = (bf16[2,4,2,2,24,704]{5,4,3,2,1,0:T(8,128)(2,1)}, bf16[2,4,2,2,24,704]{5,4,3,2,1,0:T(8,128)(2,1)S(1)}, u32[]{:S(2)}) copy-start(bf16[2,4,2,2,24,704]{5,4,3,2,1,0:T(8,128)(2,1)S(1)} %arrange.11) | copy-start | bytes 3244036
  63.6 11.0 %collective-permute-start.9 = (bf16[512,384]{1,0:T(8,128)(2,1)S(1)}, bf16[512,384]{1,0:T(8,128)(2,1)S(1)}, u32[]{:S(2)}, u32[]{:S(2)}) collective-permute-start(bf16[512,384]{1,0:T(8,128)(2,1)S(1)} %get-tuple-element.76.refs_3_.refs_9_), channel_id=1, source_target_pairs={{0,2},{2,0},{1,3},{3,1},{4,6},{6,4},{5,7},{7,5},{8,10},{10,8},{9,1... | collective-permute-start | bytes 1179656 | tf_op jit(solution)/shard_map/ppermute | solution.py:22
  65.1 10.1 %collective-permute-start.10 = (bf16[512,384]{1,0:T(8,128)(2,1)S(1)}, bf16[512,384]{1,0:T(8,128)(2,1)S(1)}, u32[]{:S(2)}, u32[]{:S(2)}) collective-permute-start(bf16[512,384]{1,0:T(8,128)(2,1)S(1)} %get-tuple-element.76.refs_3_.refs_9_), channel_id=1, source_target_pairs={{0,1},{1,0},{2,3},{3,2},{4,5},{5,4},{6,7},{7,6},{8,9},{9,8},{10,11... | collective-permute-start | bytes 1179656 | tf_op jit(solution)/shard_map/ppermute | solution.py:22
  74.7 1.7 collective-permute-start.11
  75.2 25.7 %copy-start.20 = (bf16[512,384]{1,0:T(8,128)(2,1)}, bf16[512,384]{1,0:T(8,128)(2,1)S(1)}, u32[]{:S(2)}) copy-start(bf16[512,384]{1,0:T(8,128)(2,1)S(1)} %collective-permute-done.10.refs_5_.refs_11_) | copy-start | bytes 1179652
  76.4 24.6 %copy-start.22 = (bf16[512,384]{1,0:T(8,128)(2,1)}, bf16[512,384]{1,0:T(8,128)(2,1)S(1)}, u32[]{:S(2)}) copy-start(bf16[512,384]{1,0:T(8,128)(2,1)S(1)} %collective-permute-done.11.refs_6_.refs_12_) | copy-start | bytes 1179652
  83.1 11.5 %collective-permute-start.12 = (bf16[128,192]{1,0:T(8,128)(2,1)S(1)}, bf16[128,192]{1,0:T(8,128)(2,1)S(1)}, u32[]{:S(2)}, u32[]{:S(2)}) collective-permute-start(bf16[128,192]{1,0:T(8,128)(2,1)S(1)} %get-tuple-element.78), channel_id=1, source_target_pairs={{0,4},{4,8},{8,12},{12,0},{1,5},{5,9},{9,13},{13,1},{2,6},{6,10},{... | collective-permute-start | bytes 147464 | tf_op jit(solution)/shard_map/ppermute | solution.py:22
  91.6 8.2 %collective-permute-start.13 = (bf16[128,192]{1,0:T(8,128)(2,1)S(1)}, bf16[128,192]{1,0:T(8,128)(2,1)S(1)}, u32[]{:S(2)}, u32[]{:S(2)}) collective-permute-start(bf16[128,192]{1,0:T(8,128)(2,1)S(1)} %get-tuple-element.79), channel_id=1, source_target_pairs={{0,8},{4,12},{8,0},{12,4},{1,9},{5,13},{9,1},{13,5},{2,10},{6,14},... | collective-permute-start | bytes 147464 | tf_op jit(solution)/shard_map/ppermute | solution.py:22
  91.6 8.8 %collective-permute-start.14 = (bf16[128,192]{1,0:T(8,128)(2,1)S(1)}, bf16[128,192]{1,0:T(8,128)(2,1)S(1)}, u32[]{:S(2)}, u32[]{:S(2)}) collective-permute-start(bf16[128,192]{1,0:T(8,128)(2,1)S(1)} %get-tuple-element.80), channel_id=1, source_target_pairs={{0,12},{4,0},{8,4},{12,8},{1,13},{5,1},{9,5},{13,9},{2,14},{6,2},{... | collective-permute-start | bytes 147464 | tf_op jit(solution)/shard_map/ppermute | solution.py:22
  110.7 6.8 %collective-permute-start.17 = (bf16[128,768]{1,0:T(8,128)(2,1)S(1)}, bf16[128,768]{1,0:T(8,128)(2,1)S(1)}, u32[]{:S(2)}, u32[]{:S(2)}) collective-permute-start(bf16[128,768]{1,0:T(8,128)(2,1)S(1)} %get-tuple-element.81.refs_0_.refs_5_), channel_id=1, source_target_pairs={{0,2},{2,0},{1,3},{3,1},{4,6},{6,4},{5,7},{7,5},{8,10},{10,8},{9,1... | collective-permute-start | bytes 589832 | tf_op jit(solution)/shard_map/ppermute | solution.py:22
  112.1 5.3 %collective-permute-start.18 = (bf16[128,768]{1,0:T(8,128)(2,1)S(1)}, bf16[128,768]{1,0:T(8,128)(2,1)S(1)}, u32[]{:S(2)}, u32[]{:S(2)}) collective-permute-start(bf16[128,768]{1,0:T(8,128)(2,1)S(1)} %get-tuple-element.81.refs_0_.refs_5_), channel_id=1, source_target_pairs={{0,1},{1,0},{2,3},{3,2},{4,5},{5,4},{6,7},{7,6},{8,9},{9,8},{10,11... | collective-permute-start | bytes 589832 | tf_op jit(solution)/shard_map/ppermute | solution.py:22
  117.4 1.4 collective-permute-start.19
  123.2 1.7 collective-permute-start.20
  126.4 7.3 %collective-permute-start.21 = (bf16[128,768]{1,0:T(8,128)(2,1)}, bf16[128,768]{1,0:T(8,128)(2,1)}, u32[]{:S(2)}, u32[]{:S(2)}) collective-permute-start(bf16[128,768]{1,0:T(8,128)(2,1)} %get-tuple-element.85), channel_id=1, source_target_pairs={{0,2},{2,0},{1,3},{3,1},{4,6},{6,4},{5,7},{7,5},{8,10},{10,8},{9,1... | collective-permute-start | bytes 589832 | tf_op jit(solution)/shard_map/ppermute | solution.py:22
  142.1 6.1 %collective-permute-start.22 = (bf16[128,768]{1,0:T(8,128)(2,1)S(1)}, bf16[128,768]{1,0:T(8,128)(2,1)S(1)}, u32[]{:S(2)}, u32[]{:S(2)}) collective-permute-start(bf16[128,768]{1,0:T(8,128)(2,1)S(1)} %get-tuple-element.89.refs_0_.refs_11_), channel_id=1, source_target_pairs={{0,2},{2,0},{1,3},{3,1},{4,6},{6,4},{5,7},{7,5},{8,10},{10,8},{9,1... | collective-permute-start | bytes 589832 | tf_op jit(solution)/shard_map/ppermute | solution.py:22
  143.6 4.6 %collective-permute-start.23 = (bf16[128,768]{1,0:T(8,128)(2,1)S(1)}, bf16[128,768]{1,0:T(8,128)(2,1)S(1)}, u32[]{:S(2)}, u32[]{:S(2)}) collective-permute-start(bf16[128,768]{1,0:T(8,128)(2,1)S(1)} %get-tuple-element.89.refs_0_.refs_11_), channel_id=1, source_target_pairs={{0,1},{1,0},{2,3},{3,2},{4,5},{5,4},{6,7},{7,6},{8,9},{9,8},{10,11... | collective-permute-start | bytes 589832 | tf_op jit(solution)/shard_map/ppermute | solution.py:22
  148.2 1.4 collective-permute-start.24
  159.1 2.0 collective-permute-start.25
  162.3 7.0 %collective-permute-start.26 = (bf16[128,768]{1,0:T(8,128)(2,1)S(1)}, bf16[128,768]{1,0:T(8,128)(2,1)S(1)}, u32[]{:S(2)}, u32[]{:S(2)}) collective-permute-start(bf16[128,768]{1,0:T(8,128)(2,1)S(1)} %get-tuple-element.94), channel_id=1, source_target_pairs={{0,2},{2,0},{1,3},{3,1},{4,6},{6,4},{5,7},{7,5},{8,10},{10,8},{9,1... | collective-permute-start | bytes 589832 | tf_op jit(solution)/shard_map/ppermute | solution.py:22
  175.5 8.1 %collective-permute-start.27 = (bf16[128,192]{1,0:T(8,128)(2,1)S(1)}, bf16[128,192]{1,0:T(8,128)(2,1)S(1)}, u32[]{:S(2)}, u32[]{:S(2)}) collective-permute-start(bf16[128,192]{1,0:T(8,128)(2,1)S(1)} %get-tuple-element.100), channel_id=1, source_target_pairs={{0,4},{4,8},{8,12},{12,0},{1,5},{5,9},{9,13},{13,1},{2,6},{6,10},{... | collective-permute-start | bytes 147464 | tf_op jit(solution)/shard_map/ppermute | solution.py:22
  176.8 10.8 %collective-permute-start.28 = (bf16[128,192]{1,0:T(8,128)(2,1)S(1)}, bf16[128,192]{1,0:T(8,128)(2,1)S(1)}, u32[]{:S(2)}, u32[]{:S(2)}) collective-permute-start(bf16[128,192]{1,0:T(8,128)(2,1)S(1)} %get-tuple-element.101), channel_id=1, source_target_pairs={{0,8},{4,12},{8,0},{12,4},{1,9},{5,13},{9,1},{13,5},{2,10},{6,14},... | collective-permute-start | bytes 147464 | tf_op jit(solution)/shard_map/ppermute | solution.py:22
  178.8 8.8 %collective-permute-start.29 = (bf16[128,192]{1,0:T(8,128)(2,1)S(1)}, bf16[128,192]{1,0:T(8,128)(2,1)S(1)}, u32[]{:S(2)}, u32[]{:S(2)}) collective-permute-start(bf16[128,192]{1,0:T(8,128)(2,1)S(1)} %get-tuple-element.102), channel_id=1, source_target_pairs={{0,12},{4,0},{8,4},{12,8},{1,13},{5,1},{9,5},{13,9},{2,14},{6,2},{... | collective-permute-start | bytes 147464 | tf_op jit(solution)/shard_map/ppermute | solution.py:22
  195.9 3.0 %collective-permute-start.30 = (bf16[2,512,384]{2,1,0:T(8,128)(2,1)}, bf16[2,512,384]{2,1,0:T(8,128)(2,1)S(1)}, u32[]{:S(2)}, u32[]{:S(2)}) collective-permute-start(bf16[2,512,384]{2,1,0:T(8,128)(2,1)} %get-tuple-element.106), channel_id=1, source_target_pairs={{0,1},{1,0},{2,3},{3,2},{4,5},{5,4},{6,7},{7,6},{8,9},{9,8},{10,11... | collective-permute-start | bytes 2359304 | tf_op jit(solution)/shard_map/ppermute | solution.py:22
  201.8 11.8 %collective-permute-start.31 = (bf16[512,384]{1,0:T(8,128)(2,1)}, bf16[512,384]{1,0:T(8,128)(2,1)S(1)}, u32[]{:S(2)}, u32[]{:S(2)}) collective-permute-start(bf16[512,384]{1,0:T(8,128)(2,1)} %get-tuple-element.108), channel_id=1, source_target_pairs={{0,2},{2,0},{1,3},{3,1},{4,6},{6,4},{5,7},{7,5},{8,10},{10,8},{9,1... | collective-permute-start | bytes 1179656 | tf_op jit(solution)/shard_map/ppermute | solution.py:22
  220.4 2.9 %collective-permute-start.32 = (bf16[16,24,1472]{2,1,0:T(8,128)(2,1)S(1)}, bf16[16,24,1472]{2,1,0:T(8,128)(2,1)S(1)}, u32[]{:S(2)}, u32[]{:S(2)}) collective-permute-start(bf16[16,24,1472]{2,1,0:T(8,128)(2,1)S(1)} %get-tuple-element.117), channel_id=1, source_target_pairs={{0,1},{1,0},{2,3},{3,2},{4,5},{5,4},{6,7},{7,6},{8,9},{9,8},{10,11... | collective-permute-start | bytes 3391496 | tf_op jit(solution)/shard_map/ppermute | solution.py:22
  223.5 15.4 %collective-permute-start.33 = (bf16[1,4,2,24,1472]{4,3,2,1,0:T(8,128)(2,1)S(1)}, bf16[1,4,2,24,1472]{4,3,2,1,0:T(8,128)(2,1)S(1)}, u32[]{:S(2)}, u32[]{:S(2)}) collective-permute-start(bf16[1,4,2,24,1472]{4,3,2,1,0:T(8,128)(2,1)S(1)} %get-tuple-element.119), channel_id=1, source_target_pairs={{0,16},{16,0},{1,17},{17,1},{2,18},{18,2},{3,19},{19,3},{4,20},{20... | collective-permute-start | bytes 1695752 | tf_op jit(solution)/shard_map/ppermute | solution.py:22
  239.1 8.3 %collective-permute-start.34 = (bf16[1,4,1,24,1472]{4,3,2,1,0:T(8,128)(2,1)S(1)}, bf16[1,4,1,24,1472]{4,3,2,1,0:T(8,128)(2,1)S(1)}, u32[]{:S(2)}, u32[]{:S(2)}) collective-permute-start(bf16[1,4,1,24,1472]{4,3,2,1,0:T(8,128)(2,1)S(1)} %get-tuple-element.121), channel_id=1, source_target_pairs={{0,2},{2,0},{1,3},{3,1},{4,6},{6,4},{5,7},{7,5},{8,10},{10,8},{9,1... | collective-permute-start | bytes 847880 | tf_op jit(solution)/shard_map/ppermute | solution.py:22
  240.7 11.2 %collective-permute-start.38 = (bf16[128,768]{1,0:T(8,128)(2,1)S(1)}, bf16[128,768]{1,0:T(8,128)(2,1)S(1)}, u32[]{:S(2)}, u32[]{:S(2)}) collective-permute-start(bf16[128,768]{1,0:T(8,128)(2,1)S(1)} %get-tuple-element.128), channel_id=1, source_target_pairs={{0,4},{4,8},{8,12},{12,0},{1,5},{5,9},{9,13},{13,1},{2,6},{6,10},{... | collective-permute-start | bytes 589832 | tf_op jit(solution)/shard_map/ppermute | solution.py:22
  244.5 14.3 %collective-permute-start.39 = (bf16[128,768]{1,0:T(8,128)(2,1)S(1)}, bf16[128,768]{1,0:T(8,128)(2,1)S(1)}, u32[]{:S(2)}, u32[]{:S(2)}) collective-permute-start(bf16[128,768]{1,0:T(8,128)(2,1)S(1)} %get-tuple-element.129), channel_id=1, source_target_pairs={{0,8},{4,12},{8,0},{12,4},{1,9},{5,13},{9,1},{13,5},{2,10},{6,14},... | collective-permute-start | bytes 589832 | tf_op jit(solution)/shard_map/ppermute | solution.py:22
  245.2 13.7 %collective-permute-start.40 = (bf16[128,768]{1,0:T(8,128)(2,1)S(1)}, bf16[128,768]{1,0:T(8,128)(2,1)S(1)}, u32[]{:S(2)}, u32[]{:S(2)}) collective-permute-start(bf16[128,768]{1,0:T(8,128)(2,1)S(1)} %get-tuple-element.130), channel_id=1, source_target_pairs={{0,12},{4,0},{8,4},{12,8},{1,13},{5,1},{9,5},{13,9},{2,14},{6,2},{... | collective-permute-start | bytes 589832 | tf_op jit(solution)/shard_map/ppermute | solution.py:22
  247.4 12.9 %collective-permute-start.35 = (bf16[1,1,1,24,1472]{4,3,2,1,0:T(8,128)(2,1)S(1)}, bf16[1,1,1,24,1472]{4,3,2,1,0:T(8,128)(2,1)S(1)}, u32[]{:S(2)}, u32[]{:S(2)}) collective-permute-start(bf16[1,1,1,24,1472]{4,3,2,1,0:T(8,128)(2,1)S(1)} %get-tuple-element.123), channel_id=1, source_target_pairs={{0,4},{4,8},{8,12},{12,0},{1,5},{5,9},{9,13},{13,1},{2,6},{6,10},{... | collective-permute-start | bytes 211976 | tf_op jit(solution)/shard_map/ppermute | solution.py:22
  251.4 14.8 %collective-permute-start.36 = (bf16[1,1,1,24,1472]{4,3,2,1,0:T(8,128)(2,1)S(1)}, bf16[1,1,1,24,1472]{4,3,2,1,0:T(8,128)(2,1)S(1)}, u32[]{:S(2)}, u32[]{:S(2)}) collective-permute-start(bf16[1,1,1,24,1472]{4,3,2,1,0:T(8,128)(2,1)S(1)} %get-tuple-element.124), channel_id=1, source_target_pairs={{0,8},{4,12},{8,0},{12,4},{1,9},{5,13},{9,1},{13,5},{2,10},{6,14},... | collective-permute-start | bytes 211976 | tf_op jit(solution)/shard_map/ppermute | solution.py:22
  251.9 14.3 %collective-permute-start.37 = (bf16[1,1,1,24,1472]{4,3,2,1,0:T(8,128)(2,1)S(1)}, bf16[1,1,1,24,1472]{4,3,2,1,0:T(8,128)(2,1)S(1)}, u32[]{:S(2)}, u32[]{:S(2)}) collective-permute-start(bf16[1,1,1,24,1472]{4,3,2,1,0:T(8,128)(2,1)S(1)} %get-tuple-element.125), channel_id=1, source_target_pairs={{0,12},{4,0},{8,4},{12,8},{1,13},{5,1},{9,5},{13,9},{2,14},{6,2},{... | collective-permute-start | bytes 211976 | tf_op jit(solution)/shard_map/ppermute | solution.py:22
  268.9 4.4 %collective-permute-start.41 = (bf16[1,1,1,2,24,768]{5,4,3,2,1,0:T(8,128)(2,1)S(1)}, bf16[1,1,1,2,24,768]{5,4,3,2,1,0:T(8,128)(2,1)S(1)}, u32[]{:S(2)}, u32[]{:S(2)}) collective-permute-start(bf16[1,1,1,2,24,768]{5,4,3,2,1,0:T(8,128)(2,1)S(1)} %get-tuple-element.152), channel_id=1, source_target_pairs={{0,2},{2,0},{1,3},{3,1},{4,6},{6,4},{5,7},{7,5},{8,10},{10,8},{9,1... | collective-permute-start | bytes 221192 | tf_op jit(solution)/shard_map/ppermute | solution.py:22
  273.4 1.3 collective-permute-start.42
  (107 other events, 462.3 us)
Sparse Core Ops, SparseCore 0:
  18.9 81.1 all-gather.1
  159.2 72.7 reduce-scatter.1
where the time goes:
time: 286 us; the launch traced here: 284 us
  waiting for transfers between devices  123 us (43%)
  starting transfers between devices  56.4 us (20%)
  local copies, waits for them, and re-layouts  48 us (17%)
  Pallas kernels  31.1 us (11%)
  between operations  18.9 us (7%)
  other arithmetic  7.1 us (2%)
    ppermute x43, waiting for transfers between devices, shift(): lax.ppermute(value, axis, [(a, (a + step) % size) for a in range(size)])  123 us
    ppermute x43, starting transfers between devices, shift(): lax.ppermute(value, axis, [(a, (a + step) % size) for a in range(size)])  56.3 us
    unnamed x221, local copies, waits for them, and re-layouts  42.6 us
    pallas_call x20, Pallas kernels, call(): pl.pallas_call(whole, in_specs=specs + [pl.BlockSpec(memory_space=pl.ANY)...  30.7 us
  transfers between devices with their start and end apart: 45, of which 31 were waited for; matrix products, arithmetic and copies ran while one was open for 3% of the time, Pallas kernels for 7%

commit v1 on v0

--- a/solution.py
+++ b/solution.py
@@ -116,18 +116,8 @@
             one_ref[g, :, 6 * hd:9 * hd] = qkv_ref[:, g * group:g * group + 3 * hd]
             one_ref[g, :, 9 * hd:11 * hd] = cols
 
-    specs = [pl.BlockSpec(a.shape, lambda i: (0, 0)) for a in (w_qkv, flat, seg, mask)]
-    return pl.pallas_call(
-        body,
-        grid=(1,),
-        in_specs=specs,
-        out_specs=pl.BlockSpec((ZS, rows, 11 * hd), lambda i: (0, 0, 0)),
-        out_shape=jax.ShapeDtypeStruct((ZS, rows, 11 * hd), BF),
-        scratch_shapes=[pltpu.VMEM((LANES, LANES), F32)],
-        compiler_params=params(),
-        cost_estimate=SMALL,
-        name="pack_one",
-    )(w_qkv, flat, seg, mask)
+    outs = [((ZS, rows, 11 * hd), BF)]
+    return call(body, (w_qkv, flat, seg, mask), outs, "pack_one", scratch=[pltpu.VMEM((LANES, LANES), F32)])[0]
 
 
 def pack_up(w_up, w_out, ffd, sx):
@@ -182,27 +172,35 @@
     )(place.astype(jnp.int32).reshape(1), *pieces, *after)
 
 
-def project_kernel(place, h0, h1, h2, h3, w_ref, gain_ref, shift_ref, bkv_ref, bq_ref, n1_ref, q_ref, kv_ref):
-    rows = h0.shape[0]
+def project(place, pieces, one, vectors):
+    rows, width = pieces[0].shape
+    total = ZS * rows
     hd = HEAD_DIM
-    for d, piece in enumerate((h0, h1, h2, h3)):
-        spot = pl.ds(pl.multiple_of(lax.rem(place[0] + ZS - d, ZS) * rows, rows), rows)
-        values = piece[...].astype(F32)
-        centered = values - jnp.mean(values, -1, keepdims=True)
-        rstd = lax.rsqrt(jnp.mean(centered * centered, -1, keepdims=True) + 1e-05)
-        n1 = (centered * rstd * gain_ref[...] + shift_ref[...]).astype(BF)
-        n1_ref[spot, :] = n1
-        joined = dot(n1, w_ref[:, 0:9 * hd])
-        kv_ref[spot, :] = (joined[:, 0:6 * hd] + bkv_ref[...]).astype(BF)
-        q = (joined[:, 6 * hd:9 * hd] + bq_ref[...]).astype(BF).astype(F32) * 0.125
-        q_ref[spot, 0:3 * hd] = q.astype(BF)
-        q_ref[spot, 3 * hd:4 * hd] = jnp.zeros((rows, hd), BF)
-
-
-def project(place, pieces, w, gain, shift_row, bkv, bq):
-    total, width = ZS * pieces[0].shape[0], pieces[0].shape[1]
-    outs = [((total, width), BF), ((total, 4 * HEAD_DIM), BF), ((total, 6 * HEAD_DIM), BF)]
-    return call(project_kernel, (place, *pieces, w, gain, shift_row, bkv, bq), outs, "project", 1)
+    group = 3 * hd
+
+    def body(place_ref, h0, h1, h2, h3, w_ref, vec_ref, n1_ref, q_ref, kv_ref, all_ref):
+        qb = jnp.zeros((1, group), F32)
+        vb = jnp.zeros((1, group), F32)
+        for g in range(ZS):
+            here = place_ref[0] == g
+            qb = jnp.where(here, vec_ref[0:1, g * group:(g + 1) * group], qb)
+            vb = jnp.where(here, vec_ref[1:2, g * group:(g + 1) * group], vb)
+        for d, piece in enumerate((h0, h1, h2, h3)):
+            spot = pl.ds(pl.multiple_of(lax.rem(place_ref[0] + ZS - d, ZS) * rows, rows), rows)
+            all_ref[spot, :] = piece[...]
+            normed, _ = norm_parts(piece[...].astype(F32))
+            n1 = (normed * vec_ref[4:5, :] + vec_ref[5:6, :]).astype(BF)
+            n1_ref[spot, :] = n1
+            joined = dot(n1, w_ref[:, 0:9 * hd])
+            kv_ref[spot, 0:3 * hd] = joined[:, 0:3 * hd].astype(BF)
+            kv_ref[spot, 3 * hd:4 * hd] = (joined[:, 3 * hd:4 * hd] + vb[:, 2 * hd:]).astype(BF)
+            kv_ref[spot, 4 * hd:6 * hd] = (joined[:, 4 * hd:6 * hd] + vb[:, 0:2 * hd]).astype(BF)
+            q = (joined[:, 6 * hd:9 * hd] + qb).astype(BF).astype(F32) * 0.125
+            q_ref[spot, 0:3 * hd] = q.astype(BF)
+            q_ref[spot, 3 * hd:4 * hd] = jnp.zeros((rows, hd), BF)
+
+    outs = [((total, width), BF), ((total, 4 * hd), BF), ((total, 6 * hd), BF), ((total, width), BF)]
+    return call(body, (place, pieces[0], *pieces[1:], one, vectors), outs, "project", 1)
 
 
 def fill_keys(kv_refs, keys, rows):
@@ -282,7 +280,7 @@
     span = len(kvs) * total // ZS
     outs = [((total // ZS, 3 * HEAD_DIM), BF)] * ZS + [((total, 2 * LANES), F32)] * 2
     scratch = [pltpu.VMEM((ZS * span, 3 * LANES), BF), pltpu.VMEM((span, total), F32), pltpu.VMEM((3, LANES, total), F32), pltpu.VMEM((LANES, LANES), F32)]
-    return call(attend_kernel, (order, q, seg, *kvs), outs, "attend", 1, after, scratch, 28)
+    return call(attend_kernel, (order, q, seg, *kvs), outs, "attend", 1, after, scratch, 20)
 
 
 def attend_back_kernel(order, q_ref, gc0, gc1, gc2, gc3, ctx_ref, tot_ref, seg_ref, *rest):
@@ -359,7 +357,7 @@
         pltpu.VMEM((total, 3 * HEAD_DIM), F32),
         pltpu.VMEM((LANES, LANES), F32),
     ]
-    return call(attend_back_kernel, (order, q, *gctx, ctx, tot, seg, *kvs), outs, "attend_back", 1, after, scratch, 32)
+    return call(attend_back_kernel, (order, q, *gctx, ctx, tot, seg, *kvs), outs, "attend_back", 1, after, scratch, 24)
 
 
 def norm_parts(values):
@@ -377,120 +375,170 @@
 GC = 0.7978845608028654
 
 
-def call(body, args, outs, name, smem=0, after=(), scratch=(), mib=16, keep=()):
-    large = [i for i in keep]
-    specs = [pl.BlockSpec(memory_space=pltpu.SMEM if i < smem else pl.ANY if i in large else pltpu.VMEM) for i in range(len(args))]
-    count = len(args)
-    fetched = [pltpu.VMEM(args[i].shape, args[i].dtype) for i in large]
+class Part:
+    def __init__(self, value, first, last):
+        self.value, self.first, self.last = value, first, last
+
+
+def call(body, args, outs, name, smem=0, after=(), scratch=(), mib=12):
+    values = [arg.value if isinstance(arg, Part) else arg for arg in args]
+    count, waits = len(values), len(after)
 
     def whole(*refs):
-        ins, rest = list(refs[:count]), refs[count + len(after):]
-        if large:
-            rest, slots, sems = rest[:-len(large) - 1], rest[-len(large) - 1:-1], rest[-1]
-            copies = [pltpu.make_async_copy(ins[i], slot, sems.at[n]) for n, (i, slot) in enumerate(zip(large, slots))]
-            for copy in copies:
-                copy.start()
-            for copy in copies:
-                copy.wait()
-            for i, slot in zip(large, slots):
-                ins[i] = slot
-        body(*ins, *rest)
-
+        ins = [ref.at[:, arg.first:arg.last] if isinstance(arg, Part) else ref for arg, ref in zip(args, refs)]
+        body(*ins, *refs[count + waits:])
+
+    specs = [pl.BlockSpec(memory_space=pltpu.SMEM if i < smem else pltpu.VMEM) for i in range(count)]
     return pl.pallas_call(
         whole,
-        in_specs=specs + [pl.BlockSpec(memory_space=pl.ANY)] * len(after),
+        in_specs=specs + [pl.BlockSpec(memory_space=pl.ANY)] * waits,
         out_shape=[jax.ShapeDtypeStruct(*out) for out in outs],
-        scratch_shapes=list(scratch) + fetched + ([pltpu.SemaphoreType.DMA((len(large),))] if large else []),
+        scratch_shapes=list(scratch),
         compiler_params=params(mib),
         cost_estimate=SMALL,
         name=name,
-    )(*args, *after)
-
-
-def fold(own, came, place, dim, size, name="fold"):
-    shape = list(own.shape)
-    shape[dim] //= size
-    part = shape[dim]
-
-    def body(place_ref, own_ref, *refs):
-        for d in range(size):
-            spot = lax.rem(place_ref[0] + d, size) * part
-            index = (slice(None),) * dim + (pl.ds(spot, part),)
-            total = own_ref[index].astype(F32)
-            for ref in refs[:len(came)]:
-                total = total + ref[index].astype(F32)
-            refs[len(came) + d][...] = total.astype(F32 if d == 0 else BF)
-
-    outs = [(tuple(shape), BF if d else F32) for d in range(size)]
-    return call(body, (place.astype(jnp.int32).reshape(1), own, *came), outs, name, 1)
+    )(*values, *after)
+
+
+def fold_both(kept, came, ix, iy, width):
+    sy, sz, sx, wr, wide = kept.shape
+
+    def body(at_ref, kept_ref, came_ref, *outs):
+        for d in range(sx):
+            x = lax.rem(at_ref[0] + d, sx)
+            outs[d][...] = (kept_ref[:, :, pl.ds(x, 1), :, 0:width].astype(F32) + came_ref[:, :, pl.ds(x, 1), :, 0:width].astype(F32)).astype(BF)
+        for d in range(sy):
+            y = lax.rem(at_ref[1] + d, sy)
+            outs[sx + d][...] = (kept_ref[pl.ds(y, 1), :, :, :, width:].astype(F32) + came_ref[pl.ds(y, 1), :, :, :, width:].astype(F32)).astype(BF)
+
+    outs = [((sy, sz, 1, wr, width), BF)] * sx + [((1, sz, sx, wr, wide - width), BF)] * sy
+    return call(body, (jnp.stack([ix, iy]).astype(jnp.int32), kept, came), outs, "fold_both", 1)
+
+
+def fold_cross(first, first_came, second, second_came, ix, iy):
+    sx, sy = len(first), len(second)
+    sz, wr, width = first[0].shape[1], first[0].shape[3], first[0].shape[4]
+    other = second[0].shape[4]
+
+    def body(at_ref, *refs):
+        one, two, outs = refs[:sx], refs[sx:sx + sy], refs[sx + sy:]
+        for d in range(sy):
+            y = lax.rem(at_ref[1] + d, sy)
+            total = one[0][pl.ds(y, 1)].astype(F32)
+            for ref in one[1:]:
+                total = total + ref[pl.ds(y, 1)].astype(F32)
+            outs[d][...] = total.astype(BF)
+        for d in range(sx):
+            x = lax.rem(at_ref[0] + d, sx)
+            total = two[0][:, :, pl.ds(x, 1)].astype(F32)
+            for ref in two[1:]:
+                total = total + ref[:, :, pl.ds(x, 1)].astype(F32)
+            outs[sy + d][...] = total.astype(BF)
+
+    outs = [((1, sz, 1, wr, width), BF)] * sy + [((1, sz, 1, wr, other), BF)] * sx
+    args = (jnp.stack([ix, iy]).astype(jnp.int32), first[0], *first_came, second[0], *second_came)
+    return call(body, args, outs, "fold_cross", 1)
+
+
+def fold_last(first, first_came, second, second_came, iz, after):
+    sy, sx = len(first), len(second)
+    wr, width = first[0].shape[3:]
+    wide = width + second[0].shape[4]
+
+    def body(at_ref, *refs):
+        one, two, outs = refs[:sy], refs[sy:sy + sx], refs[sy + sx:]
+        for d in range(ZS):
+            z = lax.rem(at_ref[0] + d, ZS)
+            for sums, cols in ((one, slice(0, width)), (two, slice(width, wide))):
+                total = sums[0][:, pl.ds(z, 1)].astype(F32)
+                for ref in sums[1:]:
+                    total = total + ref[:, pl.ds(z, 1)].astype(F32)
+                outs[d][:, :, :, :, cols] = total.astype(BF)
+
+    outs = [((1, 1, 1, wr, wide), BF)] * ZS
+    args = (iz.astype(jnp.int32).reshape(1), first[0], *first_came, second[0], *second_came)
+    return call(body, args, outs, "fold_last", 1, after)
 
 
 def passed(pieces, axis):
     return [shift(pieces[d], axis, d) for d in range(1, len(pieces))]
 
 
-def out_project(place, pieces, w_out, bias, hidden, gain, shift_row, at, after):
+def out_project(place, pieces, mid, ff, hidden, vectors, after):
     rows, group = pieces[0].shape
     width = hidden.shape[1]
 
-    def body(place_ref, p0, p1, p2, p3, w_ref, bias_ref, hidden_ref, gain_ref, shift_ref, res_ref, n2_ref):
-        total = hidden_ref[...].astype(F32) + bias_ref[...]
+    def body(place_ref, p0, p1, p2, p3, w_ref, hidden_ref, vec_ref, res_ref, n2_ref, cat_ref):
+        total = hidden_ref[...].astype(F32) + vec_ref[2:3, :]
         for d, piece in enumerate((p0, p1, p2, p3)):
             spot = pl.ds(pl.multiple_of(lax.rem(place_ref[0] + ZS - d, ZS) * group, group), group)
-            total = total + dot(piece[...], w_ref[spot, at:at + width])
-        res_ref[...] = total
+            total = total + dot(piece[...], w_ref[spot, :])
+            cat_ref[:, d * group:(d + 1) * group] = piece[...]
+        res_ref[:, 0:width] = total
+        res_ref[:, width:] = jnp.broadcast_to(vec_ref[15:16, 0:rows], (LANES, rows)).T
         n2, _ = norm_parts(total)
-        n2_ref[...] = (n2 * gain_ref[...] + shift_ref[...]).astype(BF)
-
-    return call(body, (place, *pieces, w_out, bias, hidden, gain, shift_row), [((rows, width), F32), ((rows, width), BF)], "out_project", 1, after)
-
-
-def mlp_up(blocks, weights, bias):
+        n2_ref[...] = (n2 * vec_ref[6:7, :] + vec_ref[7:8, :]).astype(BF)
+
+    outs = [((rows, width + LANES), F32), ((rows, width), BF), ((rows, width), BF)]
+    args = (place, *pieces, Part(mid, ff, ff + width), hidden, vectors)
+    return call(body, args, outs, "out_project", 1, after)
+
+
+def mlp_parts(weights, ff):
+    width = weights[0].shape[0]
+    if len(weights) == 2:
+        return Part(weights[0], 0, ff), weights[1]
+    return Part(weights[0], 0, ff), Part(weights[0], ff + width, ff + 2 * width)
+
+
+def mlp_up(blocks, weights, bias, ff):
     rows, width = blocks[0].shape
     count = len(blocks)
     half = count // 2
-    ff = bias.shape[1]
 
     def body(*refs):
-        n2_refs, (bias_ref, w_ref), (kept_ref, sent_ref, act_ref, slope_ref) = refs[:count], refs[count:count + 2], refs[-4:]
-        down_ref = refs[count + 2] if len(weights) == 2 else w_ref.at[:, ff + width:]
+        n2_refs, (bias_ref, up_ref, down_ref), (kept_ref, sent_ref, act_ref, slope_ref, n2_all) = refs[:count], refs[count:count + 3], refs[-5:]
         for j in range(count):
-            pre = dot(n2_refs[j][...], w_ref[:, 0:ff]) + bias_ref[...]
+            n2_all[j * rows:(j + 1) * rows, :] = n2_refs[j][...]
+            pre = dot(n2_refs[j][...], up_ref[...]) + bias_ref[0:1, 0:ff]
             square = pre * pre
             tanh = jnp.tanh(GC * pre * (1.0 + 0.044715 * square))
             half_one = 0.5 * (1.0 + tanh)
             act = (pre * half_one).astype(BF)
-            slope_ref[j] = half_one + 0.5 * pre * (1.0 - tanh * tanh) * (GC + GC * 0.134145 * square)
+            slope_ref[j] = (half_one + 0.5 * pre * (1.0 - tanh * tanh) * (GC + GC * 0.134145 * square)).astype(BF)
             act_ref[j * rows:(j + 1) * rows, :] = act
             part = dot(act, down_ref[...])
             if j < half:
-                kept_ref[j] = part
+                kept_ref[j] = part + bias_ref[1:2, 0:width] if j == 0 else part
             else:
                 sent_ref[j - half] = part.astype(BF)
 
-    outs = [((half, rows, width), F32), ((half, rows, width), BF), ((count * rows, ff), BF), ((count, rows, ff), F32)]
-    return call(body, (*blocks, bias, *weights), outs, "mlp_up")
-
-
-def finish(terms, residual, bias, teacher, cotangent, mask, scale):
-    rows, width = residual.shape
+    outs = [((half, rows, width), F32), ((half, rows, width), BF), ((count * rows, ff), BF), ((count, rows, ff), BF), ((count * rows, width), BF)]
+    return call(body, (*blocks, bias, *mlp_parts(weights, ff)), outs, "mlp_up")
+
+
+def finish(terms, residual, targets, scale):
+    rows, width = targets.shape[1:]
     size = len(terms)
 
     def body(scale_ref, *refs):
-        res_ref, bias_ref, teacher_ref, cot_ref, mask_ref, out_ref, err_ref, gfin_ref, gmlp_ref = refs[size:]
-        valid = jnp.broadcast_to(mask_ref[...].astype(F32), (LANES, rows)).T[:, 0:1]
-        final = res_ref[...] + bias_ref[...]
+        res_ref, target_ref, out_ref, err_ref, both_ref, gmlp_ref = refs[size:]
+        valid = res_ref[:, width:width + 1]
+        final = res_ref[:, 0:width]
         for ref in refs[:size]:
             final = final + ref[...].astype(F32)
         out_ref[...] = final.astype(BF)
-        deviation = final - teacher_ref[...].astype(F32)
-        err_ref[...] = jnp.sum(valid * deviation * deviation, 0, keepdims=True)
-        grad = valid * (cot_ref[...].astype(F32) + deviation * scale_ref[0])
-        gfin_ref[...] = grad
-        gmlp_ref[...] = grad.astype(BF)
-
-    outs = [((rows, width), BF), ((1, width), F32), ((rows, width), F32), ((rows, width), BF)]
-    return call(body, (scale, *terms, residual, bias, teacher, cotangent, mask), outs, "finish", 1)
+        deviation = final - target_ref[0].astype(F32)
+        grad = valid * (target_ref[1].astype(F32) + deviation * scale_ref[0])
+        both_ref[0] = res_ref[:, 0:width]
+        both_ref[1] = grad
+        low = grad.astype(BF)
+        gmlp_ref[...] = low
+        err_ref[0:1, :] = jnp.sum(valid * deviation * deviation, 0, keepdims=True)
+        err_ref[1:2, :] = jnp.sum(low.astype(F32), 0, keepdims=True)
+
+    outs = [((rows, width), BF), ((2, width), F32), ((2, rows, width), F32), ((rows, width), BF)]
+    return call(body, (scale, *terms, residual, targets), outs, "finish", 1)
 
 
 def mlp_back(grads, weights, slope):
@@ -500,76 +548,69 @@
     ff = slope.shape[2]
 
     def body(*refs):
-        g_refs, (slope_ref, w_ref), (kept_ref, sent_ref, gpre_ref) = refs[:count], refs[count:count + 2], refs[-3:]
-        down_ref = refs[count + 2] if len(weights) == 2 else w_ref.at[:, ff + width:]
+        g_refs, (slope_ref, up_ref, down_ref), (kept_ref, sent_ref, gpre_ref, g_all) = refs[:count], refs[count:count + 3], refs[-4:]
         for j in range(count):
-            gpre = (dot_nt(g_refs[j][...], down_ref[...]) * slope_ref[j]).astype(BF)
+            g_all[j * rows:(j + 1) * rows, :] = g_refs[j][...]
+            gpre = (dot_nt(g_refs[j][...], down_ref[...]) * slope_ref[j].astype(F32)).astype(BF)
             gpre_ref[j * rows:(j + 1) * rows, :] = gpre
-            part = dot_nt(gpre, w_ref[:, 0:ff])
+            part = dot_nt(gpre, up_ref[...])
             if j < half:
                 kept_ref[j] = part
             else:
                 sent_ref[j - half] = part.astype(BF)
 
-    outs = [((half, rows, width), F32), ((half, rows, width), BF), ((count * rows, ff), BF)]
-    return call(body, (*grads, slope, *weights), outs, "mlp_back")
-
-
-def mlp_weights(grads, act, blocks, gpre):
-    rows, width = grads[0].shape
-    count = len(grads)
+    outs = [((half, rows, width), F32), ((half, rows, width), BF), ((count * rows, ff), BF), ((count * rows, width), BF)]
+    return call(body, (*grads, slope, *mlp_parts(weights, ff)), outs, "mlp_back")
+
+
+def mlp_weights(grads, act, n2, gpre, after):
+    width = grads.shape[1]
     ff = act.shape[1]
 
-    def body(*refs):
-        g_refs, act_ref, n_refs, gpre_ref, outs, (g_all, n_all) = refs[:count], refs[count], refs[count + 1:2 * count + 1], refs[2 * count + 1], refs[2 * count + 2:-2], refs[-2:]
+    def body(g_ref, act_ref, n2_ref, gpre_ref, *outs):
         down_ref, up_ref = (outs[0].at[:, 0:width], outs[0].at[:, width:]) if ff == width else outs[:2]
-        for j in range(count):
-            g_all[j * rows:(j + 1) * rows, :] = g_refs[j][...]
-            n_all[j * rows:(j + 1) * rows, :] = n_refs[j][...]
-        down_ref[...] = dot_tn(act_ref[...], g_all[...]).astype(BF)
-        up_ref[...] = dot_tn(n_all[...], gpre_ref[...]).astype(BF)
+        down_ref[...] = dot_tn(act_ref[...], g_ref[...]).astype(BF)
+        up_ref[...] = dot_tn(n2_ref[...], gpre_ref[...]).astype(BF)
         outs[-1][...] = jnp.sum(gpre_ref[...].astype(F32), 0, keepdims=True)
 
     outs = [((width, 2 * width), BF)] if ff == width else [((ff, width), BF), ((width, ff), BF)]
-    scratch = [pltpu.VMEM((count * rows, width), BF)] * 2
-    *grads, sums = call(body, (*grads, act, *blocks, gpre), outs + [((1, ff), F32)], "mlp_weights", scratch=scratch)
+    *grads, sums = call(body, (grads, act, n2, gpre), outs + [((1, ff), F32)], "mlp_weights", after=after)
     return grads, sums
 
 
-def out_back(place, terms, residual, gain, gfin, pieces, w_out, gmlp, at, after):
-    rows, width = residual.shape
-    group = pieces[0].shape[1]
+def out_back(place, terms, res_and_grad, vectors, ctx_cat, mid, ff, after):
+    rows, width = res_and_grad.shape[1:]
+    group = width // ZS
     size = len(terms)
 
     def body(place_ref, *refs):
-        res_ref, gain_ref, gfin_ref = refs[size:size + 3]
-        p_refs, (w_ref, gmlp_ref), gres_ref, gctx_refs, (gw_ref, sums_ref) = refs[size + 3:size + 7], refs[size + 7:size + 9], refs[size + 9], refs[size + 10:size + 14], refs[size + 14:]
+        (both_ref, vec_ref, cat_ref, w_ref, gres_ref), gctx_refs, (gw_ref, sums_ref) = refs[size:size + 5], refs[size + 5:size + 9], refs[size + 9:]
         gn2 = refs[0][...]
         for ref in refs[1:size]:
             gn2 = gn2 + ref[...].astype(F32)
-        n2, rstd = norm_parts(res_ref[...])
-        gres = gfin_ref[...] + norm_back(n2, rstd, gn2, gain_ref[...])
+        n2, rstd = norm_parts(both_ref[0])
+        gres = both_ref[1] + norm_back(n2, rstd, gn2, vec_ref[6:7, :])
         gres_ref[...] = gres
         branch = gres.astype(BF)
         for d in range(ZS):
             spot = pl.ds(pl.multiple_of(lax.rem(place_ref[0] + d, ZS) * group, group), group)
-            gctx_refs[d][...] = dot_nt(branch, w_ref[spot, at:at + width]).astype(BF)
+            gctx_refs[d][...] = dot_nt(branch, w_ref[spot, :]).astype(BF)
         for d in range(ZS):
             spot = pl.ds(pl.multiple_of(lax.rem(place_ref[0] + ZS - d, ZS) * group, group), group)
-            gw_ref[spot, :] = dot_tn(p_refs[d][...], branch).astype(BF)
+            gw_ref[spot, :] = dot_tn(cat_ref[:, d * group:(d + 1) * group], branch).astype(BF)
         rowsum = lambda v: jnp.sum(v, 0, keepdims=True)
         sums_ref[0:1, :] = rowsum(branch.astype(F32))
-        sums_ref[1:2, :] = rowsum(gmlp_ref[...].astype(F32))
-        sums_ref[2:3, :] = rowsum(gn2 * n2)
-        sums_ref[3:4, :] = rowsum(gn2)
-
-    outs = [((rows, width), F32)] + [((rows, group), BF)] * ZS + [((width, width), BF), ((4, width), F32)]
-    return call(body, (place, *terms, residual, gain, gfin, *pieces, w_out, gmlp), outs, "out_back", 1, after)
-
-
-def join_back(place, terms, dq, w):
+        sums_ref[1:2, :] = rowsum(gn2 * n2)
+        sums_ref[2:3, :] = rowsum(gn2)
+
+    outs = [((rows, width), F32)] + [((rows, group), BF)] * ZS + [((width, width), BF), ((3, width), F32)]
+    args = (place, *terms, res_and_grad, vectors, ctx_cat, Part(mid, ff, ff + width))
+    return call(body, args, outs, "out_back", 1, after)
+
+
+def join_back(place, terms, dq, one):
     total, group = dq.shape
-    width = w.shape[0]
+    width = one.shape[0]
     rows = total // ZS
     size = len(terms)
     cols = 3 * group
@@ -587,25 +628,25 @@
             spot = pl.ds(pl.multiple_of(lax.rem(place_ref[0] + d, ZS) * rows, rows), rows)
             out_refs[d][...] = gn1_ref[spot, :].astype(out_refs[d].dtype)
 
-    outs = [((total, cols), BF), ((total, width), F32)] + [((rows, width), BF if d else F32) for d in range(ZS)]
-    return call(body, (place, *terms, dq, w), outs, "join_back", 1)
-
-
-def weights_back(place, n1, grad_joined, gn1, pieces, out_sums, up_rows, marks, gw_out, wr):
+    outs = [((total, cols), BF), ((total, width), F32), ((rows, width), F32)] + [((rows, width), BF)] * (ZS - 1)
+    return call(body, (place, *terms, dq, one), outs, "join_back", 1)
+
+
+def weights_back(place, n1, grad_joined, gn1, hidden, out_sums, fin_sums, up_rows, gw_out, wr, devices):
     total, cols = grad_joined.shape
     width = n1.shape[1]
     rows = total // ZS
     group = cols // 3
     upc = up_rows.shape[0]
-    markc = marks.shape[0]
     chips = width // (2 * wr)
-    wide = cols + LANES + width
-
-    def body(place_ref, n1_ref, gj_ref, gn1_ref, h0, h1, h2, h3, sums_ref, up_ref, marks_ref, gw_ref, kept_ref, sent_ref, vec, full):
+    wide = width + cols + HEAD_DIM + LANES
+    slots = -(-devices // wr)
+
+    def body(place_ref, n1_ref, gj_ref, gn1_ref, hidden_ref, sums_ref, fin_ref, up_ref, gw_ref, kept_ref, sent_ref, vec, full):
         gain_sum = jnp.zeros((1, width), F32)
-        for d, piece in enumerate((h0, h1, h2, h3)):
-            spot = pl.ds(pl.multiple_of(lax.rem(place_ref[0] + ZS - d, ZS) * rows, rows), rows)
-            normed, _ = norm_parts(piece[...].astype(F32))
+        for z in range(ZS):
+            spot = slice(z * rows, (z + 1) * rows)
+            normed, _ = norm_parts(hidden_ref[spot, :].astype(F32))
             gain_sum = gain_sum + jnp.sum(gn1_ref[spot, :] * normed, 0, keepdims=True)
         joined_sums = jnp.sum(gj_ref[...].astype(F32), 0, keepdims=True)
         vec[...] = jnp.zeros_like(vec)
@@ -616,15 +657,22 @@
             vec[0:1, at:at + group] = jnp.where(here, joined_sums[:, 2 * group:], 0.0)
             vec[1:2, at:at + 2 * hd] = jnp.where(here, joined_sums[:, 4 * hd:6 * hd], 0.0)
             vec[1:2, at + 2 * hd:at + 3 * hd] = jnp.where(here, joined_sums[:, 3 * hd:4 * hd], 0.0)
-        vec[2:4, :] = sums_ref[0:2, :]
+        vec[2:3, :] = sums_ref[0:1, :]
+        vec[3:4, :] = fin_ref[1:2, :]
         vec[4:5, :] = gain_sum
         vec[5:6, :] = jnp.sum(gn1_ref[...], 0, keepdims=True)
-        vec[6:8, :] = sums_ref[2:4, :]
+        vec[6:8, :] = sums_ref[1:3, :]
         vec[8:8 + upc, :] = up_ref[...]
-        vec[16:16 + markc, :] = marks_ref[...]
-        full[:, 0:cols] = dot_tn(n1_ref[...], gj_ref[...])
-        full[:, cols:cols + LANES] = vec[...].T
-        full[:, cols + LANES:] = gw_ref[...].astype(F32)
+        error = jnp.sum(fin_ref[0:1, :], -1, keepdims=True)
+        high = error.astype(BF).astype(F32)
+        turn = lax.rem(lax.broadcasted_iota(jnp.int32, (1, width), 1), wr)
+        for s in range(slots):
+            vec[16 + s:17 + s, :] = jnp.where(turn + s * wr == place_ref[2], high, 0.0)
+        vec[16 + slots:17 + slots, :] = jnp.where(turn == 0, error - high, 0.0)
+        full[:, 0:width] = gw_ref[...].astype(F32)
+        full[:, width:width + cols] = dot_tn(n1_ref[...], gj_ref[...])
+        full[:, width + cols:width + cols + hd] = jnp.zeros((width, hd), F32)
+        full[:, width + cols + hd:] = vec[...].T
         for c in range(2):
             @pl.when(place_ref[1] == c)
             def _():
@@ -635,21 +683,22 @@
 
     outs = [((chips, wr, wide), BF)] * 2
     scratch = [pltpu.VMEM((LANES, width), F32), pltpu.VMEM((width, wide), F32)]
-    return call(body, (place, n1, grad_joined, gn1, *pieces, out_sums, up_rows, marks, gw_out), outs, "weights_back", 1, scratch=scratch, mib=28)
-
-
-def input_back(terms, hidden, gain, grad_res):
+    return call(body, (place, n1, grad_joined, gn1, hidden, out_sums, fin_sums, up_rows, gw_out), outs, "weights_back", 1, scratch=scratch, mib=20)
+
+
+def input_back(terms, hidden, vectors, grad_res):
     rows, width = hidden.shape
 
-    def body(t0, t1, t2, t3, hidden_ref, gain_ref, gres_ref, out_ref):
+    def body(t0, t1, t2, t3, hidden_ref, gain_ref, gres_ref, out_ref, done_ref):
         back = t0[...] + t1[...].astype(F32) + t2[...].astype(F32) + t3[...].astype(F32)
         normed, rstd = norm_parts(hidden_ref[...].astype(F32))
-        out_ref[...] = gres_ref[...] + norm_back(normed, rstd, back, gain_ref[...])
-
-    return call(body, (*terms, hidden, gain, grad_res), [((rows, width), F32)], "input_back")[0]
-
-
-def unpack_one(place, pieces):
+        out_ref[...] = gres_ref[...] + norm_back(normed, rstd, back, gain_ref[4:5, :])
+        done_ref[...] = jnp.zeros_like(done_ref)
+
+    return call(body, (terms[0], *terms[1:], hidden, vectors, grad_res), [((rows, width), F32), ((8, LANES), F32)], "input_back")
+
+
+def unpack_one(place, pieces, after):
     rows, wide = pieces[0].shape[-2:]
     hd = HEAD_DIM
     group = 3 * hd
@@ -658,20 +707,23 @@
     def body(place_ref, p0, p1, p2, p3, qkv_ref, vec_ref, out_ref, held_ref):
         for d, piece in enumerate((p0, p1, p2, p3)):
             held_ref[pl.ds(lax.rem(place_ref[0] + ZS - d, ZS), 1)] = piece[...].reshape(1, rows, wide).astype(F32)
-        total = jnp.zeros((rows, LANES + width), F32)
+        vec_total = jnp.zeros((rows, LANES), F32)
+        out_total = jnp.zeros((rows, width), F32)
         for g in range(ZS):
             k = width + g * group
             v = 2 * width + g * group
-            qkv_ref[:, k:k + 3 * hd] = held_ref[g, :, 0:3 * hd]
-            qkv_ref[:, v + 2 * hd:v + 3 * hd] = held_ref[g, :, 3 * hd:4 * hd]
-            qkv_ref[:, v:v + 2 * hd] = held_ref[g, :, 4 * hd:6 * hd]
-            qkv_ref[:, g * group:g * group + 3 * hd] = held_ref[g, :, 6 * hd:9 * hd]
-            total = total + held_ref[g, :, 9 * hd:]
-        vec_ref[...] = total[:, 0:LANES]
-        out_ref[...] = total[:, LANES:]
+            at = width
+            qkv_ref[:, k:k + 3 * hd] = held_ref[g, :, at:at + 3 * hd]
+            qkv_ref[:, v + 2 * hd:v + 3 * hd] = held_ref[g, :, at + 3 * hd:at + 4 * hd]
+            qkv_ref[:, v:v + 2 * hd] = held_ref[g, :, at + 4 * hd:at + 6 * hd]
+            qkv_ref[:, g * group:g * group + 3 * hd] = held_ref[g, :, at + 6 * hd:at + 9 * hd]
+            vec_total = vec_total + held_ref[g, :, at + 10 * hd:]
+            out_total = out_total + held_ref[g, :, 0:width]
+        vec_ref[...] = vec_total
+        out_ref[...] = out_total
 
     outs = [((rows, 3 * width), F32), ((rows, LANES), F32), ((rows, width), F32)]
-    return call(body, (place, *pieces), outs, "unpack_one", 1, scratch=[pltpu.VMEM((ZS, rows, wide), F32)])
+    return call(body, (place, *pieces), outs, "unpack_one", 1, after, scratch=[pltpu.VMEM((ZS, rows, wide), F32)])
 
 
 def per_device(hidden_in, w_qkv, q_bias, v_bias, w_out, out_bias, w_up, up_bias, w_down, down_bias, ln1_gain, ln1_bias, ln2_gain, ln2_bias, segment_ids, padding_mask, teacher, cotangent):
@@ -698,85 +750,72 @@
         return [lax.dynamic_slice_in_dim(value, lax.rem(iz + d, sz), 1, 0) for d in range(sz)]
 
     flat = jnp.concatenate([jnp.stack([q_bias, v_bias, out_bias, down_bias, ln1_gain, ln1_bias, ln2_gain, ln2_bias]), up_bias.reshape(upc, wr)])
-    one_z = to_z(cut_z(pack_one(w_qkv, flat, segment_ids, padding_mask)))
     hidden = hidden_in[0]
     pieces = from_z(hidden)
-    one = arrange(one_z, iz, 0)
+    targets = jnp.concatenate([teacher, cotangent], 0)
+    one = arrange(to_z(cut_z(pack_one(w_qkv, flat, segment_ids, padding_mask))), iz, 0)
     one = gather(one[None, :, None], "x", 2)
     one = gather(one, "y", 0)[:, :, :, None]
     one = gather(one, "core", 3).reshape(width, -1)
 
-    mid = pack_up(w_up, w_out, ffd, sx)
-    mid = arrange([lax.dynamic_slice_in_dim(mid, core, 1, 0), shift(lax.dynamic_slice_in_dim(mid, 1 - core, 1, 0), "core", 1)], core, 0)
-    mid_x = [lax.dynamic_slice_in_dim(mid, lax.rem(ix + d, sx), 1, 1) for d in range(sx)]
-    mid = arrange([mid_x[0]] + [shift(mid_x[d], "x", d) for d in range(1, sx)], ix, 1)
-    weights = [mid.transpose(1, 0, 2, 3).reshape(2 * sx * wr, ff + width), w_down]
+    up = pack_up(w_up, w_out, ffd, sx)
+    up = arrange([lax.dynamic_slice_in_dim(up, core, 1, 0), shift(lax.dynamic_slice_in_dim(up, 1 - core, 1, 0), "core", 1)], core, 0)
+    up_x = [lax.dynamic_slice_in_dim(up, lax.rem(ix + d, sx), 1, 1) for d in range(sx)]
+    up = arrange([up_x[0]] + [shift(up_x[d], "x", d) for d in range(1, sx)], ix, 1)
+    weights = [up.transpose(1, 0, 2, 3).reshape(2 * sx * wr, ff + width), w_down]
     if ff == width:
         weights = [jnp.concatenate(weights, 1)]
     weights = [lax.all_gather(member, ("y", "z"), axis=0, tiled=True) for member in weights]
-    mid = weights[0]
-
-    vec = one[:, wcols:wcols + LANES]
-    vec_rows = vec[:, :16].T.astype(F32)
-    qb, vb, ob, db, g1, b1, g2, b2 = (vec_rows[i][None] for i in range(8))
-    ub = vec_rows[8:8 + upc].reshape(upc, sy * sz, sx * 2, wr)
+
+    vec = one[:, wcols:]
+    vectors = jnp.concatenate([vec[:, :15].T.astype(F32), jnp.pad(padding_mask.astype(F32), ((0, 0), (0, width - rows)))])
+    ub = vectors[8:8 + upc].reshape(upc, sy * sz, sx * 2, wr)
     ub = lax.dynamic_index_in_dim(ub, ix * 2 + core, 2, keepdims=False).transpose(1, 0, 2).reshape(1, ff)
-    count = jnp.sum(vec_rows[8 + upc]) / wr
+    wide = max(ff, width)
+    biases = jnp.concatenate([jnp.pad(ub, ((0, 0), (0, wide - ff))), jnp.pad(vectors[3:4], ((0, 0), (0, wide - width)))])
+    count = jnp.sum(vectors[8 + upc]) / wr
     seg = lax.dynamic_index_in_dim(vec.reshape(sy, sz * sx * 2, wr, LANES), iy, 0, keepdims=False)[:, :2, HEAD_DIM:].astype(F32).reshape(sz * sx * 2, rows)
-    qb_g = lax.dynamic_slice_in_dim(qb, iz * group, group, 1)
-    vb_g = lax.dynamic_slice_in_dim(vb, iz * group, group, 1)
-    bkv = jnp.concatenate([jnp.zeros((1, group), F32), vb_g[:, 2 * HEAD_DIM:], vb_g[:, :2 * HEAD_DIM]], 1)
     spots = [(lax.rem(ix + sx - d, sx), core) for d in range(sx)]
     spots = spots + [(at, 1 - core) for at, _ in spots]
     order = jnp.stack([at * 2 + c for at, c in spots] + [iz]).astype(jnp.int32)
-    yplace = iy.astype(jnp.int32).reshape(1)
-
-    n1_low, q, kv = project(place, pieces, one, g1, b1, bkv, qb_g)
+
+    n1_low, q, kv, hidden_all = project(place, pieces, one, vectors)
     kvs = spread_tokens(kv)
     *ctx_parts, ctx, tot = attend(order, q, seg, kvs)
-    ctx_parts = to_z(ctx_parts)
-    residual, n2_low = out_project(place, ctx_parts, mid, ob, hidden, g2, b2, ff, after=[ub])
-    n2_all = spread_tokens(n2_low)
-    kept, sent, act, slope = mlp_up(n2_all, weights, ub)
-    layer_out, errors, grad_final, grad_mlp = finish(fold_tokens(kept, sent), residual, db, teacher[0], cotangent[0], padding_mask, (2.0 / (count * width)).reshape(1))
-
-    grads = spread_tokens(grad_mlp)
-    kept, sent, grad_pre = mlp_back(grads, weights, slope)
+    residual, n2_low, ctx_cat = out_project(place, to_z(ctx_parts), weights[0], ff, hidden, vectors, after=[biases])
+    kept, sent, act, slope, n2_all = mlp_up(spread_tokens(n2_low), weights, biases, ff)
+    layer_out, fin_sums, res_and_grad, grad_mlp = finish(fold_tokens(kept, sent), residual, targets, (2.0 / (count * width)).reshape(1))
+
+    kept, sent, grad_pre, grads = mlp_back(spread_tokens(grad_mlp), weights, slope)
     gn2_terms = fold_tokens(kept, sent)
-    gw_mlp, up_sums = mlp_weights(grads, act, n2_all, grad_pre)
+    gw_mlp, up_sums = mlp_weights(grads, act, n2_all, grad_pre, after=gn2_terms[:1])
     gw_sums = [lax.psum_scatter(member, ("y", "z"), scatter_dimension=0, tiled=True) for member in gw_mlp]
-    grad_res, *gctx, gw_out, out_sums = out_back(place, gn2_terms, residual, g2, grad_final, ctx_parts, mid, grad_mlp, ff, after=gw_mlp)
+    grad_res, *gctx, gw_out, out_sums = out_back(place, gn2_terms, res_and_grad, vectors, ctx_cat, weights[0], ff, after=[up_sums])
     dq, dkv_kept, dkv_sent = attend_back(order, q, to_z(gctx), ctx, tot, seg, kvs)
-    dkv_terms = fold_tokens(dkv_kept, dkv_sent)
-    grad_joined, gn1, *gn1_parts = join_back(place, dkv_terms, dq, one)
-    input_grad = input_back(to_z(gn1_parts), hidden, g1, grad_res)
+    grad_joined, gn1, *gn1_parts = join_back(place, fold_tokens(dkv_kept, dkv_sent), dq, one)
+    input_grad, back_done = input_back(to_z(gn1_parts), hidden, vectors, grad_res)
 
     up_rows = jnp.zeros((upc, sy * sz, sx * 2, wr), F32)
     up_rows = lax.dynamic_update_slice_in_dim(up_rows, up_sums.reshape(sy * sz, upc, wr).transpose(1, 0, 2)[:, :, None], ix * 2 + core, 2).reshape(upc, width)
-    slots = -(-devices // wr)
-    error = jnp.sum(errors)
-    high = error.astype(BF).astype(F32)
-    turn = lax.broadcasted_iota(jnp.int32, (slots, width), 1) % wr
-    at = turn + wr * lax.broadcasted_iota(jnp.int32, (slots, width), 0)
-    marks = jnp.concatenate([jnp.where(at == device, high, 0.0), jnp.where(turn[:1] == 0, error - high, 0.0)])
-    at_zc = jnp.stack([iz, core]).astype(jnp.int32)
-    kept, sent = weights_back(at_zc, n1_low, grad_joined, gn1, pieces, out_sums, up_rows, marks, gw_out, wr)
-    grid = (sy, sz, sx, wr, kept.shape[-1])
-    third = fold(kept.reshape(grid), [shift(sent, "core", 1).reshape(grid)], iy, 0, sy, "fold_core")
-    third = fold(third[0], passed(third, "y"), ix, 2, sx, "fold_y")
-    third = fold(third[0], passed(third, "x"), iz, 1, sz, "fold_x")
+    places = jnp.stack([iz, core, device]).astype(jnp.int32)
+    kept, sent = weights_back(places, n1_low, grad_joined, gn1, hidden_all, out_sums, fin_sums, up_rows, gw_out, wr, devices)
+    third = fold_both(kept.reshape(sy, sz, sx, wr, -1), shift(sent, "core", 1).reshape(sy, sz, sx, wr, -1), ix, iy, width)
+    third = fold_cross(third[:sx], passed(third[:sx], "x"), third[sx:], passed(third[sx:], "y"), ix, iy)
+    third = fold_last(third[:sy], passed(third[:sy], "y"), third[sy:], passed(third[sy:], "x"), iz, after=[back_done])
+    ready = third[0][0, 0, 0, :, :LANES]
+    gw_sums = [held(member, [ready]) for member in gw_sums]
     third = [third[0]] + passed(third, "z")
-    grad_w_qkv, sums, gw_out = unpack_one(place, third)
-    sums = sums.T
-    loss = jnp.sum(sums[16:17 + slots]) / (count * width)
 
     gw_down = gw_sums[0][:, :width].astype(F32)
-    gw_up = gw_sums[-1][:, -ff:]
-    gw_up = gw_up.reshape(1, 1, sx, 2, wr, ff)
+    gw_up = gw_sums[-1][:, -ff:].reshape(1, 1, sx, 2, wr, ff)
     up_x = [lax.dynamic_slice_in_dim(gw_up, lax.rem(ix + d, sx), 1, 2) for d in range(sx)]
     gw_up = arrange([up_x[0]] + [shift(up_x[d], "x", d) for d in range(1, sx)], ix, 2)
     gw_up = arrange([lax.dynamic_slice_in_dim(gw_up, core, 1, 3), shift(lax.dynamic_slice_in_dim(gw_up, 1 - core, 1, 3), "core", 1)], core, 3)
     gw_up = gw_up.reshape(sx, 2, wr, sy * sz, ffd).transpose(2, 3, 0, 1, 4).reshape(wr, -1).astype(F32)
+
+    grad_w_qkv, sums, gw_out = unpack_one(place, third, after=[gw_up])
+    sums = sums.T
+    loss = jnp.sum(sums[16:17 + -(-devices // wr)]) / (count * width)
     return (
         layer_out[None], loss, input_grad[None], grad_w_qkv, sums[0], sums[1], gw_out, sums[2],
         gw_up, sums[8:8 + upc].reshape(-1), gw_down, sums[3], sums[4], sums[5], sums[6], sums[7],

time: 286 us -> 271 us (0.948)
  local copies, waits for them, and re-layouts: 48 us -> 37.5 us
  other arithmetic: 7.1 us -> 3.91 us
    unnamed x221 -> x171, local copies, waits for them, and re-layouts: 42.6 us -> 33.6 us
    ppermute x43 -> x45, starting transfers between devices: 56.3 us -> 58.5 us  [shift(): lax.ppermute(value, axis, [(a, (a + step) % size) for a in range(size)])]
    ppermute x43 -> x45, waiting for transfers between devices: 123 us -> 121 us  [shift(): lax.ppermute(value, axis, [(a, (a + step) % size) for a in range(size)])]
    pallas_call x20 -> x21, Pallas kernels: 30.7 us -> 31.2 us  [call(): pl.pallas_call(whole, in_specs=specs + [pl.BlockSpec(memory_space=pl.ANY)...]
  transfers between devices with their start and end apart: 45 -> 47, of which waited for: 31 -> 33; matrix products, arithmetic and copies ran while one was open for 3% -> 1% of each run, Pallas kernels for 7% -> 8%
where the time goes in v1:
time: 271 us; the launch traced here: 270 us
  waiting for transfers between devices  121 us (45%)
  starting transfers between devices  58.6 us (22%)
  local copies, waits for them, and re-layouts  37.5 us (14%)
  Pallas kernels  31.5 us (12%)
  between operations  17.5 us (6%)
  other arithmetic  3.91 us (1%)
    ppermute x45, waiting for transfers between devices, shift(): lax.ppermute(value, axis, [(a, (a + step) % size) for a in range(size)])  121 us
    ppermute x45, starting transfers between devices, shift(): lax.ppermute(value, axis, [(a, (a + step) % size) for a in range(size)])  58.5 us
    unnamed x171, local copies, waits for them, and re-layouts  33.6 us
    pallas_call x21, Pallas kernels, call(): pl.pallas_call(whole, in_specs=specs + [pl.BlockSpec(memory_space=pl.ANY)...  31.2 us
  transfers between devices with their start and end apart: 47, of which 33 were waited for; matrix products, arithmetic and copies ran while one was open for 1% of the time, Pallas kernels for 8%

profile of v1, /device:TPU:0, one launch (start us, length us, event | category | flops | bytes accessed | tf_op | source)
XLA Modules:
  0.0 270.3 jit_solution(11160207007368313785)
XLA Ops:
  10.7 2.9 %collective-permute-start.16 = (bf16[2,1,24,1536]{3,2,1,0:T(8,128)(2,1)S(1)}, bf16[2,1,24,1536]{3,2,1,0:T(8,128)(2,1)S(1)}, u32[]{:S(2)}, u32[]{:S(2)}) collective-permute-start(bf16[2,1,24,1536]{3,2,1,0:T(8,128)(2,1)S(1)} %get-tuple-element.164), channel_id=1, source_target_pairs={{0,2},{2,0},{1,3},{3,1},{4,6},{6,4},{5,7},{7,5},{8,10},{10,8},{9,1... | collective-permute-start | bytes 442376 | tf_op jit(solution)/shard_map/ppermute | solution.py:22
  13.6 4.2 %collective-permute-done.16.refs_1_ = bf16[2,1,24,1536]{3,2,1,0:T(8,128)(2,1)S(1)} collective-permute-done((bf16[2,1,24,1536]{3,2,1,0:T(8,128)(2,1)S(1)}, bf16[2,1,24,1536]{3,2,1,0:T(8,128)(2,1)S(1)}, u32[]{:S(2)}, u32[]{:S(2)}) %collective-permute-start.16) | collective-permute-done | bytes 147488 | tf_op jit(solution)/shard_map/ppermute | solution.py:22
  19.3 1.9 collective-permute-start
  21.1 2.6 collective-permute-start.1
  27.7 1.6 collective-permute-start.3
  29.3 3.7 %collective-permute-done.3.refs_1_ = bf16[1,4,1,24,704]{4,3,2,1,0:T(8,128)(2,1)S(1)} collective-permute-done((bf16[1,4,1,24,704]{4,3,2,1,0:T(8,128)(2,1)S(1)}, bf16[1,4,1,24,704]{4,3,2,1,0:T(8,128)(2,1)S(1)}, u32[]{:S(2)}, u32[]{:S(2)}) %collective-permute-start.3) | collective-permute-done | bytes 135200 | tf_op jit(solution)/shard_map/ppermute | solution.py:22
  33.0 1.6 collective-permute-start.4
  34.5 7.7 %collective-permute-done.4.refs_1_ = bf16[1,4,2,24,704]{4,3,2,1,0:T(8,128)(2,1)S(1)} collective-permute-done((bf16[1,4,2,24,704]{4,3,2,1,0:T(8,128)(2,1)S(1)}, bf16[1,4,2,24,704]{4,3,2,1,0:T(8,128)(2,1)S(1)}, u32[]{:S(2)}, u32[]{:S(2)}) %collective-permute-start.4) | collective-permute-done | bytes 270368 | tf_op jit(solution)/shard_map/ppermute | solution.py:22
  42.4 1.5 collective-permute-start.6
  43.9 2.4 collective-permute-start.7
  47.8 5.5 %collective-permute-done.6.refs_2_ = bf16[128,768]{1,0:T(8,128)(2,1)S(1)} collective-permute-done((bf16[128,768]{1,0:T(8,128)(2,1)S(1)}, bf16[128,768]{1,0:T(8,128)(2,1)S(1)}, u32[]{:S(2)}, u32[]{:S(2)}) %collective-permute-start.6) | collective-permute-done | bytes 196640 | tf_op jit(solution)/shard_map/ppermute | solution.py:22
  53.3 8.3 %collective-permute-done.7.refs_3_ = bf16[128,768]{1,0:T(8,128)(2,1)S(1)} collective-permute-done((bf16[128,768]{1,0:T(8,128)(2,1)S(1)}, bf16[128,768]{1,0:T(8,128)(2,1)S(1)}, u32[]{:S(2)}, u32[]{:S(2)}) %collective-permute-start.7) | collective-permute-done | bytes 196640 | tf_op jit(solution)/shard_map/ppermute | solution.py:22
  66.4 9.3 %collective-permute-done.9.refs_4_.refs_10_ = bf16[512,384]{1,0:T(8,128)(2,1)S(1)} collective-permute-done((bf16[512,384]{1,0:T(8,128)(2,1)S(1)}, bf16[512,384]{1,0:T(8,128)(2,1)S(1)}, u32[]{:S(2)}, u32[]{:S(2)}) %collective-permute-start.9) | collective-permute-done | bytes 393248 | tf_op jit(solution)/shard_map/ppermute | solution.py:22
  77.4 4.4 %attend.1 = (bf16[128,192]{1,0:T(8,128)(2,1)S(1)}, bf16[128,192]{1,0:T(8,128)(2,1)S(1)}, bf16[128,192]{1,0:T(8,128)(2,1)S(1)}, bf16[128,192]{1,0:T(8,128)(2,1)S(...) custom-call(s32[5]{0:T(128)S(1)} %stack.68.refs_0_, bf16[512,256]{1,0:T(8,128)(2,1)S(1)} %get-tuple-element.85.refs_1_, ...), custom_call_target="tpu_custom_call" | custom-call | flops 1 | bytes 1 | tf_op jit(solution)/shard_map/attend/pallas_call | solution.py:392
  84.1 8.5 %collective-permute-start.12 = (bf16[128,192]{1,0:T(8,128)(2,1)S(1)}, bf16[128,192]{1,0:T(8,128)(2,1)S(1)}, u32[]{:S(2)}, u32[]{:S(2)}) collective-permute-start(bf16[128,192]{1,0:T(8,128)(2,1)S(1)} %get-tuple-element.88), channel_id=1, source_target_pairs={{0,4},{4,8},{8,12},{12,0},{1,5},{5,9},{9,13},{13,1},{2,6},{6,10},{... | collective-permute-start | bytes 147464 | tf_op jit(solution)/shard_map/ppermute | solution.py:22
  92.5 2.4 collective-permute-start.14
  95.5 4.2 %collective-permute-done.13.refs_3_ = bf16[128,192]{1,0:T(8,128)(2,1)S(1)} collective-permute-done((bf16[128,192]{1,0:T(8,128)(2,1)S(1)}, bf16[128,192]{1,0:T(8,128)(2,1)S(1)}, u32[]{:S(2)}, u32[]{:S(2)}) %collective-permute-start.13) | collective-permute-done | bytes 49184 | tf_op jit(solution)/shard_map/ppermute | solution.py:22
  101.0 2.0 copy-done
  109.5 1.5 collective-permute-start.17
  111.0 5.1 %collective-permute-done.17.refs_1_ = bf16[128,768]{1,0:T(8,128)(2,1)S(1)} collective-permute-done((bf16[128,768]{1,0:T(8,128)(2,1)S(1)}, bf16[128,768]{1,0:T(8,128)(2,1)S(1)}, u32[]{:S(2)}, u32[]{:S(2)}) %collective-permute-start.17) | collective-permute-done | bytes 196640 | tf_op jit(solution)/shard_map/ppermute | solution.py:22
  117.6 2.3 mlp_up.1
  122.8 1.6 collective-permute-done.20.refs_1_
  125.9 1.5 collective-permute-start.21
  128.8 4.3 %collective-permute-done.21.refs_2_ = bf16[128,768]{1,0:T(8,128)(2,1)} collective-permute-done((bf16[128,768]{1,0:T(8,128)(2,1)}, bf16[128,768]{1,0:T(8,128)(2,1)}, u32[]{:S(2)}, u32[]{:S(2)}) %collective-permute-start.21) | collective-permute-done | bytes 196640 | tf_op jit(solution)/shard_map/ppermute | solution.py:22
  136.1 2.0 finish.1
  141.1 4.6 %collective-permute-done.22.refs_1_ = bf16[128,768]{1,0:T(8,128)(2,1)S(1)} collective-permute-done((bf16[128,768]{1,0:T(8,128)(2,1)S(1)}, bf16[128,768]{1,0:T(8,128)(2,1)S(1)}, u32[]{:S(2)}, u32[]{:S(2)}) %collective-permute-start.22) | collective-permute-done | bytes 196640 | tf_op jit(solution)/shard_map/ppermute | solution.py:22
  147.2 2.9 %mlp_back.1 = (f32[2,128,768]{2,1,0:T(8,128)S(1)}, bf16[2,128,768]{2,1,0:T(8,128)(2,1)S(1)}, bf16[512,768]{1,0:T(8,128)(2,1)S(1)}, bf16[512,768]{1,0:T(8,128)(2,1)S(1)}) custom-call(bf16[128,768]{1,0:T(8,128)(2,1)S(1)} %get-tuple-element.99.refs_0_, bf16[128,768]{1,0:T(8,128)(2,1)S(1)} %collective-permute-done.22.refs_1_, ...), custom_call_target="tpu_custom_call" | custom-call | flops 1 | bytes 1 | tf_op jit(solution)/shard_map/mlp_back/pallas_call | solution.py:392
  150.3 1.6 collective-permute-done.25.refs_1_
  154.1 1.5 copy-done.4
  155.6 1.5 collective-permute-start.26
  157.1 5.7 %collective-permute-done.26.refs_2_ = bf16[128,768]{1,0:T(8,128)(2,1)S(1)} collective-permute-done((bf16[128,768]{1,0:T(8,128)(2,1)}, bf16[128,768]{1,0:T(8,128)(2,1)S(1)}, u32[]{:S(2)}, u32[]{:S(2)}) %collective-permute-start.26) | collective-permute-done | bytes 196640 | tf_op jit(solution)/shard_map/ppermute | solution.py:22
  171.6 2.1 collective-permute-start.28
  174.1 4.4 %collective-permute-done.27.refs_3_ = bf16[128,192]{1,0:T(8,128)(2,1)S(1)} collective-permute-done((bf16[128,192]{1,0:T(8,128)(2,1)S(1)}, bf16[128,192]{1,0:T(8,128)(2,1)S(1)}, u32[]{:S(2)}, u32[]{:S(2)}) %collective-permute-start.27) | collective-permute-done | bytes 49184 | tf_op jit(solution)/shard_map/ppermute | solution.py:22
  178.5 4.1 %collective-permute-done.28.refs_4_ = bf16[128,192]{1,0:T(8,128)(2,1)S(1)} collective-permute-done((bf16[128,192]{1,0:T(8,128)(2,1)S(1)}, bf16[128,192]{1,0:T(8,128)(2,1)S(1)}, u32[]{:S(2)}, u32[]{:S(2)}) %collective-permute-start.28) | collective-permute-done | bytes 49184 | tf_op jit(solution)/shard_map/ppermute | solution.py:22
  182.7 6.5 %attend_back.1 = (bf16[512,192]{1,0:T(8,128)(2,1)S(1)}, f32[2,512,384]{2,1,0:T(8,128)S(1)}, bf16[2,512,384]{2,1,0:T(8,128)(2,1)S(1)}) custom-call(s32[5]{0:T(128)S(1)} %copy-done.69, bf16[512,256]{1,0:T(8,128)(2,1)S(1)} %copy-done.27, bf16[128,192]{1,0:T(8,128)(2,1)S(1)} %get-tuple-element.112.refs_2_, bf16[128,192]{1,0:T(8,128)(2,1)S(1)} %collective-permute-done.27.refs_3_, ...), custom_call_target="tpu_custom_call" | custom-call | flops 1 | bytes 1 | tf_op jit(solution)/shard_map/attend_back/pallas_call | solution.py:392
  189.3 2.3 collective-permute-done.30.refs_1_
  192.4 1.6 collective-permute-start.31
  194.5 9.3 %collective-permute-done.31.refs_2_ = bf16[512,384]{1,0:T(8,128)(2,1)S(1)} collective-permute-done((bf16[512,384]{1,0:T(8,128)(2,1)}, bf16[512,384]{1,0:T(8,128)(2,1)S(1)}, u32[]{:S(2)}, u32[]{:S(2)}) %collective-permute-start.31) | collective-permute-done | bytes 393248 | tf_op jit(solution)/shard_map/ppermute | solution.py:22
  205.3 2.2 weights_back.1
  207.6 2.8 %collective-permute-done.32 = bf16[16,24,1536]{2,1,0:T(8,128)(2,1)S(1)} collective-permute-done((bf16[16,24,1536]{2,1,0:T(8,128)(2,1)S(1)}, bf16[16,24,1536]{2,1,0:T(8,128)(2,1)S(1)}, u32[]{:S(2)}, u32[]{:S(2)}) %collective-permute-start.32) | collective-permute-done | bytes 1179680 | tf_op jit(solution)/shard_map/ppermute | solution.py:22
  211.3 1.7 collective-permute-start.33
  213.0 3.9 %collective-permute-start.37 = (bf16[128,768]{1,0:T(8,128)(2,1)S(1)}, bf16[128,768]{1,0:T(8,128)(2,1)S(1)}, u32[]{:S(2)}, u32[]{:S(2)}) collective-permute-start(bf16[128,768]{1,0:T(8,128)(2,1)S(1)} %get-tuple-element.140), channel_id=1, source_target_pairs={{0,4},{4,8},{8,12},{12,0},{1,5},{5,9},{9,13},{13,1},{2,6},{6,10},{... | collective-permute-start | bytes 589832 | tf_op jit(solution)/shard_map/ppermute | solution.py:22
  217.7 1.6 collective-permute-start.39
  220.4 4.5 %collective-permute-done.34.refs_4_ = bf16[1,4,2,24,768]{4,3,2,1,0:T(8,128)(2,1)S(1)} collective-permute-done((bf16[1,4,2,24,768]{4,3,2,1,0:T(8,128)(2,1)S(1)}, bf16[1,4,2,24,768]{4,3,2,1,0:T(8,128)(2,1)S(1)}, u32[]{:S(2)}, u32[]{:S(2)}) %collective-permute-start.34) | collective-permute-done | bytes 294944 | tf_op jit(solution)/shard_map/ppermute | solution.py:22
  226.5 12.8 %collective-permute-done.38.refs_2_ = bf16[128,768]{1,0:T(8,128)(2,1)S(1)} collective-permute-done((bf16[128,768]{1,0:T(8,128)(2,1)S(1)}, bf16[128,768]{1,0:T(8,128)(2,1)S(1)}, u32[]{:S(2)}, u32[]{:S(2)}) %collective-permute-start.38) | collective-permute-done | bytes 196640 | tf_op jit(solution)/shard_map/ppermute | solution.py:22
  243.3 3.5 %collective-permute-done.43.refs_1_ = bf16[1,1,1,2,24,768]{5,4,3,2,1,0:T(8,128)(2,1)S(1)} collective-permute-done((bf16[1,1,1,2,24,768]{5,4,3,2,1,0:T(8,128)(2,1)S(1)}, bf16[1,1,1,2,24,768]{5,4,3,2,1,0:T(8,128)(2,1)S(1)}, u32[]{:S(2)}, u32[]{:S(2)}) %collective-permute-start.43) | collective-permute-done | bytes 73760 | tf_op jit(solution)/shard_map/ppermute | solution.py:22
  246.9 4.7 %collective-permute-start.40 = (bf16[1,1,1,24,1536]{4,3,2,1,0:T(8,128)(2,1)S(1)}, bf16[1,1,1,24,1536]{4,3,2,1,0:T(8,128)(2,1)S(1)}, u32[]{:S(2)}, u32[]{:S(2)}) collective-permute-start(bf16[1,1,1,24,1536]{4,3,2,1,0:T(8,128)(2,1)S(1)} %get-tuple-element.146), channel_id=1, source_target_pairs={{0,4},{4,8},{8,12},{12,0},{1,5},{5,9},{9,13},{13,1},{2,6},{6,10},{... | collective-permute-start | bytes 221192 | tf_op jit(solution)/shard_map/ppermute | solution.py:22
  255.2 3.2 %collective-permute-done.41.refs_3_ = bf16[1,1,1,24,1536]{4,3,2,1,0:T(8,128)(2,1)S(1)} collective-permute-done((bf16[1,1,1,24,1536]{4,3,2,1,0:T(8,128)(2,1)S(1)}, bf16[1,1,1,24,1536]{4,3,2,1,0:T(8,128)(2,1)S(1)}, u32[]{:S(2)}, u32[]{:S(2)}) %collective-permute-start.41) | collective-permute-done | bytes 73760 | tf_op jit(solution)/shard_map/ppermute | solution.py:22
  (293 shorter events, 71.3 us)
Async XLA Ops:
  7.2 93.8 %all-gather.2.cloned.1.call-start = ((), (), s32[]{:S(2)}) async-start(), calls=%async_computation.1 | async-start | bytes 3981312 | tf_op jit(solution)/shard_map/all_gather | solution.py:768
  9.1 1.5 collective-permute-start.15
  10.7 7.1 %collective-permute-start.16 = (bf16[2,1,24,1536]{3,2,1,0:T(8,128)(2,1)S(1)}, bf16[2,1,24,1536]{3,2,1,0:T(8,128)(2,1)S(1)}, u32[]{:S(2)}, u32[]{:S(2)}) collective-permute-start(bf16[2,1,24,1536]{3,2,1,0:T(8,128)(2,1)S(1)} %get-tuple-element.164), channel_id=1, source_target_pairs={{0,2},{2,0},{1,3},{3,1},{4,6},{6,4},{5,7},{7,5},{8,10},{10,8},{9,1... | collective-permute-start | bytes 442376 | tf_op jit(solution)/shard_map/ppermute | solution.py:22
  18.8 221.8 %reduce-scatter.2.cloned.1.call-start = ((), (), s32[]{:S(2)}) async-start(), calls=%async_computation.2 | async-start | bytes 2654208 | tf_op jit(solution)/shard_map/reduce_scatter | solution.py:792
  19.3 6.4 %collective-permute-start = (bf16[1,24,704]{2,1,0:T(8,128)(2,1)S(1)}, bf16[1,24,704]{2,1,0:T(8,128)(2,1)S(1)}, u32[]{:S(2)}, u32[]{:S(2)}) collective-permute-start(bf16[1,24,704]{2,1,0:T(8,128)(2,1)S(1)} %get-tuple-element.174), channel_id=1, source_target_pairs={{0,4},{4,8},{8,12},{12,0},{1,5},{5,9},{9,13},{13,1},{2,6},{6,10},{... | collective-permute-start | bytes 101384 | tf_op jit(solution)/shard_map/ppermute | solution.py:22
  21.1 5.1 %collective-permute-start.1 = (bf16[1,24,704]{2,1,0:T(8,128)(2,1)S(1)}, bf16[1,24,704]{2,1,0:T(8,128)(2,1)S(1)}, u32[]{:S(2)}, u32[]{:S(2)}) collective-permute-start(bf16[1,24,704]{2,1,0:T(8,128)(2,1)S(1)} %get-tuple-element.173), channel_id=1, source_target_pairs={{0,8},{4,12},{8,0},{12,4},{1,9},{5,13},{9,1},{13,5},{2,10},{6,14},... | collective-permute-start | bytes 101384 | tf_op jit(solution)/shard_map/ppermute | solution.py:22
  23.7 4.0 %collective-permute-start.2 = (bf16[1,24,704]{2,1,0:T(8,128)(2,1)S(1)}, bf16[1,24,704]{2,1,0:T(8,128)(2,1)S(1)}, u32[]{:S(2)}, u32[]{:S(2)}) collective-permute-start(bf16[1,24,704]{2,1,0:T(8,128)(2,1)S(1)} %get-tuple-element.172), channel_id=1, source_target_pairs={{0,12},{4,0},{8,4},{12,8},{1,13},{5,1},{9,5},{13,9},{2,14},{6,2},{... | collective-permute-start | bytes 101384 | tf_op jit(solution)/shard_map/ppermute | solution.py:22
  27.7 5.2 %collective-permute-start.3 = (bf16[1,4,1,24,704]{4,3,2,1,0:T(8,128)(2,1)S(1)}, bf16[1,4,1,24,704]{4,3,2,1,0:T(8,128)(2,1)S(1)}, u32[]{:S(2)}, u32[]{:S(2)}) collective-permute-start(bf16[1,4,1,24,704]{4,3,2,1,0:T(8,128)(2,1)S(1)} %bitcast.68), channel_id=1, source_target_pairs={{0,2},{2,0},{1,3},{3,1},{4,6},{6,4},{5,7},{7,5},{8,10},{10,8},{9,1... | collective-permute-start | bytes 405512 | tf_op jit(solution)/shard_map/ppermute | solution.py:22
  33.0 9.3 %collective-permute-start.4 = (bf16[1,4,2,24,704]{4,3,2,1,0:T(8,128)(2,1)S(1)}, bf16[1,4,2,24,704]{4,3,2,1,0:T(8,128)(2,1)S(1)}, u32[]{:S(2)}, u32[]{:S(2)}) collective-permute-start(bf16[1,4,2,24,704]{4,3,2,1,0:T(8,128)(2,1)S(1)} %arrange.9.refs_0_), channel_id=1, source_target_pairs={{0,16},{16,0},{1,17},{17,1},{2,18},{18,2},{3,19},{19,3},{4,20},{20... | collective-permute-start | bytes 811016 | tf_op jit(solution)/shard_map/ppermute | solution.py:22
  42.3 5.1 %collective-permute-start.5 = (bf16[2,4,2,1,24,704]{5,4,3,2,1,0:T(8,128)(2,1)S(1)}, bf16[2,4,2,1,24,704]{5,4,3,2,1,0:T(8,128)(2,1)S(1)}, u32[]{:S(2)}, u32[]{:S(2)}) collective-permute-start(bf16[2,4,2,1,24,704]{5,4,3,2,1,0:T(8,128)(2,1)S(1)} %bitcast.54), channel_id=1, source_target_pairs={{0,1},{1,0},{2,3},{3,2},{4,5},{5,4},{6,7},{7,6},{8,9},{9,8},{10,11... | collective-permute-start | bytes 1622024 | tf_op jit(solution)/shard_map/ppermute | solution.py:22
  42.4 10.9 %collective-permute-start.6 = (bf16[128,768]{1,0:T(8,128)(2,1)S(1)}, bf16[128,768]{1,0:T(8,128)(2,1)S(1)}, u32[]{:S(2)}, u32[]{:S(2)}) collective-permute-start(bf16[128,768]{1,0:T(8,128)(2,1)S(1)} %bitcast.56), channel_id=1, source_target_pairs={{0,4},{4,8},{8,12},{12,0},{1,5},{5,9},{9,13},{13,1},{2,6},{6,10},{... | collective-permute-start | bytes 589832 | tf_op jit(solution)/shard_map/ppermute | solution.py:22
  43.9 17.7 %collective-permute-start.7 = (bf16[128,768]{1,0:T(8,128)(2,1)S(1)}, bf16[128,768]{1,0:T(8,128)(2,1)S(1)}, u32[]{:S(2)}, u32[]{:S(2)}) collective-permute-start(bf16[128,768]{1,0:T(8,128)(2,1)S(1)} %bitcast.57), channel_id=1, source_target_pairs={{0,8},{4,12},{8,0},{12,4},{1,9},{5,13},{9,1},{13,5},{2,10},{6,14},... | collective-permute-start | bytes 589832 | tf_op jit(solution)/shard_map/ppermute | solution.py:22
  46.3 15.3 %collective-permute-start.8 = (bf16[128,768]{1,0:T(8,128)(2,1)S(1)}, bf16[128,768]{1,0:T(8,128)(2,1)S(1)}, u32[]{:S(2)}, u32[]{:S(2)}) collective-permute-start(bf16[128,768]{1,0:T(8,128)(2,1)S(1)} %bitcast.58), channel_id=1, source_target_pairs={{0,12},{4,0},{8,4},{12,8},{1,13},{5,1},{9,5},{13,9},{2,14},{6,2},{... | collective-permute-start | bytes 589832 | tf_op jit(solution)/shard_map/ppermute | solution.py:22
  64.7 11.0 %collective-permute-start.9 = (bf16[512,384]{1,0:T(8,128)(2,1)S(1)}, bf16[512,384]{1,0:T(8,128)(2,1)S(1)}, u32[]{:S(2)}, u32[]{:S(2)}) collective-permute-start(bf16[512,384]{1,0:T(8,128)(2,1)S(1)} %get-tuple-element.86.refs_3_.refs_9_), channel_id=1, source_target_pairs={{0,2},{2,0},{1,3},{3,1},{4,6},{6,4},{5,7},{7,5},{8,10},{10,8},{9,1... | collective-permute-start | bytes 1179656 | tf_op jit(solution)/shard_map/ppermute | solution.py:22
  66.2 10.5 %collective-permute-start.10 = (bf16[512,384]{1,0:T(8,128)(2,1)S(1)}, bf16[512,384]{1,0:T(8,128)(2,1)S(1)}, u32[]{:S(2)}, u32[]{:S(2)}) collective-permute-start(bf16[512,384]{1,0:T(8,128)(2,1)S(1)} %get-tuple-element.86.refs_3_.refs_9_), channel_id=1, source_target_pairs={{0,1},{1,0},{2,3},{3,2},{4,5},{5,4},{6,7},{7,6},{8,9},{9,8},{10,11... | collective-permute-start | bytes 1179656 | tf_op jit(solution)/shard_map/ppermute | solution.py:22
  75.7 1.7 collective-permute-start.11
  84.1 10.8 %collective-permute-start.12 = (bf16[128,192]{1,0:T(8,128)(2,1)S(1)}, bf16[128,192]{1,0:T(8,128)(2,1)S(1)}, u32[]{:S(2)}, u32[]{:S(2)}) collective-permute-start(bf16[128,192]{1,0:T(8,128)(2,1)S(1)} %get-tuple-element.88), channel_id=1, source_target_pairs={{0,4},{4,8},{8,12},{12,0},{1,5},{5,9},{9,13},{13,1},{2,6},{6,10},{... | collective-permute-start | bytes 147464 | tf_op jit(solution)/shard_map/ppermute | solution.py:22
  92.5 7.2 %collective-permute-start.13 = (bf16[128,192]{1,0:T(8,128)(2,1)S(1)}, bf16[128,192]{1,0:T(8,128)(2,1)S(1)}, u32[]{:S(2)}, u32[]{:S(2)}) collective-permute-start(bf16[128,192]{1,0:T(8,128)(2,1)S(1)} %get-tuple-element.89), channel_id=1, source_target_pairs={{0,8},{4,12},{8,0},{12,4},{1,9},{5,13},{9,1},{13,5},{2,10},{6,14},... | collective-permute-start | bytes 147464 | tf_op jit(solution)/shard_map/ppermute | solution.py:22
  92.5 7.9 %collective-permute-start.14 = (bf16[128,192]{1,0:T(8,128)(2,1)S(1)}, bf16[128,192]{1,0:T(8,128)(2,1)S(1)}, u32[]{:S(2)}, u32[]{:S(2)}) collective-permute-start(bf16[128,192]{1,0:T(8,128)(2,1)S(1)} %get-tuple-element.90), channel_id=1, source_target_pairs={{0,12},{4,0},{8,4},{12,8},{1,13},{5,1},{9,5},{13,9},{2,14},{6,2},{... | collective-permute-start | bytes 147464 | tf_op jit(solution)/shard_map/ppermute | solution.py:22
  109.5 6.6 %collective-permute-start.17 = (bf16[128,768]{1,0:T(8,128)(2,1)S(1)}, bf16[128,768]{1,0:T(8,128)(2,1)S(1)}, u32[]{:S(2)}, u32[]{:S(2)}) collective-permute-start(bf16[128,768]{1,0:T(8,128)(2,1)S(1)} %get-tuple-element.91.refs_0_), channel_id=1, source_target_pairs={{0,2},{2,0},{1,3},{3,1},{4,6},{6,4},{5,7},{7,5},{8,10},{10,8},{9,1... | collective-permute-start | bytes 589832 | tf_op jit(solution)/shard_map/ppermute | solution.py:22
  111.0 5.1 %collective-permute-start.18 = (bf16[128,768]{1,0:T(8,128)(2,1)S(1)}, bf16[128,768]{1,0:T(8,128)(2,1)S(1)}, u32[]{:S(2)}, u32[]{:S(2)}) collective-permute-start(bf16[128,768]{1,0:T(8,128)(2,1)S(1)} %get-tuple-element.91.refs_0_), channel_id=1, source_target_pairs={{0,1},{1,0},{2,3},{3,2},{4,5},{5,4},{6,7},{7,6},{8,9},{9,8},{10,11... | collective-permute-start | bytes 589832 | tf_op jit(solution)/shard_map/ppermute | solution.py:22
  116.1 1.4 collective-permute-start.19
  122.7 1.7 collective-permute-start.20
  125.9 7.3 %collective-permute-start.21 = (bf16[128,768]{1,0:T(8,128)(2,1)}, bf16[128,768]{1,0:T(8,128)(2,1)}, u32[]{:S(2)}, u32[]{:S(2)}) collective-permute-start(bf16[128,768]{1,0:T(8,128)(2,1)} %get-tuple-element.95), channel_id=1, source_target_pairs={{0,2},{2,0},{1,3},{3,1},{4,6},{6,4},{5,7},{7,5},{8,10},{10,8},{9,1... | collective-permute-start | bytes 589832 | tf_op jit(solution)/shard_map/ppermute | solution.py:22
  139.6 6.1 %collective-permute-start.22 = (bf16[128,768]{1,0:T(8,128)(2,1)S(1)}, bf16[128,768]{1,0:T(8,128)(2,1)S(1)}, u32[]{:S(2)}, u32[]{:S(2)}) collective-permute-start(bf16[128,768]{1,0:T(8,128)(2,1)S(1)} %get-tuple-element.99.refs_0_), channel_id=1, source_target_pairs={{0,2},{2,0},{1,3},{3,1},{4,6},{6,4},{5,7},{7,5},{8,10},{10,8},{9,1... | collective-permute-start | bytes 589832 | tf_op jit(solution)/shard_map/ppermute | solution.py:22
  141.1 4.7 %collective-permute-start.23 = (bf16[128,768]{1,0:T(8,128)(2,1)S(1)}, bf16[128,768]{1,0:T(8,128)(2,1)S(1)}, u32[]{:S(2)}, u32[]{:S(2)}) collective-permute-start(bf16[128,768]{1,0:T(8,128)(2,1)S(1)} %get-tuple-element.99.refs_0_), channel_id=1, source_target_pairs={{0,1},{1,0},{2,3},{3,2},{4,5},{5,4},{6,7},{7,6},{8,9},{9,8},{10,11... | collective-permute-start | bytes 589832 | tf_op jit(solution)/shard_map/ppermute | solution.py:22
  145.7 1.4 collective-permute-start.24
  150.1 1.8 collective-permute-start.25
  155.6 7.2 %collective-permute-start.26 = (bf16[128,768]{1,0:T(8,128)(2,1)}, bf16[128,768]{1,0:T(8,128)(2,1)S(1)}, u32[]{:S(2)}, u32[]{:S(2)}) collective-permute-start(bf16[128,768]{1,0:T(8,128)(2,1)} %copy-done.72), channel_id=1, source_target_pairs={{0,2},{2,0},{1,3},{3,1},{4,6},{6,4},{5,7},{7,5},{8,10},{10,8},{9,1... | collective-permute-start | bytes 589832 | tf_op jit(solution)/shard_map/ppermute | solution.py:22
  170.3 8.3 %collective-permute-start.27 = (bf16[128,192]{1,0:T(8,128)(2,1)S(1)}, bf16[128,192]{1,0:T(8,128)(2,1)S(1)}, u32[]{:S(2)}, u32[]{:S(2)}) collective-permute-start(bf16[128,192]{1,0:T(8,128)(2,1)S(1)} %get-tuple-element.113), channel_id=1, source_target_pairs={{0,4},{4,8},{8,12},{12,0},{1,5},{5,9},{9,13},{13,1},{2,6},{6,10},{... | collective-permute-start | bytes 147464 | tf_op jit(solution)/shard_map/ppermute | solution.py:22
  171.6 11.0 %collective-permute-start.28 = (bf16[128,192]{1,0:T(8,128)(2,1)S(1)}, bf16[128,192]{1,0:T(8,128)(2,1)S(1)}, u32[]{:S(2)}, u32[]{:S(2)}) collective-permute-start(bf16[128,192]{1,0:T(8,128)(2,1)S(1)} %get-tuple-element.114), channel_id=1, source_target_pairs={{0,8},{4,12},{8,0},{12,4},{1,9},{5,13},{9,1},{13,5},{2,10},{6,14},... | collective-permute-start | bytes 147464 | tf_op jit(solution)/shard_map/ppermute | solution.py:22
  173.7 8.9 %collective-permute-start.29 = (bf16[128,192]{1,0:T(8,128)(2,1)S(1)}, bf16[128,192]{1,0:T(8,128)(2,1)S(1)}, u32[]{:S(2)}, u32[]{:S(2)}) collective-permute-start(bf16[128,192]{1,0:T(8,128)(2,1)S(1)} %get-tuple-element.115), channel_id=1, source_target_pairs={{0,12},{4,0},{8,4},{12,8},{1,13},{5,1},{9,5},{13,9},{2,14},{6,2},{... | collective-permute-start | bytes 147464 | tf_op jit(solution)/shard_map/ppermute | solution.py:22
  189.2 2.4 collective-permute-start.30
  192.4 11.4 %collective-permute-start.31 = (bf16[512,384]{1,0:T(8,128)(2,1)}, bf16[512,384]{1,0:T(8,128)(2,1)S(1)}, u32[]{:S(2)}, u32[]{:S(2)}) collective-permute-start(bf16[512,384]{1,0:T(8,128)(2,1)} %get-tuple-element.121), channel_id=1, source_target_pairs={{0,2},{2,0},{1,3},{3,1},{4,6},{6,4},{5,7},{7,5},{8,10},{10,8},{9,1... | collective-permute-start | bytes 1179656 | tf_op jit(solution)/shard_map/ppermute | solution.py:22
  207.5 2.9 %collective-permute-start.32 = (bf16[16,24,1536]{2,1,0:T(8,128)(2,1)S(1)}, bf16[16,24,1536]{2,1,0:T(8,128)(2,1)S(1)}, u32[]{:S(2)}, u32[]{:S(2)}) collective-permute-start(bf16[16,24,1536]{2,1,0:T(8,128)(2,1)S(1)} %get-tuple-element.130), channel_id=1, source_target_pairs={{0,1},{1,0},{2,3},{3,2},{4,5},{5,4},{6,7},{7,6},{8,9},{9,8},{10,11... | collective-permute-start | bytes 3538952 | tf_op jit(solution)/shard_map/ppermute | solution.py:22
  211.2 28.1 %copy-start.7 = (bf16[1,128,768]{2,1,0:T(8,128)(2,1)S(1)}, bf16[1,128,768]{2,1,0:T(8,128)(2,1)}, u32[]{:S(2)}) copy-start(bf16[1,128,768]{2,1,0:T(8,128)(2,1)} %param.18) | copy-start | bytes 589828
  211.3 9.1 %collective-permute-start.33 = (bf16[2,4,1,24,768]{4,3,2,1,0:T(8,128)(2,1)S(1)}, bf16[2,4,1,24,768]{4,3,2,1,0:T(8,128)(2,1)S(1)}, u32[]{:S(2)}, u32[]{:S(2)}) collective-permute-start(bf16[2,4,1,24,768]{4,3,2,1,0:T(8,128)(2,1)S(1)} %get-tuple-element.132), channel_id=1, source_target_pairs={{0,2},{2,0},{1,3},{3,1},{4,6},{6,4},{5,7},{7,5},{8,10},{10,8},{9,1... | collective-permute-start | bytes 884744 | tf_op jit(solution)/shard_map/ppermute | solution.py:22
  212.9 11.9 %collective-permute-start.34 = (bf16[1,4,2,24,768]{4,3,2,1,0:T(8,128)(2,1)S(1)}, bf16[1,4,2,24,768]{4,3,2,1,0:T(8,128)(2,1)S(1)}, u32[]{:S(2)}, u32[]{:S(2)}) collective-permute-start(bf16[1,4,2,24,768]{4,3,2,1,0:T(8,128)(2,1)S(1)} %get-tuple-element.134), channel_id=1, source_target_pairs={{0,16},{16,0},{1,17},{17,1},{2,18},{18,2},{3,19},{19,3},{4,20},{20... | collective-permute-start | bytes 884744 | tf_op jit(solution)/shard_map/ppermute | solution.py:22
  213.0 13.5 %collective-permute-start.37 = (bf16[128,768]{1,0:T(8,128)(2,1)S(1)}, bf16[128,768]{1,0:T(8,128)(2,1)S(1)}, u32[]{:S(2)}, u32[]{:S(2)}) collective-permute-start(bf16[128,768]{1,0:T(8,128)(2,1)S(1)} %get-tuple-element.140), channel_id=1, source_target_pairs={{0,4},{4,8},{8,12},{12,0},{1,5},{5,9},{9,13},{13,1},{2,6},{6,10},{... | collective-permute-start | bytes 589832 | tf_op jit(solution)/shard_map/ppermute | solution.py:22
  216.9 22.5 %collective-permute-start.38 = (bf16[128,768]{1,0:T(8,128)(2,1)S(1)}, bf16[128,768]{1,0:T(8,128)(2,1)S(1)}, u32[]{:S(2)}, u32[]{:S(2)}) collective-permute-start(bf16[128,768]{1,0:T(8,128)(2,1)S(1)} %get-tuple-element.141), channel_id=1, source_target_pairs={{0,8},{4,12},{8,0},{12,4},{1,9},{5,13},{9,1},{13,5},{2,10},{6,14},... | collective-permute-start | bytes 589832 | tf_op jit(solution)/shard_map/ppermute | solution.py:22
  217.7 21.6 %collective-permute-start.39 = (bf16[128,768]{1,0:T(8,128)(2,1)S(1)}, bf16[128,768]{1,0:T(8,128)(2,1)S(1)}, u32[]{:S(2)}, u32[]{:S(2)}) collective-permute-start(bf16[128,768]{1,0:T(8,128)(2,1)S(1)} %get-tuple-element.142), channel_id=1, source_target_pairs={{0,12},{4,0},{8,4},{12,8},{1,13},{5,1},{9,5},{13,9},{2,14},{6,2},{... | collective-permute-start | bytes 589832 | tf_op jit(solution)/shard_map/ppermute | solution.py:22
  225.5 15.0 %collective-permute-start.35 = (bf16[1,4,1,24,768]{4,3,2,1,0:T(8,128)(2,1)S(1)}, bf16[1,4,1,24,768]{4,3,2,1,0:T(8,128)(2,1)S(1)}, u32[]{:S(2)}, u32[]{:S(2)}) collective-permute-start(bf16[1,4,1,24,768]{4,3,2,1,0:T(8,128)(2,1)S(1)} %get-tuple-element.136), channel_id=1, source_target_pairs={{0,16},{16,0},{1,17},{17,1},{2,18},{18,2},{3,19},{19,3},{4,20},{20... | collective-permute-start | bytes 442376 | tf_op jit(solution)/shard_map/ppermute | solution.py:22
  225.9 14.6 %collective-permute-start.36 = (bf16[1,4,1,24,768]{4,3,2,1,0:T(8,128)(2,1)S(1)}, bf16[1,4,1,24,768]{4,3,2,1,0:T(8,128)(2,1)S(1)}, u32[]{:S(2)}, u32[]{:S(2)}) collective-permute-start(bf16[1,4,1,24,768]{4,3,2,1,0:T(8,128)(2,1)S(1)} %get-tuple-element.138), channel_id=1, source_target_pairs={{0,2},{2,0},{1,3},{3,1},{4,6},{6,4},{5,7},{7,5},{8,10},{10,8},{9,1... | collective-permute-start | bytes 442376 | tf_op jit(solution)/shard_map/ppermute | solution.py:22
  242.4 4.4 %collective-permute-start.43 = (bf16[1,1,1,2,24,768]{5,4,3,2,1,0:T(8,128)(2,1)S(1)}, bf16[1,1,1,2,24,768]{5,4,3,2,1,0:T(8,128)(2,1)S(1)}, u32[]{:S(2)}, u32[]{:S(2)}) collective-permute-start(bf16[1,1,1,2,24,768]{5,4,3,2,1,0:T(8,128)(2,1)S(1)} %get-tuple-element.170), channel_id=1, source_target_pairs={{0,2},{2,0},{1,3},{3,1},{4,6},{6,4},{5,7},{7,5},{8,10},{10,8},{9,1... | collective-permute-start | bytes 221192 | tf_op jit(solution)/shard_map/ppermute | solution.py:22
  246.8 7.2 %collective-permute-start.44 = (bf16[1,1,2,1,24,768]{5,4,3,2,1,0:T(8,128)(2,1)S(1)}, bf16[1,1,2,1,24,768]{5,4,3,2,1,0:T(8,128)(2,1)S(1)}, u32[]{:S(2)}, u32[]{:S(2)}) collective-permute-start(bf16[1,1,2,1,24,768]{5,4,3,2,1,0:T(8,128)(2,1)S(1)} %get-tuple-element.168), channel_id=1, source_target_pairs={{0,1},{1,0},{2,3},{3,2},{4,5},{5,4},{6,7},{7,6},{8,9},{9,8},{10,11... | collective-permute-start | bytes 221192 | tf_op jit(solution)/shard_map/ppermute | solution.py:22
  246.9 8.3 %collective-permute-start.40 = (bf16[1,1,1,24,1536]{4,3,2,1,0:T(8,128)(2,1)S(1)}, bf16[1,1,1,24,1536]{4,3,2,1,0:T(8,128)(2,1)S(1)}, u32[]{:S(2)}, u32[]{:S(2)}) collective-permute-start(bf16[1,1,1,24,1536]{4,3,2,1,0:T(8,128)(2,1)S(1)} %get-tuple-element.146), channel_id=1, source_target_pairs={{0,4},{4,8},{8,12},{12,0},{1,5},{5,9},{9,13},{13,1},{2,6},{6,10},{... | collective-permute-start | bytes 221192 | tf_op jit(solution)/shard_map/ppermute | solution.py:22
  251.6 6.8 %collective-permute-start.41 = (bf16[1,1,1,24,1536]{4,3,2,1,0:T(8,128)(2,1)S(1)}, bf16[1,1,1,24,1536]{4,3,2,1,0:T(8,128)(2,1)S(1)}, u32[]{:S(2)}, u32[]{:S(2)}) collective-permute-start(bf16[1,1,1,24,1536]{4,3,2,1,0:T(8,128)(2,1)S(1)} %get-tuple-element.147), channel_id=1, source_target_pairs={{0,8},{4,12},{8,0},{12,4},{1,9},{5,13},{9,1},{13,5},{2,10},{6,14},... | collective-permute-start | bytes 221192 | tf_op jit(solution)/shard_map/ppermute | solution.py:22
  252.8 5.8 %collective-permute-start.42 = (bf16[1,1,1,24,1536]{4,3,2,1,0:T(8,128)(2,1)S(1)}, bf16[1,1,1,24,1536]{4,3,2,1,0:T(8,128)(2,1)S(1)}, u32[]{:S(2)}, u32[]{:S(2)}) collective-permute-start(bf16[1,1,1,24,1536]{4,3,2,1,0:T(8,128)(2,1)S(1)} %get-tuple-element.148), channel_id=1, source_target_pairs={{0,12},{4,0},{8,4},{12,8},{1,13},{5,1},{9,5},{13,9},{2,14},{6,2},{... | collective-permute-start | bytes 221192 | tf_op jit(solution)/shard_map/ppermute | solution.py:22
  (84 other events, 503.5 us)
Sparse Core Ops, SparseCore 0:
  18.9 80.2 all-gather.1
  155.7 84.2 reduce-scatter.1

commit v2 on v1

--- a/solution.py
+++ b/solution.py
@@ -120,34 +120,56 @@
     return call(body, (w_qkv, flat, seg, mask), outs, "pack_one", scratch=[pltpu.VMEM((LANES, LANES), F32)])[0]
 
 
-def pack_up(w_up, w_out, ffd, sx):
+def pack_up(place, w_up, w_out, ffd, sx):
     rows, width = w_out.shape
+    half = width // 2
     blocks = w_up.shape[1] // (2 * sx * ffd)
     ff = blocks * ffd
 
-    def body(up_ref, out_ref, to_ref):
+    def body(at_ref, up_ref, out_ref, *refs):
+        outs, every = refs[:-1], refs[-1]
         for c in range(2):
             for x in range(sx):
                 for b in range(blocks):
                     at = ((b * sx + x) * 2 + c) * ffd
-                    to_ref[c, x, :, b * ffd:(b + 1) * ffd] = up_ref[:, at:at + ffd]
-                to_ref[c, x, :, ff:] = out_ref[...]
-
-    return call(body, (w_up, w_out), [((2, sx, rows, ff + width), BF)], "pack_up")[0]
+                    every[c * sx + x, :, b * ffd:(b + 1) * ffd] = up_ref[:, at:at + ffd]
+                every[c * sx + x, :, ff:] = out_ref[:, c * half:(c + 1) * half]
+        for dc in range(2):
+            core = at_ref[1] if dc == 0 else 1 - at_ref[1]
+            for dx in range(sx):
+                outs[dc * sx + dx][...] = every[core * sx + lax.rem(at_ref[0] + dx, sx)]
+
+    outs = [((rows, ff + half), BF)] * (2 * sx)
+    return call(body, (place, w_up, w_out), outs, "pack_up", 1, scratch=[pltpu.VMEM((2 * sx, rows, ff + half), BF)])
+
+
+def join_up(place, pieces, w_down):
+    sx = len(pieces) // 2
+    rows, cols = pieces[0].shape
+    joined = w_down.shape[0] == 2 * sx * rows
+    wide = cols + w_down.shape[1] if joined else cols
+
+    def body(at_ref, *refs):
+        out = refs[-1]
+        for dc in range(2):
+            core = at_ref[1] if dc == 0 else 1 - at_ref[1]
+            for dx in range(sx):
+                spot = lax.rem(at_ref[0] + sx - dx, sx) * 2 + core
+                out[pl.ds(spot, 1), :, 0:cols] = refs[dc * sx + dx][...].reshape(1, rows, cols)
+        if joined:
+            out[:, :, cols:] = refs[2 * sx][...]
+
+    args = (place, *pieces, w_down.reshape(2 * sx, rows, -1)) if joined else (place, *pieces)
+    return call(body, args, [((2 * sx, rows, wide), BF)], "join_up", 1)[0].reshape(2 * sx * rows, wide)
 
 
 def held(value, after):
-    def body(value_ref, *rest):
-        rest[-1][...] = value_ref[...]
-
-    return pl.pallas_call(
-        body,
-        in_specs=[pl.BlockSpec(memory_space=pltpu.VMEM)] + [pl.BlockSpec(memory_space=pl.ANY)] * len(after),
-        out_shape=jax.ShapeDtypeStruct(value.shape, value.dtype),
-        compiler_params=params(),
-        cost_estimate=SMALL,
-        name="held",
-    )(value, *after)
+    def body(value_ref, out_ref):
+        out_ref[...] = value_ref[...]
+
+    array = value.value if isinstance(value, Part) else value
+    shape = (array.shape[0], value.last - value.first) if isinstance(value, Part) else array.shape
+    return call(body, (value,), [(shape, array.dtype)], "held", 0, after)[0]
 
 
 def arrange(pieces, place, dim, after=()):
@@ -238,8 +260,9 @@
 
 
 def attend_kernel(order, q_ref, seg_ref, *rest):
-    count = len(rest) - 10
-    kv_refs, low_refs, (ctx_ref, tot_ref), (keys, bias, acc, turned) = rest[:count], rest[count:count + 4], rest[count + 4:count + 6], rest[count + 6:]
+    count = len(rest) - 9
+    kv_refs, low_refs, both_ref, (keys, bias, acc, turned) = rest[:count], rest[count:count + 4], rest[count + 4], rest[count + 5:]
+    ctx_ref, tot_ref = both_ref.at[0], both_ref.at[1]
     total = q_ref.shape[0]
     rows = total // ZS
     span = count * rows
@@ -278,12 +301,13 @@
 def attend(order, q, seg, kvs, after=()):
     total = q.shape[0]
     span = len(kvs) * total // ZS
-    outs = [((total // ZS, 3 * HEAD_DIM), BF)] * ZS + [((total, 2 * LANES), F32)] * 2
+    outs = [((total // ZS, 3 * HEAD_DIM), BF)] * ZS + [((2, total, 2 * LANES), F32)]
     scratch = [pltpu.VMEM((ZS * span, 3 * LANES), BF), pltpu.VMEM((span, total), F32), pltpu.VMEM((3, LANES, total), F32), pltpu.VMEM((LANES, LANES), F32)]
     return call(attend_kernel, (order, q, seg, *kvs), outs, "attend", 1, after, scratch, 20)
 
 
-def attend_back_kernel(order, q_ref, gc0, gc1, gc2, gc3, ctx_ref, tot_ref, seg_ref, *rest):
+def attend_back_kernel(order, q_ref, gc0, gc1, gc2, gc3, both_ref, seg_ref, *rest):
+    ctx_ref, tot_ref = both_ref.at[0], both_ref.at[1]
     count = len(rest) - 9
     kv_refs, (dq_ref, kept_ref, sent_ref), (keys, bias, ge, acc, gctx_ref, turned) = rest[:count], rest[count:count + 3], rest[count + 3:]
     total = q_ref.shape[0]
@@ -344,7 +368,7 @@
     dq_ref[:, LANES:] = (0.125 * acc[2]).T[:, 0:HEAD_DIM].astype(BF)
 
 
-def attend_back(order, q, gctx, ctx, tot, seg, kvs, after=()):
+def attend_back(order, q, gctx, both, seg, kvs, after=()):
     total = q.shape[0]
     count = len(kvs)
     span = count * total // ZS
@@ -357,7 +381,7 @@
         pltpu.VMEM((total, 3 * HEAD_DIM), F32),
         pltpu.VMEM((LANES, LANES), F32),
     ]
-    return call(attend_back_kernel, (order, q, *gctx, ctx, tot, seg, *kvs), outs, "attend_back", 1, after, scratch, 24)
+    return call(attend_back_kernel, (order, q, *gctx, both, seg, *kvs), outs, "attend_back", 1, after, scratch, 24)
 
 
 def norm_parts(values):
@@ -464,31 +488,46 @@
     return [shift(pieces[d], axis, d) for d in range(1, len(pieces))]
 
 
-def out_project(place, pieces, mid, ff, hidden, vectors, after):
+def beside(pieces):
     rows, group = pieces[0].shape
-    width = hidden.shape[1]
-
-    def body(place_ref, p0, p1, p2, p3, w_ref, hidden_ref, vec_ref, res_ref, n2_ref, cat_ref):
-        total = hidden_ref[...].astype(F32) + vec_ref[2:3, :]
-        for d, piece in enumerate((p0, p1, p2, p3)):
+
+    def body(*refs):
+        for d, ref in enumerate(refs[:-1]):
+            refs[-1][:, d * group:(d + 1) * group] = ref[...]
+
+    return call(body, tuple(pieces), [((rows, len(pieces) * group), BF)], "beside")[0]
+
+
+def out_project(place, cat, halves, hidden, vectors):
+    rows, width = hidden.shape
+    group = width // ZS
+    half = width // 2
+
+    def body(place_ref, cat_ref, own_ref, other_ref, hidden_ref, vec_ref, res_ref, n2_ref):
+        own = jnp.zeros((rows, half), F32)
+        other = jnp.zeros((rows, half), F32)
+        for d in range(ZS):
+            piece = cat_ref[:, d * group:(d + 1) * group]
             spot = pl.ds(pl.multiple_of(lax.rem(place_ref[0] + ZS - d, ZS) * group, group), group)
-            total = total + dot(piece[...], w_ref[spot, :])
-            cat_ref[:, d * group:(d + 1) * group] = piece[...]
+            own = own + dot(piece, own_ref[spot, :])
+            other = other + dot(piece, other_ref[spot, :])
+        first = place_ref[1] == 0
+        branch = jnp.concatenate([jnp.where(first, own, other), jnp.where(first, other, own)], 1)
+        total = hidden_ref[...].astype(F32) + branch + vec_ref[2:3, :]
         res_ref[:, 0:width] = total
         res_ref[:, width:] = jnp.broadcast_to(vec_ref[15:16, 0:rows], (LANES, rows)).T
         n2, _ = norm_parts(total)
         n2_ref[...] = (n2 * vec_ref[6:7, :] + vec_ref[7:8, :]).astype(BF)
 
-    outs = [((rows, width + LANES), F32), ((rows, width), BF), ((rows, width), BF)]
-    args = (place, *pieces, Part(mid, ff, ff + width), hidden, vectors)
-    return call(body, args, outs, "out_project", 1, after)
+    outs = [((rows, width + LANES), F32), ((rows, width), BF)]
+    return call(body, (place, cat, *halves, hidden, vectors), outs, "out_project", 1)
 
 
 def mlp_parts(weights, ff):
     width = weights[0].shape[0]
     if len(weights) == 2:
         return Part(weights[0], 0, ff), weights[1]
-    return Part(weights[0], 0, ff), Part(weights[0], ff + width, ff + 2 * width)
+    return Part(weights[0], 0, ff), Part(weights[0], ff + width // 2, ff + width // 2 + width)
 
 
 def mlp_up(blocks, weights, bias, ff):
@@ -497,23 +536,23 @@
     half = count // 2
 
     def body(*refs):
-        n2_refs, (bias_ref, up_ref, down_ref), (kept_ref, sent_ref, act_ref, slope_ref, n2_all) = refs[:count], refs[count:count + 3], refs[-5:]
+        n2_refs, (bias_ref, up_ref, down_ref), (kept_ref, sent_ref, slope_ref, saved_ref) = refs[:count], refs[count:count + 3], refs[-4:]
         for j in range(count):
-            n2_all[j * rows:(j + 1) * rows, :] = n2_refs[j][...]
+            saved_ref[j * rows:(j + 1) * rows, ff:] = n2_refs[j][...]
             pre = dot(n2_refs[j][...], up_ref[...]) + bias_ref[0:1, 0:ff]
             square = pre * pre
             tanh = jnp.tanh(GC * pre * (1.0 + 0.044715 * square))
             half_one = 0.5 * (1.0 + tanh)
             act = (pre * half_one).astype(BF)
             slope_ref[j] = (half_one + 0.5 * pre * (1.0 - tanh * tanh) * (GC + GC * 0.134145 * square)).astype(BF)
-            act_ref[j * rows:(j + 1) * rows, :] = act
+            saved_ref[j * rows:(j + 1) * rows, 0:ff] = act
             part = dot(act, down_ref[...])
             if j < half:
                 kept_ref[j] = part + bias_ref[1:2, 0:width] if j == 0 else part
             else:
                 sent_ref[j - half] = part.astype(BF)
 
-    outs = [((half, rows, width), F32), ((half, rows, width), BF), ((count * rows, ff), BF), ((count, rows, ff), BF), ((count * rows, width), BF)]
+    outs = [((half, rows, width), F32), ((half, rows, width), BF), ((count, rows, ff), BF), ((count * rows, ff + width), BF)]
     return call(body, (*blocks, bias, *mlp_parts(weights, ff)), outs, "mlp_up")
 
 
@@ -563,28 +602,28 @@
     return call(body, (*grads, slope, *mlp_parts(weights, ff)), outs, "mlp_back")
 
 
-def mlp_weights(grads, act, n2, gpre, after):
+def mlp_weights(grads, saved, gpre, after):
     width = grads.shape[1]
-    ff = act.shape[1]
-
-    def body(g_ref, act_ref, n2_ref, gpre_ref, *outs):
+    ff = gpre.shape[1]
+
+    def body(g_ref, saved_ref, gpre_ref, *outs):
         down_ref, up_ref = (outs[0].at[:, 0:width], outs[0].at[:, width:]) if ff == width else outs[:2]
-        down_ref[...] = dot_tn(act_ref[...], g_ref[...]).astype(BF)
-        up_ref[...] = dot_tn(n2_ref[...], gpre_ref[...]).astype(BF)
+        down_ref[...] = dot_tn(saved_ref[:, 0:ff], g_ref[...]).astype(BF)
+        up_ref[...] = dot_tn(saved_ref[:, ff:], gpre_ref[...]).astype(BF)
         outs[-1][...] = jnp.sum(gpre_ref[...].astype(F32), 0, keepdims=True)
 
     outs = [((width, 2 * width), BF)] if ff == width else [((ff, width), BF), ((width, ff), BF)]
-    *grads, sums = call(body, (grads, act, n2, gpre), outs + [((1, ff), F32)], "mlp_weights", after=after)
+    *grads, sums = call(body, (grads, saved, gpre), outs + [((1, ff), F32)], "mlp_weights", after=after)
     return grads, sums
 
 
-def out_back(place, terms, res_and_grad, vectors, ctx_cat, mid, ff, after):
+def out_back(place, terms, res_and_grad, vectors, ctx_cat, halves, after):
     rows, width = res_and_grad.shape[1:]
     group = width // ZS
     size = len(terms)
 
     def body(place_ref, *refs):
-        (both_ref, vec_ref, cat_ref, w_ref, gres_ref), gctx_refs, (gw_ref, sums_ref) = refs[size:size + 5], refs[size + 5:size + 9], refs[size + 9:]
+        (both_ref, vec_ref, cat_ref, own_ref, other_ref, gres_ref), gctx_refs, (gw_ref, sums_ref) = refs[size:size + 6], refs[size + 6:size + 10], refs[size + 10:]
         gn2 = refs[0][...]
         for ref in refs[1:size]:
             gn2 = gn2 + ref[...].astype(F32)
@@ -592,9 +631,12 @@
         gres = both_ref[1] + norm_back(n2, rstd, gn2, vec_ref[6:7, :])
         gres_ref[...] = gres
         branch = gres.astype(BF)
+        left, right = branch[:, 0:width // 2], branch[:, width // 2:]
+        first = place_ref[1] == 0
+        own, other = jnp.where(first, left, right), jnp.where(first, right, left)
         for d in range(ZS):
             spot = pl.ds(pl.multiple_of(lax.rem(place_ref[0] + d, ZS) * group, group), group)
-            gctx_refs[d][...] = dot_nt(branch, w_ref[spot, :]).astype(BF)
+            gctx_refs[d][...] = (dot_nt(own, own_ref[spot, :]) + dot_nt(other, other_ref[spot, :])).astype(BF)
         for d in range(ZS):
             spot = pl.ds(pl.multiple_of(lax.rem(place_ref[0] + ZS - d, ZS) * group, group), group)
             gw_ref[spot, :] = dot_tn(cat_ref[:, d * group:(d + 1) * group], branch).astype(BF)
@@ -604,7 +646,7 @@
         sums_ref[2:3, :] = rowsum(gn2)
 
     outs = [((rows, width), F32)] + [((rows, group), BF)] * ZS + [((width, width), BF), ((3, width), F32)]
-    args = (place, *terms, res_and_grad, vectors, ctx_cat, Part(mid, ff, ff + width))
+    args = (place, *terms, res_and_grad, vectors, ctx_cat, *halves)
     return call(body, args, outs, "out_back", 1, after)
 
 
@@ -689,13 +731,12 @@
 def input_back(terms, hidden, vectors, grad_res):
     rows, width = hidden.shape
 
-    def body(t0, t1, t2, t3, hidden_ref, gain_ref, gres_ref, out_ref, done_ref):
+    def body(t0, t1, t2, t3, hidden_ref, gain_ref, gres_ref, out_ref):
         back = t0[...] + t1[...].astype(F32) + t2[...].astype(F32) + t3[...].astype(F32)
         normed, rstd = norm_parts(hidden_ref[...].astype(F32))
         out_ref[...] = gres_ref[...] + norm_back(normed, rstd, back, gain_ref[4:5, :])
-        done_ref[...] = jnp.zeros_like(done_ref)
-
-    return call(body, (terms[0], *terms[1:], hidden, vectors, grad_res), [((rows, width), F32), ((8, LANES), F32)], "input_back")
+
+    return call(body, (terms[0], *terms[1:], hidden, vectors, grad_res), [((rows, width), F32)], "input_back")[0]
 
 
 def unpack_one(place, pieces, after):
@@ -739,6 +780,7 @@
     wcols = 9 * HEAD_DIM
     group = width // sz
     place = iz.astype(jnp.int32).reshape(1)
+    at_zc = jnp.stack([iz, core]).astype(jnp.int32)
 
     def from_z(value):
         return [value] + [shift(value, "z", d) for d in range(1, sz)]
@@ -754,17 +796,19 @@
     pieces = from_z(hidden)
     targets = jnp.concatenate([teacher, cotangent], 0)
     one = arrange(to_z(cut_z(pack_one(w_qkv, flat, segment_ids, padding_mask))), iz, 0)
-    one = gather(one[None, :, None], "x", 2)
-    one = gather(one, "y", 0)[:, :, :, None]
+    one = gather(one[None, :, None], "x", 2, after=[pieces[1]])
+    one = gather(one, "y", 0, after=pieces[2:])[:, :, :, None]
     one = gather(one, "core", 3).reshape(width, -1)
 
-    up = pack_up(w_up, w_out, ffd, sx)
-    up = arrange([lax.dynamic_slice_in_dim(up, core, 1, 0), shift(lax.dynamic_slice_in_dim(up, 1 - core, 1, 0), "core", 1)], core, 0)
-    up_x = [lax.dynamic_slice_in_dim(up, lax.rem(ix + d, sx), 1, 1) for d in range(sx)]
-    up = arrange([up_x[0]] + [shift(up_x[d], "x", d) for d in range(1, sx)], ix, 1)
-    weights = [up.transpose(1, 0, 2, 3).reshape(2 * sx * wr, ff + width), w_down]
-    if ff == width:
-        weights = [jnp.concatenate(weights, 1)]
+    at_xc = jnp.stack([ix, core]).astype(jnp.int32)
+    ups = list(pack_up(at_xc, w_up, w_out, ffd, sx))
+    for d in range(1, 2 * sx):
+        dc, dx = d // sx, d % sx
+        pairs = [(x * 2 + c, (x + dx) % sx * 2 + (c + dc) % 2) for x in range(sx) for c in range(2)]
+        ups[d] = lax.ppermute(ups[d], ("x", "core"), pairs)
+    weights = [join_up(at_xc, ups, w_down)]
+    if ffd != 2 * sx * wr:
+        weights = weights + [w_down]
     weights = [lax.all_gather(member, ("y", "z"), axis=0, tiled=True) for member in weights]
 
     vec = one[:, wcols:]
@@ -781,19 +825,23 @@
 
     n1_low, q, kv, hidden_all = project(place, pieces, one, vectors)
     kvs = spread_tokens(kv)
-    *ctx_parts, ctx, tot = attend(order, q, seg, kvs)
-    residual, n2_low, ctx_cat = out_project(place, to_z(ctx_parts), weights[0], ff, hidden, vectors, after=[biases])
-    kept, sent, act, slope, n2_all = mlp_up(spread_tokens(n2_low), weights, biases, ff)
+    *ctx_parts, ctx_tot = attend(order, q, seg, kvs, after=[biases])
+    ctx_cat = beside(to_z(ctx_parts))
+    wo = [held(Part(weights[0], ff, ff + width // 2), [ctx_cat])]
+    wo = wo + [shift(wo[0], "core", 1)]
+    residual, n2_low = out_project(at_zc, ctx_cat, wo, hidden, vectors)
+    kept, sent, slope, saved = mlp_up(spread_tokens(n2_low), weights, biases, ff)
     layer_out, fin_sums, res_and_grad, grad_mlp = finish(fold_tokens(kept, sent), residual, targets, (2.0 / (count * width)).reshape(1))
 
     kept, sent, grad_pre, grads = mlp_back(spread_tokens(grad_mlp), weights, slope)
     gn2_terms = fold_tokens(kept, sent)
-    gw_mlp, up_sums = mlp_weights(grads, act, n2_all, grad_pre, after=gn2_terms[:1])
+    gw_mlp, up_sums = mlp_weights(grads, saved, grad_pre, after=gn2_terms[:1])
     gw_sums = [lax.psum_scatter(member, ("y", "z"), scatter_dimension=0, tiled=True) for member in gw_mlp]
-    grad_res, *gctx, gw_out, out_sums = out_back(place, gn2_terms, res_and_grad, vectors, ctx_cat, weights[0], ff, after=[up_sums])
-    dq, dkv_kept, dkv_sent = attend_back(order, q, to_z(gctx), ctx, tot, seg, kvs)
+    grad_res, *gctx, gw_out, out_sums = out_back(at_zc, gn2_terms, res_and_grad, vectors, ctx_cat, wo, after=[up_sums])
+    dq, dkv_kept, dkv_sent = attend_back(order, q, to_z(gctx), ctx_tot, seg, kvs)
     grad_joined, gn1, *gn1_parts = join_back(place, fold_tokens(dkv_kept, dkv_sent), dq, one)
-    input_grad, back_done = input_back(to_z(gn1_parts), hidden, vectors, grad_res)
+    gn1_parts = to_z(gn1_parts)
+    input_grad = input_back(gn1_parts, hidden, vectors, grad_res)
 
     up_rows = jnp.zeros((upc, sy * sz, sx * 2, wr), F32)
     up_rows = lax.dynamic_update_slice_in_dim(up_rows, up_sums.reshape(sy * sz, upc, wr).transpose(1, 0, 2)[:, :, None], ix * 2 + core, 2).reshape(upc, width)
@@ -801,7 +849,7 @@
     kept, sent = weights_back(places, n1_low, grad_joined, gn1, hidden_all, out_sums, fin_sums, up_rows, gw_out, wr, devices)
     third = fold_both(kept.reshape(sy, sz, sx, wr, -1), shift(sent, "core", 1).reshape(sy, sz, sx, wr, -1), ix, iy, width)
     third = fold_cross(third[:sx], passed(third[:sx], "x"), third[sx:], passed(third[sx:], "y"), ix, iy)
-    third = fold_last(third[:sy], passed(third[:sy], "y"), third[sy:], passed(third[sy:], "x"), iz, after=[back_done])
+    third = fold_last(third[:sy], passed(third[:sy], "y"), third[sy:], passed(third[sy:], "x"), iz, after=[gn1_parts[2], gn1_parts[3]])
     ready = third[0][0, 0, 0, :, :LANES]
     gw_sums = [held(member, [ready]) for member in gw_sums]
     third = [third[0]] + passed(third, "z")

time: 271 us -> 256 us (0.945)
  waiting for transfers between devices: 121 us -> 106 us
  Pallas kernels: 31.5 us -> 34.4 us
    ppermute x45 -> x44, waiting for transfers between devices: 121 us -> 98.8 us  [shift(): lax.ppermute(value, axis, [(a, (a + step) % size) for a in range(size)])]
    unnamed x171 -> x135, local copies, waits for them, and re-layouts: 33.6 us -> 29.6 us
    ppermute x0 -> x3, waiting for transfers between devices: none -> 3.37 us  [per_device(): ups[d] = lax.ppermute(ups[d], ('x', 'core'), pairs)]
    ppermute x0 -> x3, starting transfers between devices: none -> 3.21 us  [per_device(): ups[d] = lax.ppermute(ups[d], ('x', 'core'), pairs)]
    pallas_call x21 -> x25, Pallas kernels: 31.2 us -> 34.2 us  [call(): pl.pallas_call(whole, in_specs=specs + [pl.BlockSpec(memory_space=pl.ANY)...]
    ppermute x45 -> x44, starting transfers between devices: 58.5 us -> 55.5 us  [shift(): lax.ppermute(value, axis, [(a, (a + step) % size) for a in range(size)])]
  transfers between devices with their start and end apart: 47 -> 49, of which waited for: 33 -> 32; matrix products, arithmetic and copies ran while one was open for 1% -> 2% of each run, Pallas kernels for 8% -> 8%
where the time goes in v2:
time: 256 us; the launch traced here: 255 us
  waiting for transfers between devices  106 us (41%)
  starting transfers between devices  58.8 us (23%)
  local copies, waits for them, and re-layouts  34.8 us (14%)
  Pallas kernels  34.4 us (13%)
  between operations  17.4 us (7%)
  other arithmetic  3.23 us (1%)
    ppermute x44, waiting for transfers between devices, shift(): lax.ppermute(value, axis, [(a, (a + step) % size) for a in range(size)])  98.8 us
    ppermute x44, starting transfers between devices, shift(): lax.ppermute(value, axis, [(a, (a + step) % size) for a in range(size)])  55.5 us
    pallas_call x25, Pallas kernels, call(): pl.pallas_call(whole, in_specs=specs + [pl.BlockSpec(memory_space=pl.ANY)...  34.2 us
    unnamed x135, local copies, waits for them, and re-layouts  29.6 us
  transfers between devices with their start and end apart: 49, of which 32 were waited for; matrix products, arithmetic and copies ran while one was open for 2% of the time, Pallas kernels for 8%

profile of v2, /device:TPU:0, one launch (start us, length us, event | category | flops | bytes accessed | tf_op | source)
XLA Modules:
  0.0 255.1 jit_solution(14082102767484688308)
XLA Ops:
  9.7 3.0 %collective-permute-start.15 = (bf16[24,1152]{1,0:T(8,128)(2,1)S(1)}, bf16[24,1152]{1,0:T(8,128)(2,1)S(1)}, u32[]{:S(2)}, u32[]{:S(2)}) collective-permute-start(bf16[24,1152]{1,0:T(8,128)(2,1)S(1)} %get-tuple-element.91), channel_id=1, source_target_pairs={{0,2},{1,3},{2,0},{3,1},{4,6},{5,7},{6,4},{7,5},{8,10},{9,11},{10,... | collective-permute-start | bytes 165896 | tf_op jit(solution)/shard_map/ppermute | solution.py:808
  12.9 1.9 collective-permute-done.15.refs_2_
  18.6 1.6 collective-permute-start.4
  24.2 1.6 collective-permute-start
  27.1 2.7 %collective-permute-start.2 = (bf16[1,24,704]{2,1,0:T(8,128)(2,1)S(1)}, bf16[1,24,704]{2,1,0:T(8,128)(2,1)S(1)}, u32[]{:S(2)}, u32[]{:S(2)}) collective-permute-start(bf16[1,24,704]{2,1,0:T(8,128)(2,1)S(1)} %get-tuple-element.166), channel_id=1, source_target_pairs={{0,12},{4,0},{8,4},{12,8},{1,13},{5,1},{9,5},{13,9},{2,14},{6,2},{... | collective-permute-start | bytes 101384 | tf_op jit(solution)/shard_map/ppermute | solution.py:22
  30.1 1.7 collective-permute-done.1.refs_2_
  33.2 4.6 %collective-permute-done.3.refs_1_ = bf16[1,4,1,24,704]{4,3,2,1,0:T(8,128)(2,1)S(1)} collective-permute-done((bf16[1,4,1,24,704]{4,3,2,1,0:T(8,128)(2,1)S(1)}, bf16[1,4,1,24,704]{4,3,2,1,0:T(8,128)(2,1)S(1)}, u32[]{:S(2)}, u32[]{:S(2)}) %collective-permute-start.3) | collective-permute-done | bytes 135200 | tf_op jit(solution)/shard_map/ppermute | solution.py:22
  39.6 4.1 %collective-permute-start.7 = (bf16[128,768]{1,0:T(8,128)(2,1)S(1)}, bf16[128,768]{1,0:T(8,128)(2,1)S(1)}, u32[]{:S(2)}, u32[]{:S(2)}) collective-permute-start(bf16[128,768]{1,0:T(8,128)(2,1)S(1)} %bitcast.58), channel_id=1, source_target_pairs={{0,12},{4,0},{8,4},{12,8},{1,13},{5,1},{9,5},{13,9},{2,14},{6,2},{... | collective-permute-start | bytes 589832 | tf_op jit(solution)/shard_map/ppermute | solution.py:22
  43.8 9.2 %collective-permute-done.6.refs_2_.refs_3_ = bf16[128,768]{1,0:T(8,128)(2,1)S(1)} collective-permute-done((bf16[128,768]{1,0:T(8,128)(2,1)S(1)}, bf16[128,768]{1,0:T(8,128)(2,1)S(1)}, u32[]{:S(2)}, u32[]{:S(2)}) %collective-permute-start.6) | collective-permute-done | bytes 196640 | tf_op jit(solution)/shard_map/ppermute | solution.py:22
  53.2 2.0 collective-permute-done.8.refs_1_
  60.2 9.5 %collective-permute-done.9.refs_4_.refs_9_ = bf16[512,384]{1,0:T(8,128)(2,1)S(1)} collective-permute-done((bf16[512,384]{1,0:T(8,128)(2,1)S(1)}, bf16[512,384]{1,0:T(8,128)(2,1)S(1)}, u32[]{:S(2)}, u32[]{:S(2)}) %collective-permute-start.9) | collective-permute-done | bytes 393248 | tf_op jit(solution)/shard_map/ppermute | solution.py:22
  71.4 4.3 %attend.1 = (bf16[128,192]{1,0:T(8,128)(2,1)S(1)}, bf16[128,192]{1,0:T(8,128)(2,1)S(1)}, bf16[128,192]{1,0:T(8,128)(2,1)S(1)}, bf16[128,192]{1,0:T(8,128)(2,1)S(1)}, f32[2,512,256]{2,1,0:T(8,128)S(1)}) custom-call(s32[5]{0:T(128)S(1)} %stack.79.refs_0_, bf16[512,256]{1,0:T(8,128)(2,1)S(1)} %get-tuple-element.84.refs_1_, ...), custom_call_target="tpu_custom_call" | custom-call | flops 1 | bytes 1 | tf_op jit(solution)/shard_map/attend/pallas_call | solution.py:416
  76.8 4.3 %collective-permute-start.12 = (bf16[128,192]{1,0:T(8,128)(2,1)S(1)}, bf16[128,192]{1,0:T(8,128)(2,1)S(1)}, u32[]{:S(2)}, u32[]{:S(2)}) collective-permute-start(bf16[128,192]{1,0:T(8,128)(2,1)S(1)} %get-tuple-element.87), channel_id=1, source_target_pairs={{0,4},{4,8},{8,12},{12,0},{1,5},{5,9},{9,13},{13,1},{2,6},{6,10},{... | collective-permute-start | bytes 147464 | tf_op jit(solution)/shard_map/ppermute | solution.py:22
  81.1 1.8 collective-permute-start.13
  83.4 3.2 %collective-permute-done.12.refs_1_ = bf16[128,192]{1,0:T(8,128)(2,1)S(1)} collective-permute-done((bf16[128,192]{1,0:T(8,128)(2,1)S(1)}, bf16[128,192]{1,0:T(8,128)(2,1)S(1)}, u32[]{:S(2)}, u32[]{:S(2)}) %collective-permute-start.12) | collective-permute-done | bytes 49184 | tf_op jit(solution)/shard_map/ppermute | solution.py:22
  86.6 5.0 %collective-permute-done.13.refs_2_ = bf16[128,192]{1,0:T(8,128)(2,1)S(1)} collective-permute-done((bf16[128,192]{1,0:T(8,128)(2,1)S(1)}, bf16[128,192]{1,0:T(8,128)(2,1)S(1)}, u32[]{:S(2)}, u32[]{:S(2)}) %collective-permute-start.13) | collective-permute-done | bytes 49184 | tf_op jit(solution)/shard_map/ppermute | solution.py:22
  92.5 1.9 all-gather.2.cloned.1.call-done.refs_0_.refs_5_.refs_6_
  94.4 1.8 copy-done
  97.4 1.9 collective-permute-done.18.refs_3_.refs_7_
  101.4 1.6 collective-permute-start.19
  103.0 5.3 %collective-permute-done.19.refs_1_ = bf16[128,768]{1,0:T(8,128)(2,1)S(1)} collective-permute-done((bf16[128,768]{1,0:T(8,128)(2,1)S(1)}, bf16[128,768]{1,0:T(8,128)(2,1)S(1)}, u32[]{:S(2)}, u32[]{:S(2)}) %collective-permute-start.19) | collective-permute-done | bytes 196640 | tf_op jit(solution)/shard_map/ppermute | solution.py:22
  109.8 2.3 mlp_up.1
  120.4 4.2 %collective-permute-done.23.refs_2_ = bf16[128,768]{1,0:T(8,128)(2,1)} collective-permute-done((bf16[128,768]{1,0:T(8,128)(2,1)}, bf16[128,768]{1,0:T(8,128)(2,1)}, u32[]{:S(2)}, u32[]{:S(2)}) %collective-permute-start.23) | collective-permute-done | bytes 196640 | tf_op jit(solution)/shard_map/ppermute | solution.py:22
  127.6 2.0 finish.1
  130.5 1.6 collective-permute-start.24
  132.1 4.5 %collective-permute-done.24.refs_1_ = bf16[128,768]{1,0:T(8,128)(2,1)S(1)} collective-permute-done((bf16[128,768]{1,0:T(8,128)(2,1)S(1)}, bf16[128,768]{1,0:T(8,128)(2,1)S(1)}, u32[]{:S(2)}, u32[]{:S(2)}) %collective-permute-start.24) | collective-permute-done | bytes 196640 | tf_op jit(solution)/shard_map/ppermute | solution.py:22
  138.1 2.8 %mlp_back.1 = (f32[2,128,768]{2,1,0:T(8,128)S(1)}, bf16[2,128,768]{2,1,0:T(8,128)(2,1)S(1)}, bf16[512,768]{1,0:T(8,128)(2,1)S(1)}, bf16[512,768]{1,0:T(8,128)(2,1)S(1)}) custom-call(bf16[128,768]{1,0:T(8,128)(2,1)S(1)} %get-tuple-element.102.refs_0_, bf16[128,768]{1,0:T(8,128)(2,1)S(1)} %collective-permute-done.24.refs_1_, ...), custom_call_target="tpu_custom_call" | custom-call | flops 1 | bytes 1 | tf_op jit(solution)/shard_map/mlp_back/pallas_call | solution.py:416
  145.8 1.7 collective-permute-start.28
  147.4 5.3 %collective-permute-done.28.refs_2_ = bf16[128,768]{1,0:T(8,128)(2,1)S(1)} collective-permute-done((bf16[128,768]{1,0:T(8,128)(2,1)S(1)}, bf16[128,768]{1,0:T(8,128)(2,1)S(1)}, u32[]{:S(2)}, u32[]{:S(2)}) %collective-permute-start.28) | collective-permute-done | bytes 196640 | tf_op jit(solution)/shard_map/ppermute | solution.py:22
  153.9 1.8 out_back.1
  160.3 4.5 %collective-permute-done.29.refs_3_ = bf16[128,192]{1,0:T(8,128)(2,1)S(1)} collective-permute-done((bf16[128,192]{1,0:T(8,128)(2,1)S(1)}, bf16[128,192]{1,0:T(8,128)(2,1)S(1)}, u32[]{:S(2)}, u32[]{:S(2)}) %collective-permute-start.29) | collective-permute-done | bytes 49184 | tf_op jit(solution)/shard_map/ppermute | solution.py:22
  164.8 4.0 %collective-permute-done.30.refs_4_ = bf16[128,192]{1,0:T(8,128)(2,1)S(1)} collective-permute-done((bf16[128,192]{1,0:T(8,128)(2,1)S(1)}, bf16[128,192]{1,0:T(8,128)(2,1)S(1)}, u32[]{:S(2)}, u32[]{:S(2)}) %collective-permute-start.30) | collective-permute-done | bytes 49184 | tf_op jit(solution)/shard_map/ppermute | solution.py:22
  169.5 6.5 %attend_back.1 = (bf16[512,192]{1,0:T(8,128)(2,1)S(1)}, f32[2,512,384]{2,1,0:T(8,128)S(1)}, bf16[2,512,384]{2,1,0:T(8,128)(2,1)S(1)}) custom-call(s32[5]{0:T(128)S(1)} %copy-done.57, bf16[512,256]{1,0:T(8,128)(2,1)S(1)} %copy-done.32, bf16[128,192]{1,0:T(8,128)(2,1)S(1)} %get-tuple-element.113.refs_2_, bf16[128,192]{1,0:T(8,128)(2,1)S(1)} %collective-permute-done.29.refs_3_, ...), custom_call_target="tpu_custom_call" | custom-call | flops 1 | bytes 1 | tf_op jit(solution)/shard_map/attend_back/pallas_call | solution.py:416
  176.0 2.3 collective-permute-done.32.refs_1_
  181.3 9.2 %collective-permute-done.33.refs_2_ = bf16[512,384]{1,0:T(8,128)(2,1)S(1)} collective-permute-done((bf16[512,384]{1,0:T(8,128)(2,1)S(1)}, bf16[512,384]{1,0:T(8,128)(2,1)S(1)}, u32[]{:S(2)}, u32[]{:S(2)}) %collective-permute-start.33) | collective-permute-done | bytes 393248 | tf_op jit(solution)/shard_map/ppermute | solution.py:22
  192.6 1.7 join_back.1
  197.3 2.2 weights_back.1
  199.6 2.8 %collective-permute-done.34 = bf16[16,24,1536]{2,1,0:T(8,128)(2,1)S(1)} collective-permute-done((bf16[16,24,1536]{2,1,0:T(8,128)(2,1)S(1)}, bf16[16,24,1536]{2,1,0:T(8,128)(2,1)S(1)}, u32[]{:S(2)}, u32[]{:S(2)}) %collective-permute-start.34) | collective-permute-done | bytes 1179680 | tf_op jit(solution)/shard_map/ppermute | solution.py:22
  205.0 2.8 %collective-permute-start.39 = (bf16[128,768]{1,0:T(8,128)(2,1)}, bf16[128,768]{1,0:T(8,128)(2,1)S(1)}, u32[]{:S(2)}, u32[]{:S(2)}) collective-permute-start(bf16[128,768]{1,0:T(8,128)(2,1)} %get-tuple-element.139), channel_id=1, source_target_pairs={{0,8},{4,12},{8,0},{12,4},{1,9},{5,13},{9,1},{13,5},{2,10},{6,14},... | collective-permute-start | bytes 589832 | tf_op jit(solution)/shard_map/ppermute | solution.py:22
  207.8 3.7 %collective-permute-start.40 = (bf16[128,768]{1,0:T(8,128)(2,1)}, bf16[128,768]{1,0:T(8,128)(2,1)S(1)}, u32[]{:S(2)}, u32[]{:S(2)}) collective-permute-start(bf16[128,768]{1,0:T(8,128)(2,1)} %get-tuple-element.140), channel_id=1, source_target_pairs={{0,12},{4,0},{8,4},{12,8},{1,13},{5,1},{9,5},{13,9},{2,14},{6,2},{... | collective-permute-start | bytes 589832 | tf_op jit(solution)/shard_map/ppermute | solution.py:22
  212.3 2.5 collective-permute-done.36.refs_4_
  215.9 1.7 collective-permute-start.38
  217.6 6.5 %collective-permute-done.39.refs_5_.refs_2_ = bf16[128,768]{1,0:T(8,128)(2,1)S(1)} collective-permute-done((bf16[128,768]{1,0:T(8,128)(2,1)}, bf16[128,768]{1,0:T(8,128)(2,1)S(1)}, u32[]{:S(2)}, u32[]{:S(2)}) %collective-permute-start.39) | collective-permute-done | bytes 196640 | tf_op jit(solution)/shard_map/ppermute | solution.py:22
  224.3 2.3 reduce-scatter.2.cloned.1.call-done.refs_0_
  228.4 4.2 %collective-permute-start.46 = (bf16[128,768]{1,0:T(8,128)(2,1)S(1)}, bf16[128,768]{1,0:T(8,128)(2,1)S(1)}, u32[]{:S(2)}, u32[]{:S(2)}) collective-permute-start(bf16[128,768]{1,0:T(8,128)(2,1)S(1)} %copy-done.64), channel_id=1, source_target_pairs={{0,4},{4,8},{8,12},{12,0},{1,5},{5,9},{9,13},{13,1},{2,6},{6,10},{... | collective-permute-start | bytes 589832 | tf_op jit(solution)/shard_map/ppermute | solution.py:22
  232.8 3.4 %collective-permute-start.41 = (bf16[1,1,1,24,1536]{4,3,2,1,0:T(8,128)(2,1)S(1)}, bf16[1,1,1,24,1536]{4,3,2,1,0:T(8,128)(2,1)S(1)}, u32[]{:S(2)}, u32[]{:S(2)}) collective-permute-start(bf16[1,1,1,24,1536]{4,3,2,1,0:T(8,128)(2,1)S(1)} %get-tuple-element.142), channel_id=1, source_target_pairs={{0,4},{4,8},{8,12},{12,0},{1,5},{5,9},{9,13},{13,1},{2,6},{6,10},{... | collective-permute-start | bytes 221192 | tf_op jit(solution)/shard_map/ppermute | solution.py:22
  237.6 1.8 collective-permute-start.43
  241.6 1.8 collective-permute-done.42.refs_3_
  (260 shorter events, 74.4 us)
Async XLA Ops:
  7.2 87.2 %all-gather.2.cloned.1.call-start = ((), (), s32[]{:S(2)}) async-start(), calls=%async_computation.1 | async-start | bytes 3317760 | tf_op jit(solution)/shard_map/all_gather | solution.py:812
  9.7 5.1 %collective-permute-start.15 = (bf16[24,1152]{1,0:T(8,128)(2,1)S(1)}, bf16[24,1152]{1,0:T(8,128)(2,1)S(1)}, u32[]{:S(2)}, u32[]{:S(2)}) collective-permute-start(bf16[24,1152]{1,0:T(8,128)(2,1)S(1)} %get-tuple-element.91), channel_id=1, source_target_pairs={{0,2},{1,3},{2,0},{3,1},{4,6},{5,7},{6,4},{7,5},{8,10},{9,11},{10,... | collective-permute-start | bytes 165896 | tf_op jit(solution)/shard_map/ppermute | solution.py:808
  12.7 2.1 collective-permute-start.16
  12.7 3.6 %collective-permute-start.17 = (bf16[24,1152]{1,0:T(8,128)(2,1)S(1)}, bf16[24,1152]{1,0:T(8,128)(2,1)S(1)}, u32[]{:S(2)}, u32[]{:S(2)}) collective-permute-start(bf16[24,1152]{1,0:T(8,128)(2,1)S(1)} %get-tuple-element.93), channel_id=1, source_target_pairs={{0,3},{1,2},{2,1},{3,0},{4,7},{5,6},{6,5},{7,4},{8,11},{9,10},{10,... | collective-permute-start | bytes 165896 | tf_op jit(solution)/shard_map/ppermute | solution.py:808
  18.5 208.0 %reduce-scatter.2.cloned.1.call-start = ((), (), s32[]{:S(2)}) async-start(), calls=%async_computation.2 | async-start | bytes 2654208 | tf_op jit(solution)/shard_map/reduce_scatter | solution.py:839
  18.6 19.2 %collective-permute-start.4 = (bf16[128,768]{1,0:T(8,128)(2,1)}, bf16[128,768]{1,0:T(8,128)(2,1)S(1)}, u32[]{:S(2)}, u32[]{:S(2)}) collective-permute-start(bf16[128,768]{1,0:T(8,128)(2,1)} %bitcast.56), channel_id=1, source_target_pairs={{0,4},{4,8},{8,12},{12,0},{1,5},{5,9},{9,13},{13,1},{2,6},{6,10},{... | collective-permute-start | bytes 589832 | tf_op jit(solution)/shard_map/ppermute | solution.py:22
  24.2 5.9 %collective-permute-start = (bf16[1,24,704]{2,1,0:T(8,128)(2,1)S(1)}, bf16[1,24,704]{2,1,0:T(8,128)(2,1)S(1)}, u32[]{:S(2)}, u32[]{:S(2)}) collective-permute-start(bf16[1,24,704]{2,1,0:T(8,128)(2,1)S(1)} %get-tuple-element.168), channel_id=1, source_target_pairs={{0,4},{4,8},{8,12},{12,0},{1,5},{5,9},{9,13},{13,1},{2,6},{6,10},{... | collective-permute-start | bytes 101384 | tf_op jit(solution)/shard_map/ppermute | solution.py:22
  25.8 6.0 %collective-permute-start.1 = (bf16[1,24,704]{2,1,0:T(8,128)(2,1)S(1)}, bf16[1,24,704]{2,1,0:T(8,128)(2,1)S(1)}, u32[]{:S(2)}, u32[]{:S(2)}) collective-permute-start(bf16[1,24,704]{2,1,0:T(8,128)(2,1)S(1)} %get-tuple-element.167), channel_id=1, source_target_pairs={{0,8},{4,12},{8,0},{12,4},{1,9},{5,13},{9,1},{13,5},{2,10},{6,14},... | collective-permute-start | bytes 101384 | tf_op jit(solution)/shard_map/ppermute | solution.py:22
  27.1 5.5 %collective-permute-start.2 = (bf16[1,24,704]{2,1,0:T(8,128)(2,1)S(1)}, bf16[1,24,704]{2,1,0:T(8,128)(2,1)S(1)}, u32[]{:S(2)}, u32[]{:S(2)}) collective-permute-start(bf16[1,24,704]{2,1,0:T(8,128)(2,1)S(1)} %get-tuple-element.166), channel_id=1, source_target_pairs={{0,12},{4,0},{8,4},{12,8},{1,13},{5,1},{9,5},{13,9},{2,14},{6,2},{... | collective-permute-start | bytes 101384 | tf_op jit(solution)/shard_map/ppermute | solution.py:22
  32.6 5.2 %collective-permute-start.3 = (bf16[1,4,1,24,704]{4,3,2,1,0:T(8,128)(2,1)S(1)}, bf16[1,4,1,24,704]{4,3,2,1,0:T(8,128)(2,1)S(1)}, u32[]{:S(2)}, u32[]{:S(2)}) collective-permute-start(bf16[1,4,1,24,704]{4,3,2,1,0:T(8,128)(2,1)S(1)} %bitcast.67), channel_id=1, source_target_pairs={{0,2},{2,0},{1,3},{3,1},{4,6},{6,4},{5,7},{7,5},{8,10},{10,8},{9,1... | collective-permute-start | bytes 405512 | tf_op jit(solution)/shard_map/ppermute | solution.py:22
  37.8 15.2 %collective-permute-start.5 = (bf16[1,4,2,24,704]{4,3,2,1,0:T(8,128)(2,1)S(1)}, bf16[1,4,2,24,704]{4,3,2,1,0:T(8,128)(2,1)S(1)}, u32[]{:S(2)}, u32[]{:S(2)}) collective-permute-start(bf16[1,4,2,24,704]{4,3,2,1,0:T(8,128)(2,1)S(1)} %arrange.7.refs_0_), channel_id=1, source_target_pairs={{0,16},{16,0},{1,17},{17,1},{2,18},{18,2},{3,19},{19,3},{4,20},{20... | collective-permute-start | bytes 811016 | tf_op jit(solution)/shard_map/ppermute | solution.py:22
  39.3 13.7 %collective-permute-start.6 = (bf16[128,768]{1,0:T(8,128)(2,1)S(1)}, bf16[128,768]{1,0:T(8,128)(2,1)S(1)}, u32[]{:S(2)}, u32[]{:S(2)}) collective-permute-start(bf16[128,768]{1,0:T(8,128)(2,1)S(1)} %bitcast.57), channel_id=1, source_target_pairs={{0,8},{4,12},{8,0},{12,4},{1,9},{5,13},{9,1},{13,5},{2,10},{6,14},... | collective-permute-start | bytes 589832 | tf_op jit(solution)/shard_map/ppermute | solution.py:22
  39.6 13.4 %collective-permute-start.7 = (bf16[128,768]{1,0:T(8,128)(2,1)S(1)}, bf16[128,768]{1,0:T(8,128)(2,1)S(1)}, u32[]{:S(2)}, u32[]{:S(2)}) collective-permute-start(bf16[128,768]{1,0:T(8,128)(2,1)S(1)} %bitcast.58), channel_id=1, source_target_pairs={{0,12},{4,0},{8,4},{12,8},{1,13},{5,1},{9,5},{13,9},{2,14},{6,2},{... | collective-permute-start | bytes 589832 | tf_op jit(solution)/shard_map/ppermute | solution.py:22
  53.1 2.1 collective-permute-start.8
  58.5 11.2 %collective-permute-start.9 = (bf16[512,384]{1,0:T(8,128)(2,1)S(1)}, bf16[512,384]{1,0:T(8,128)(2,1)S(1)}, u32[]{:S(2)}, u32[]{:S(2)}) collective-permute-start(bf16[512,384]{1,0:T(8,128)(2,1)S(1)} %get-tuple-element.85.refs_3_.refs_8_), channel_id=1, source_target_pairs={{0,2},{2,0},{1,3},{3,1},{4,6},{6,4},{5,7},{7,5},{8,10},{10,8},{9,1... | collective-permute-start | bytes 1179656 | tf_op jit(solution)/shard_map/ppermute | solution.py:22
  59.8 10.8 %collective-permute-start.10 = (bf16[512,384]{1,0:T(8,128)(2,1)S(1)}, bf16[512,384]{1,0:T(8,128)(2,1)S(1)}, u32[]{:S(2)}, u32[]{:S(2)}) collective-permute-start(bf16[512,384]{1,0:T(8,128)(2,1)S(1)} %get-tuple-element.85.refs_3_.refs_8_), channel_id=1, source_target_pairs={{0,1},{1,0},{2,3},{3,2},{4,5},{5,4},{6,7},{7,6},{8,9},{9,8},{10,11... | collective-permute-start | bytes 1179656 | tf_op jit(solution)/shard_map/ppermute | solution.py:22
  69.7 1.7 collective-permute-start.11
  76.8 9.8 %collective-permute-start.12 = (bf16[128,192]{1,0:T(8,128)(2,1)S(1)}, bf16[128,192]{1,0:T(8,128)(2,1)S(1)}, u32[]{:S(2)}, u32[]{:S(2)}) collective-permute-start(bf16[128,192]{1,0:T(8,128)(2,1)S(1)} %get-tuple-element.87), channel_id=1, source_target_pairs={{0,4},{4,8},{8,12},{12,0},{1,5},{5,9},{9,13},{13,1},{2,6},{6,10},{... | collective-permute-start | bytes 147464 | tf_op jit(solution)/shard_map/ppermute | solution.py:22
  81.1 10.6 %collective-permute-start.13 = (bf16[128,192]{1,0:T(8,128)(2,1)S(1)}, bf16[128,192]{1,0:T(8,128)(2,1)S(1)}, u32[]{:S(2)}, u32[]{:S(2)}) collective-permute-start(bf16[128,192]{1,0:T(8,128)(2,1)S(1)} %get-tuple-element.88), channel_id=1, source_target_pairs={{0,8},{4,12},{8,0},{12,4},{1,9},{5,13},{9,1},{13,5},{2,10},{6,14},... | collective-permute-start | bytes 147464 | tf_op jit(solution)/shard_map/ppermute | solution.py:22
  82.9 8.8 %collective-permute-start.14 = (bf16[128,192]{1,0:T(8,128)(2,1)S(1)}, bf16[128,192]{1,0:T(8,128)(2,1)S(1)}, u32[]{:S(2)}, u32[]{:S(2)}) collective-permute-start(bf16[128,192]{1,0:T(8,128)(2,1)S(1)} %get-tuple-element.89), channel_id=1, source_target_pairs={{0,12},{4,0},{8,4},{12,8},{1,13},{5,1},{9,5},{13,9},{2,14},{6,2},{... | collective-permute-start | bytes 147464 | tf_op jit(solution)/shard_map/ppermute | solution.py:22
  97.3 2.1 collective-permute-start.18
  101.4 6.9 %collective-permute-start.19 = (bf16[128,768]{1,0:T(8,128)(2,1)S(1)}, bf16[128,768]{1,0:T(8,128)(2,1)S(1)}, u32[]{:S(2)}, u32[]{:S(2)}) collective-permute-start(bf16[128,768]{1,0:T(8,128)(2,1)S(1)} %get-tuple-element.94.refs_0_), channel_id=1, source_target_pairs={{0,2},{2,0},{1,3},{3,1},{4,6},{6,4},{5,7},{7,5},{8,10},{10,8},{9,1... | collective-permute-start | bytes 589832 | tf_op jit(solution)/shard_map/ppermute | solution.py:22
  103.0 5.3 %collective-permute-start.20 = (bf16[128,768]{1,0:T(8,128)(2,1)S(1)}, bf16[128,768]{1,0:T(8,128)(2,1)S(1)}, u32[]{:S(2)}, u32[]{:S(2)}) collective-permute-start(bf16[128,768]{1,0:T(8,128)(2,1)S(1)} %get-tuple-element.94.refs_0_), channel_id=1, source_target_pairs={{0,1},{1,0},{2,3},{3,2},{4,5},{5,4},{6,7},{7,6},{8,9},{9,8},{10,11... | collective-permute-start | bytes 589832 | tf_op jit(solution)/shard_map/ppermute | solution.py:22
  108.4 1.4 collective-permute-start.21
  114.1 1.7 collective-permute-start.22
  117.3 7.3 %collective-permute-start.23 = (bf16[128,768]{1,0:T(8,128)(2,1)}, bf16[128,768]{1,0:T(8,128)(2,1)}, u32[]{:S(2)}, u32[]{:S(2)}) collective-permute-start(bf16[128,768]{1,0:T(8,128)(2,1)} %get-tuple-element.98), channel_id=1, source_target_pairs={{0,2},{2,0},{1,3},{3,1},{4,6},{6,4},{5,7},{7,5},{8,10},{10,8},{9,1... | collective-permute-start | bytes 589832 | tf_op jit(solution)/shard_map/ppermute | solution.py:22
  130.5 6.1 %collective-permute-start.24 = (bf16[128,768]{1,0:T(8,128)(2,1)S(1)}, bf16[128,768]{1,0:T(8,128)(2,1)S(1)}, u32[]{:S(2)}, u32[]{:S(2)}) collective-permute-start(bf16[128,768]{1,0:T(8,128)(2,1)S(1)} %get-tuple-element.102.refs_0_), channel_id=1, source_target_pairs={{0,2},{2,0},{1,3},{3,1},{4,6},{6,4},{5,7},{7,5},{8,10},{10,8},{9,1... | collective-permute-start | bytes 589832 | tf_op jit(solution)/shard_map/ppermute | solution.py:22
  132.1 4.5 %collective-permute-start.25 = (bf16[128,768]{1,0:T(8,128)(2,1)S(1)}, bf16[128,768]{1,0:T(8,128)(2,1)S(1)}, u32[]{:S(2)}, u32[]{:S(2)}) collective-permute-start(bf16[128,768]{1,0:T(8,128)(2,1)S(1)} %get-tuple-element.102.refs_0_), channel_id=1, source_target_pairs={{0,1},{1,0},{2,3},{3,2},{4,5},{5,4},{6,7},{7,6},{8,9},{9,8},{10,11... | collective-permute-start | bytes 589832 | tf_op jit(solution)/shard_map/ppermute | solution.py:22
  140.9 1.8 collective-permute-start.27
  145.8 7.0 %collective-permute-start.28 = (bf16[128,768]{1,0:T(8,128)(2,1)S(1)}, bf16[128,768]{1,0:T(8,128)(2,1)S(1)}, u32[]{:S(2)}, u32[]{:S(2)}) collective-permute-start(bf16[128,768]{1,0:T(8,128)(2,1)S(1)} %get-tuple-element.107), channel_id=1, source_target_pairs={{0,2},{2,0},{1,3},{3,1},{4,6},{6,4},{5,7},{7,5},{8,10},{10,8},{9,1... | collective-permute-start | bytes 589832 | tf_op jit(solution)/shard_map/ppermute | solution.py:22
  156.5 8.4 %collective-permute-start.29 = (bf16[128,192]{1,0:T(8,128)(2,1)S(1)}, bf16[128,192]{1,0:T(8,128)(2,1)S(1)}, u32[]{:S(2)}, u32[]{:S(2)}) collective-permute-start(bf16[128,192]{1,0:T(8,128)(2,1)S(1)} %get-tuple-element.114), channel_id=1, source_target_pairs={{0,4},{4,8},{8,12},{12,0},{1,5},{5,9},{9,13},{13,1},{2,6},{6,10},{... | collective-permute-start | bytes 147464 | tf_op jit(solution)/shard_map/ppermute | solution.py:22
  157.5 11.2 %collective-permute-start.30 = (bf16[128,192]{1,0:T(8,128)(2,1)S(1)}, bf16[128,192]{1,0:T(8,128)(2,1)S(1)}, u32[]{:S(2)}, u32[]{:S(2)}) collective-permute-start(bf16[128,192]{1,0:T(8,128)(2,1)S(1)} %get-tuple-element.115), channel_id=1, source_target_pairs={{0,8},{4,12},{8,0},{12,4},{1,9},{5,13},{9,1},{13,5},{2,10},{6,14},... | collective-permute-start | bytes 147464 | tf_op jit(solution)/shard_map/ppermute | solution.py:22
  159.0 9.8 %collective-permute-start.31 = (bf16[128,192]{1,0:T(8,128)(2,1)S(1)}, bf16[128,192]{1,0:T(8,128)(2,1)S(1)}, u32[]{:S(2)}, u32[]{:S(2)}) collective-permute-start(bf16[128,192]{1,0:T(8,128)(2,1)S(1)} %get-tuple-element.116), channel_id=1, source_target_pairs={{0,12},{4,0},{8,4},{12,8},{1,13},{5,1},{9,5},{13,9},{2,14},{6,2},{... | collective-permute-start | bytes 147464 | tf_op jit(solution)/shard_map/ppermute | solution.py:22
  176.0 2.4 collective-permute-start.32
  179.4 11.2 %collective-permute-start.33 = (bf16[512,384]{1,0:T(8,128)(2,1)S(1)}, bf16[512,384]{1,0:T(8,128)(2,1)S(1)}, u32[]{:S(2)}, u32[]{:S(2)}) collective-permute-start(bf16[512,384]{1,0:T(8,128)(2,1)S(1)} %get-tuple-element.121), channel_id=1, source_target_pairs={{0,2},{2,0},{1,3},{3,1},{4,6},{6,4},{5,7},{7,5},{8,10},{10,8},{9,1... | collective-permute-start | bytes 1179656 | tf_op jit(solution)/shard_map/ppermute | solution.py:22
  199.5 2.9 %collective-permute-start.34 = (bf16[16,24,1536]{2,1,0:T(8,128)(2,1)S(1)}, bf16[16,24,1536]{2,1,0:T(8,128)(2,1)S(1)}, u32[]{:S(2)}, u32[]{:S(2)}) collective-permute-start(bf16[16,24,1536]{2,1,0:T(8,128)(2,1)S(1)} %get-tuple-element.130), channel_id=1, source_target_pairs={{0,1},{1,0},{2,3},{3,2},{4,5},{5,4},{6,7},{7,6},{8,9},{9,8},{10,11... | collective-permute-start | bytes 3538952 | tf_op jit(solution)/shard_map/ppermute | solution.py:22
  203.2 9.1 %collective-permute-start.35 = (bf16[2,4,1,24,768]{4,3,2,1,0:T(8,128)(2,1)S(1)}, bf16[2,4,1,24,768]{4,3,2,1,0:T(8,128)(2,1)S(1)}, u32[]{:S(2)}, u32[]{:S(2)}) collective-permute-start(bf16[2,4,1,24,768]{4,3,2,1,0:T(8,128)(2,1)S(1)} %get-tuple-element.132), channel_id=1, source_target_pairs={{0,2},{2,0},{1,3},{3,1},{4,6},{6,4},{5,7},{7,5},{8,10},{10,8},{9,1... | collective-permute-start | bytes 884744 | tf_op jit(solution)/shard_map/ppermute | solution.py:22
  204.8 10.0 %collective-permute-start.36 = (bf16[1,4,2,24,768]{4,3,2,1,0:T(8,128)(2,1)S(1)}, bf16[1,4,2,24,768]{4,3,2,1,0:T(8,128)(2,1)S(1)}, u32[]{:S(2)}, u32[]{:S(2)}) collective-permute-start(bf16[1,4,2,24,768]{4,3,2,1,0:T(8,128)(2,1)S(1)} %get-tuple-element.134), channel_id=1, source_target_pairs={{0,16},{16,0},{1,17},{17,1},{2,18},{18,2},{3,19},{19,3},{4,20},{20... | collective-permute-start | bytes 884744 | tf_op jit(solution)/shard_map/ppermute | solution.py:22
  205.0 19.2 %collective-permute-start.39 = (bf16[128,768]{1,0:T(8,128)(2,1)}, bf16[128,768]{1,0:T(8,128)(2,1)S(1)}, u32[]{:S(2)}, u32[]{:S(2)}) collective-permute-start(bf16[128,768]{1,0:T(8,128)(2,1)} %get-tuple-element.139), channel_id=1, source_target_pairs={{0,8},{4,12},{8,0},{12,4},{1,9},{5,13},{9,1},{13,5},{2,10},{6,14},... | collective-permute-start | bytes 589832 | tf_op jit(solution)/shard_map/ppermute | solution.py:22
  207.8 16.3 %collective-permute-start.40 = (bf16[128,768]{1,0:T(8,128)(2,1)}, bf16[128,768]{1,0:T(8,128)(2,1)S(1)}, u32[]{:S(2)}, u32[]{:S(2)}) collective-permute-start(bf16[128,768]{1,0:T(8,128)(2,1)} %get-tuple-element.140), channel_id=1, source_target_pairs={{0,12},{4,0},{8,4},{12,8},{1,13},{5,1},{9,5},{13,9},{2,14},{6,2},{... | collective-permute-start | bytes 589832 | tf_op jit(solution)/shard_map/ppermute | solution.py:22
  215.5 8.6 %collective-permute-start.37 = (bf16[1,4,1,24,768]{4,3,2,1,0:T(8,128)(2,1)S(1)}, bf16[1,4,1,24,768]{4,3,2,1,0:T(8,128)(2,1)S(1)}, u32[]{:S(2)}, u32[]{:S(2)}) collective-permute-start(bf16[1,4,1,24,768]{4,3,2,1,0:T(8,128)(2,1)S(1)} %get-tuple-element.136), channel_id=1, source_target_pairs={{0,16},{16,0},{1,17},{17,1},{2,18},{18,2},{3,19},{19,3},{4,20},{20... | collective-permute-start | bytes 442376 | tf_op jit(solution)/shard_map/ppermute | solution.py:22
  215.9 8.3 %collective-permute-start.38 = (bf16[1,4,1,24,768]{4,3,2,1,0:T(8,128)(2,1)S(1)}, bf16[1,4,1,24,768]{4,3,2,1,0:T(8,128)(2,1)S(1)}, u32[]{:S(2)}, u32[]{:S(2)}) collective-permute-start(bf16[1,4,1,24,768]{4,3,2,1,0:T(8,128)(2,1)S(1)} %get-tuple-element.138), channel_id=1, source_target_pairs={{0,2},{2,0},{1,3},{3,1},{4,6},{6,4},{5,7},{7,5},{8,10},{10,8},{9,1... | collective-permute-start | bytes 442376 | tf_op jit(solution)/shard_map/ppermute | solution.py:22
  228.3 4.4 %collective-permute-start.44 = (bf16[1,1,1,2,24,768]{5,4,3,2,1,0:T(8,128)(2,1)S(1)}, bf16[1,1,1,2,24,768]{5,4,3,2,1,0:T(8,128)(2,1)S(1)}, u32[]{:S(2)}, u32[]{:S(2)}) collective-permute-start(bf16[1,1,1,2,24,768]{5,4,3,2,1,0:T(8,128)(2,1)S(1)} %get-tuple-element.164), channel_id=1, source_target_pairs={{0,2},{2,0},{1,3},{3,1},{4,6},{6,4},{5,7},{7,5},{8,10},{10,8},{9,1... | collective-permute-start | bytes 221192 | tf_op jit(solution)/shard_map/ppermute | solution.py:22
  228.4 11.0 %collective-permute-start.46 = (bf16[128,768]{1,0:T(8,128)(2,1)S(1)}, bf16[128,768]{1,0:T(8,128)(2,1)S(1)}, u32[]{:S(2)}, u32[]{:S(2)}) collective-permute-start(bf16[128,768]{1,0:T(8,128)(2,1)S(1)} %copy-done.64), channel_id=1, source_target_pairs={{0,4},{4,8},{8,12},{12,0},{1,5},{5,9},{9,13},{13,1},{2,6},{6,10},{... | collective-permute-start | bytes 589832 | tf_op jit(solution)/shard_map/ppermute | solution.py:22
  232.7 7.8 %collective-permute-start.45 = (bf16[1,1,2,1,24,768]{5,4,3,2,1,0:T(8,128)(2,1)S(1)}, bf16[1,1,2,1,24,768]{5,4,3,2,1,0:T(8,128)(2,1)S(1)}, u32[]{:S(2)}, u32[]{:S(2)}) collective-permute-start(bf16[1,1,2,1,24,768]{5,4,3,2,1,0:T(8,128)(2,1)S(1)} %get-tuple-element.162), channel_id=1, source_target_pairs={{0,1},{1,0},{2,3},{3,2},{4,5},{5,4},{6,7},{7,6},{8,9},{9,8},{10,11... | collective-permute-start | bytes 221192 | tf_op jit(solution)/shard_map/ppermute | solution.py:22
  232.8 8.8 %collective-permute-start.41 = (bf16[1,1,1,24,1536]{4,3,2,1,0:T(8,128)(2,1)S(1)}, bf16[1,1,1,24,1536]{4,3,2,1,0:T(8,128)(2,1)S(1)}, u32[]{:S(2)}, u32[]{:S(2)}) collective-permute-start(bf16[1,1,1,24,1536]{4,3,2,1,0:T(8,128)(2,1)S(1)} %get-tuple-element.142), channel_id=1, source_target_pairs={{0,4},{4,8},{8,12},{12,0},{1,5},{5,9},{9,13},{13,1},{2,6},{6,10},{... | collective-permute-start | bytes 221192 | tf_op jit(solution)/shard_map/ppermute | solution.py:22
  236.3 7.1 %collective-permute-start.42 = (bf16[1,1,1,24,1536]{4,3,2,1,0:T(8,128)(2,1)S(1)}, bf16[1,1,1,24,1536]{4,3,2,1,0:T(8,128)(2,1)S(1)}, u32[]{:S(2)}, u32[]{:S(2)}) collective-permute-start(bf16[1,1,1,24,1536]{4,3,2,1,0:T(8,128)(2,1)S(1)} %get-tuple-element.143), channel_id=1, source_target_pairs={{0,8},{4,12},{8,0},{12,4},{1,9},{5,13},{9,1},{13,5},{2,10},{6,14},... | collective-permute-start | bytes 221192 | tf_op jit(solution)/shard_map/ppermute | solution.py:22
  237.6 5.8 %collective-permute-start.43 = (bf16[1,1,1,24,1536]{4,3,2,1,0:T(8,128)(2,1)S(1)}, bf16[1,1,1,24,1536]{4,3,2,1,0:T(8,128)(2,1)S(1)}, u32[]{:S(2)}, u32[]{:S(2)}) collective-permute-start(bf16[1,1,1,24,1536]{4,3,2,1,0:T(8,128)(2,1)S(1)} %get-tuple-element.144), channel_id=1, source_target_pairs={{0,12},{4,0},{8,4},{12,8},{1,13},{5,1},{9,5},{13,9},{2,14},{6,2},{... | collective-permute-start | bytes 221192 | tf_op jit(solution)/shard_map/ppermute | solution.py:22
  (68 other events, 586.1 us)
Sparse Core Ops, SparseCore 0:
  18.7 75.7 all-gather.1
  145.8 80.6 reduce-scatter.1

commit v3 on v2

--- a/solution.py
+++ b/solution.py
@@ -59,7 +59,7 @@
     return some + [shift(member, "core", 1) for member in some]
 
 
-def fold_tokens(kept, sent, after=()):
+def fold_tokens(kept, sent, own=F32):
     came = shift(sent, "core", 1)
     size = kept.shape[0]
     shape = kept.shape[1:]
@@ -68,7 +68,7 @@
         for d in range(size):
             outs[d][...] = (kept_ref[d] + came_ref[d].astype(F32)).astype(outs[d].dtype)
 
-    terms = call(body, (kept, came), [(shape, BF if d else F32) for d in range(size)], "fold_tokens", 0, after)
+    terms = call(body, (kept, came), [(shape, BF if d else own) for d in range(size)], "fold_tokens")
     return [terms[0]] + [shift(terms[d], "x", -d) for d in range(1, size)]
 
 
@@ -91,19 +91,19 @@
     return pltpu.CompilerParams(vmem_limit_bytes=mib * 1024 * 1024)
 
 
-def pack_one(w_qkv, flat, seg, mask):
+def pack_one(w_qkv, flat, marks):
     rows, width = w_qkv.shape[0], w_qkv.shape[1] // 3
     group = width // ZS
     hd = HEAD_DIM
     upc = flat.shape[0] - 8
 
-    def body(qkv_ref, flat_ref, seg_ref, mask_ref, one_ref, vec):
+    def body(qkv_ref, flat_ref, marks_ref, one_ref, vec):
         vec[...] = jnp.zeros_like(vec)
         vec[0:8 + upc, 0:rows] = flat_ref[...].astype(F32)
-        count = jnp.sum(mask_ref[...].astype(F32), -1, keepdims=True)
+        count = jnp.sum(marks_ref[1:2, :].astype(F32), -1, keepdims=True)
         lane = lax.broadcasted_iota(jnp.int32, (LANES, LANES), 1)
         vec[...] = jnp.where(lane == 8 + upc, count, vec[...].T)
-        ids = seg_ref[...].astype(F32)
+        ids = marks_ref[0:1, :].astype(F32)
         vec[0:1, hd:] = ids[:, 0:hd]
         vec[1:2, hd:] = ids[:, hd:]
         cols = vec[0:rows, :].astype(BF)
@@ -117,7 +117,7 @@
             one_ref[g, :, 9 * hd:11 * hd] = cols
 
     outs = [((ZS, rows, 11 * hd), BF)]
-    return call(body, (w_qkv, flat, seg, mask), outs, "pack_one", scratch=[pltpu.VMEM((LANES, LANES), F32)])[0]
+    return call(body, (w_qkv, flat, marks), outs, "pack_one", scratch=[pltpu.VMEM((LANES, LANES), F32)])[0]
 
 
 def pack_up(place, w_up, w_out, ffd, sx):
@@ -200,7 +200,7 @@
     hd = HEAD_DIM
     group = 3 * hd
 
-    def body(place_ref, h0, h1, h2, h3, w_ref, vec_ref, n1_ref, q_ref, kv_ref, all_ref):
+    def body(place_ref, h0, h1, h2, h3, w_ref, vec_ref, kv_ref, q_ref, saved_ref):
         qb = jnp.zeros((1, group), F32)
         vb = jnp.zeros((1, group), F32)
         for g in range(ZS):
@@ -209,10 +209,10 @@
             vb = jnp.where(here, vec_ref[1:2, g * group:(g + 1) * group], vb)
         for d, piece in enumerate((h0, h1, h2, h3)):
             spot = pl.ds(pl.multiple_of(lax.rem(place_ref[0] + ZS - d, ZS) * rows, rows), rows)
-            all_ref[spot, :] = piece[...]
+            saved_ref[spot, width:] = piece[...]
             normed, _ = norm_parts(piece[...].astype(F32))
             n1 = (normed * vec_ref[4:5, :] + vec_ref[5:6, :]).astype(BF)
-            n1_ref[spot, :] = n1
+            saved_ref[spot, 0:width] = n1
             joined = dot(n1, w_ref[:, 0:9 * hd])
             kv_ref[spot, 0:3 * hd] = joined[:, 0:3 * hd].astype(BF)
             kv_ref[spot, 3 * hd:4 * hd] = (joined[:, 3 * hd:4 * hd] + vb[:, 2 * hd:]).astype(BF)
@@ -221,7 +221,7 @@
             q_ref[spot, 0:3 * hd] = q.astype(BF)
             q_ref[spot, 3 * hd:4 * hd] = jnp.zeros((rows, hd), BF)
 
-    outs = [((total, width), BF), ((total, 4 * hd), BF), ((total, 6 * hd), BF), ((total, width), BF)]
+    outs = [((total, 6 * hd), BF), ((total, 4 * hd), BF), ((total, 2 * width), BF)]
     return call(body, (place, pieces[0], *pieces[1:], one, vectors), outs, "project", 1)
 
 
@@ -308,8 +308,9 @@
 
 def attend_back_kernel(order, q_ref, gc0, gc1, gc2, gc3, both_ref, seg_ref, *rest):
     ctx_ref, tot_ref = both_ref.at[0], both_ref.at[1]
-    count = len(rest) - 9
-    kv_refs, (dq_ref, kept_ref, sent_ref), (keys, bias, ge, acc, gctx_ref, turned) = rest[:count], rest[count:count + 3], rest[count + 3:]
+    count = len(rest) - 10
+    kv_refs, (dq_ref, kept_ref, sent_ref, done_ref), (keys, bias, ge, acc, gctx_ref, turned) = rest[:count], rest[count:count + 4], rest[count + 4:]
+    done_ref[...] = jnp.zeros_like(done_ref)
     total = q_ref.shape[0]
     rows = total // ZS
     for d, ref in enumerate((gc0, gc1, gc2, gc3)):
@@ -372,7 +373,7 @@
     total = q.shape[0]
     count = len(kvs)
     span = count * total // ZS
-    outs = [((total, 3 * HEAD_DIM), BF), ((count // 2, total, 6 * HEAD_DIM), F32), ((count // 2, total, 6 * HEAD_DIM), BF)]
+    outs = [((total, 3 * HEAD_DIM), BF), ((count // 2, total, 6 * HEAD_DIM), F32), ((count // 2, total, 6 * HEAD_DIM), BF), ((8, LANES), F32)]
     scratch = [
         pltpu.VMEM((ZS * span, 3 * LANES), BF),
         pltpu.VMEM((span, total), F32),
@@ -602,19 +603,48 @@
     return call(body, (*grads, slope, *mlp_parts(weights, ff)), outs, "mlp_back")
 
 
-def mlp_weights(grads, saved, gpre, after):
+def mlp_weights(place, grads, saved, gpre, size, after):
     width = grads.shape[1]
     ff = gpre.shape[1]
-
-    def body(g_ref, saved_ref, gpre_ref, *outs):
-        down_ref, up_ref = (outs[0].at[:, 0:width], outs[0].at[:, width:]) if ff == width else outs[:2]
-        down_ref[...] = dot_tn(saved_ref[:, 0:ff], g_ref[...]).astype(BF)
-        up_ref[...] = dot_tn(saved_ref[:, ff:], gpre_ref[...]).astype(BF)
-        outs[-1][...] = jnp.sum(gpre_ref[...].astype(F32), 0, keepdims=True)
-
-    outs = [((width, 2 * width), BF)] if ff == width else [((ff, width), BF), ((width, ff), BF)]
-    *grads, sums = call(body, (grads, saved, gpre), outs + [((1, ff), F32)], "mlp_weights", after=after)
-    return grads, sums
+    joined = ff == width
+    down, up = ff // size, width // size
+    direct = down % LANES == 0 and up % LANES == 0
+
+    def body(place_ref, g_ref, saved_ref, gpre_ref, *refs):
+        outs, sums_ref, rest = refs[:size if joined else 2 * size], refs[size if joined else 2 * size], refs[size + 1 if joined else 2 * size + 1:]
+        if not direct:
+            rest[0][...] = dot_tn(saved_ref[:, 0:ff], g_ref[...])
+            rest[1][...] = dot_tn(saved_ref[:, ff:], gpre_ref[...])
+        for d in range(size):
+            y = lax.rem(place_ref[0] + d, size)
+            if direct:
+                first = dot_tn(saved_ref[:, pl.ds(pl.multiple_of(y * down, LANES), down)], g_ref[...])
+                second = dot_tn(saved_ref[:, pl.ds(pl.multiple_of(ff + y * up, LANES), up)], gpre_ref[...])
+            else:
+                first = rest[0][pl.ds(pl.multiple_of(y * down, 16), down), :]
+                second = rest[1][pl.ds(pl.multiple_of(y * up, 16), up), :]
+            if joined:
+                outs[d][:, 0:width] = first.astype(BF)
+                outs[d][:, width:] = second.astype(BF)
+            else:
+                outs[d][...] = first.astype(BF)
+                outs[size + d][...] = second.astype(BF)
+        sums_ref[...] = jnp.sum(gpre_ref[...].astype(F32), 0, keepdims=True)
+
+    outs = [((up, 2 * width), BF)] * size if joined else [((down, width), BF)] * size + [((up, ff), BF)] * size
+    scratch = [] if direct else [pltpu.VMEM((ff, width), F32), pltpu.VMEM((width, ff), F32)]
+    *pieces, sums = call(body, (place, grads, saved, gpre), outs + [((1, ff), F32)], "mlp_weights", 1, after, scratch, 20)
+    return [pieces[i:i + size] for i in range(0, len(pieces), size)], sums
+
+
+def fold_first(own, came, after):
+    def body(own_ref, *refs):
+        total = own_ref[...].astype(F32)
+        for ref in refs[:-1]:
+            total = total + ref[...].astype(F32)
+        refs[-1][...] = total.astype(BF)
+
+    return call(body, (own, *came), [(own.shape, BF)], "fold_first", 0, after)[0]
 
 
 def out_back(place, terms, res_and_grad, vectors, ctx_cat, halves, after):
@@ -660,7 +690,7 @@
     def body(place_ref, *refs):
         dq_ref, w_ref, gj_ref, gn1_ref = refs[size:size + 4]
         out_refs = refs[size + 4:]
-        dkv = refs[0][...]
+        dkv = refs[0][...].astype(F32)
         for ref in refs[1:size]:
             dkv = dkv + ref[...].astype(F32)
         gj_ref[:, 0:2 * group] = dkv.astype(BF)
@@ -674,9 +704,9 @@
     return call(body, (place, *terms, dq, one), outs, "join_back", 1)
 
 
-def weights_back(place, n1, grad_joined, gn1, hidden, out_sums, fin_sums, up_rows, gw_out, wr, devices):
+def weights_back(place, saved, grad_joined, gn1, out_sums, fin_sums, up_rows, gw_out, wr, devices):
     total, cols = grad_joined.shape
-    width = n1.shape[1]
+    width = gn1.shape[1]
     rows = total // ZS
     group = cols // 3
     upc = up_rows.shape[0]
@@ -684,11 +714,11 @@
     wide = width + cols + HEAD_DIM + LANES
     slots = -(-devices // wr)
 
-    def body(place_ref, n1_ref, gj_ref, gn1_ref, hidden_ref, sums_ref, fin_ref, up_ref, gw_ref, kept_ref, sent_ref, vec, full):
+    def body(place_ref, saved_ref, gj_ref, gn1_ref, sums_ref, fin_ref, up_ref, gw_ref, kept_ref, sent_ref, vec, full):
         gain_sum = jnp.zeros((1, width), F32)
         for z in range(ZS):
             spot = slice(z * rows, (z + 1) * rows)
-            normed, _ = norm_parts(hidden_ref[spot, :].astype(F32))
+            normed, _ = norm_parts(saved_ref[spot, width:].astype(F32))
             gain_sum = gain_sum + jnp.sum(gn1_ref[spot, :] * normed, 0, keepdims=True)
         joined_sums = jnp.sum(gj_ref[...].astype(F32), 0, keepdims=True)
         vec[...] = jnp.zeros_like(vec)
@@ -712,7 +742,7 @@
             vec[16 + s:17 + s, :] = jnp.where(turn + s * wr == place_ref[2], high, 0.0)
         vec[16 + slots:17 + slots, :] = jnp.where(turn == 0, error - high, 0.0)
         full[:, 0:width] = gw_ref[...].astype(F32)
-        full[:, width:width + cols] = dot_tn(n1_ref[...], gj_ref[...])
+        full[:, width:width + cols] = dot_tn(saved_ref[:, 0:width], gj_ref[...])
         full[:, width + cols:width + cols + hd] = jnp.zeros((width, hd), F32)
         full[:, width + cols + hd:] = vec[...].T
         for c in range(2):
@@ -725,7 +755,7 @@
 
     outs = [((chips, wr, wide), BF)] * 2
     scratch = [pltpu.VMEM((LANES, width), F32), pltpu.VMEM((width, wide), F32)]
-    return call(body, (place, n1, grad_joined, gn1, hidden, out_sums, fin_sums, up_rows, gw_out), outs, "weights_back", 1, scratch=scratch, mib=20)
+    return call(body, (place, saved, grad_joined, gn1, out_sums, fin_sums, up_rows, gw_out), outs, "weights_back", 1, scratch=scratch, mib=20)
 
 
 def input_back(terms, hidden, vectors, grad_res):
@@ -781,6 +811,7 @@
     group = width // sz
     place = iz.astype(jnp.int32).reshape(1)
     at_zc = jnp.stack([iz, core]).astype(jnp.int32)
+    yplace = iy.astype(jnp.int32).reshape(1)
 
     def from_z(value):
         return [value] + [shift(value, "z", d) for d in range(1, sz)]
@@ -795,7 +826,7 @@
     hidden = hidden_in[0]
     pieces = from_z(hidden)
     targets = jnp.concatenate([teacher, cotangent], 0)
-    one = arrange(to_z(cut_z(pack_one(w_qkv, flat, segment_ids, padding_mask))), iz, 0)
+    one = arrange(to_z(cut_z(pack_one(w_qkv, flat, jnp.concatenate([segment_ids, padding_mask])))), iz, 0)
     one = gather(one[None, :, None], "x", 2, after=[pieces[1]])
     one = gather(one, "y", 0, after=pieces[2:])[:, :, :, None]
     one = gather(one, "core", 3).reshape(width, -1)
@@ -823,7 +854,7 @@
     spots = spots + [(at, 1 - core) for at, _ in spots]
     order = jnp.stack([at * 2 + c for at, c in spots] + [iz]).astype(jnp.int32)
 
-    n1_low, q, kv, hidden_all = project(place, pieces, one, vectors)
+    kv, q, saved_one = project(place, pieces, one, vectors)
     kvs = spread_tokens(kv)
     *ctx_parts, ctx_tot = attend(order, q, seg, kvs, after=[biases])
     ctx_cat = beside(to_z(ctx_parts))
@@ -835,18 +866,19 @@
 
     kept, sent, grad_pre, grads = mlp_back(spread_tokens(grad_mlp), weights, slope)
     gn2_terms = fold_tokens(kept, sent)
-    gw_mlp, up_sums = mlp_weights(grads, saved, grad_pre, after=gn2_terms[:1])
-    gw_sums = [lax.psum_scatter(member, ("y", "z"), scatter_dimension=0, tiled=True) for member in gw_mlp]
+    gw_mlp, up_sums = mlp_weights(yplace, grads, saved, grad_pre, sy, after=gn2_terms[:1])
+    gw_came = [passed(members, "y") for members in gw_mlp]
     grad_res, *gctx, gw_out, out_sums = out_back(at_zc, gn2_terms, res_and_grad, vectors, ctx_cat, wo, after=[up_sums])
-    dq, dkv_kept, dkv_sent = attend_back(order, q, to_z(gctx), ctx_tot, seg, kvs)
-    grad_joined, gn1, *gn1_parts = join_back(place, fold_tokens(dkv_kept, dkv_sent), dq, one)
+    dq, dkv_kept, dkv_sent, done = attend_back(order, q, to_z(gctx), ctx_tot, seg, kvs)
+    gw_sums = [lax.psum_scatter(fold_first(members[0], came, [done]), "z", scatter_dimension=0, tiled=True) for members, came in zip(gw_mlp, gw_came)]
+    grad_joined, gn1, *gn1_parts = join_back(place, fold_tokens(dkv_kept, dkv_sent, BF), dq, one)
     gn1_parts = to_z(gn1_parts)
     input_grad = input_back(gn1_parts, hidden, vectors, grad_res)
 
     up_rows = jnp.zeros((upc, sy * sz, sx * 2, wr), F32)
     up_rows = lax.dynamic_update_slice_in_dim(up_rows, up_sums.reshape(sy * sz, upc, wr).transpose(1, 0, 2)[:, :, None], ix * 2 + core, 2).reshape(upc, width)
     places = jnp.stack([iz, core, device]).astype(jnp.int32)
-    kept, sent = weights_back(places, n1_low, grad_joined, gn1, hidden_all, out_sums, fin_sums, up_rows, gw_out, wr, devices)
+    kept, sent = weights_back(places, saved_one, grad_joined, gn1, out_sums, fin_sums, up_rows, gw_out, wr, devices)
     third = fold_both(kept.reshape(sy, sz, sx, wr, -1), shift(sent, "core", 1).reshape(sy, sz, sx, wr, -1), ix, iy, width)
     third = fold_cross(third[:sx], passed(third[:sx], "x"), third[sx:], passed(third[sx:], "y"), ix, iy)
     third = fold_last(third[:sy], passed(third[:sy], "y"), third[sy:], passed(third[sy:], "x"), iz, after=[gn1_parts[2], gn1_parts[3]])

time: 256 us -> 244 us (0.953)
  starting transfers between devices: 58.8 us -> 52.9 us
  local copies, waits for them, and re-layouts: 34.8 us -> 29.5 us
  Pallas kernels: 34.4 us -> 38.6 us
  waiting for transfers between devices: 106 us -> 102 us
    unnamed x135 -> x153, local copies, waits for them, and re-layouts: 29.6 us -> 22.7 us
    ppermute x44 -> x45, starting transfers between devices: 55.5 us -> 49.6 us  [shift(): lax.ppermute(value, axis, [(a, (a + step) % size) for a in range(size)])]
    pallas_call x25 -> x26, Pallas kernels: 34.2 us -> 38.4 us  [call(): pl.pallas_call(whole, in_specs=specs + [pl.BlockSpec(memory_space=pl.ANY)...]
    ppermute x44 -> x45, waiting for transfers between devices: 98.8 us -> 94.8 us  [shift(): lax.ppermute(value, axis, [(a, (a + step) % size) for a in range(size)])]
  transfers between devices with their start and end apart: 49 -> 50, of which waited for: 32 -> 35; matrix products, arithmetic and copies ran while one was open for 2% -> 3% of each run, Pallas kernels for 8% -> 10%
where the time goes in v3:
time: 244 us
  waiting for transfers between devices  102 us (42%)
  starting transfers between devices  52.9 us (22%)
  Pallas kernels  38.6 us (16%)
  local copies, waits for them, and re-layouts  29.5 us (12%)
  between operations  17.5 us (7%)
  other arithmetic  3.24 us (1%)
    ppermute x45, waiting for transfers between devices, shift(): lax.ppermute(value, axis, [(a, (a + step) % size) for a in range(size)])  94.8 us
    ppermute x45, starting transfers between devices, shift(): lax.ppermute(value, axis, [(a, (a + step) % size) for a in range(size)])  49.6 us
    pallas_call x26, Pallas kernels, call(): pl.pallas_call(whole, in_specs=specs + [pl.BlockSpec(memory_space=pl.ANY)...  38.4 us
    unnamed x153, local copies, waits for them, and re-layouts  22.7 us
  transfers between devices with their start and end apart: 50, of which 35 were waited for; matrix products, arithmetic and copies ran while one was open for 3% of the time, Pallas kernels for 10%

profile of v3, /device:TPU:0, one launch (start us, length us, event | category | flops | bytes accessed | tf_op | source)
XLA Modules:
  0.0 243.8 jit_solution(5621529257620696623)
XLA Ops:
  9.8 3.0 %collective-permute-start.15 = (bf16[24,1152]{1,0:T(8,128)(2,1)S(1)}, bf16[24,1152]{1,0:T(8,128)(2,1)S(1)}, u32[]{:S(2)}, u32[]{:S(2)}) collective-permute-start(bf16[24,1152]{1,0:T(8,128)(2,1)S(1)} %get-tuple-element.92), channel_id=1, source_target_pairs={{0,2},{1,3},{2,0},{3,1},{4,6},{5,7},{6,4},{7,5},{8,10},{9,11},{10,... | collective-permute-start | bytes 165896 | tf_op jit(solution)/shard_map/ppermute | solution.py:839
  13.0 1.9 collective-permute-done.15.refs_2_
  18.7 1.6 collective-permute-start.4
  20.8 1.6 collective-permute-start
  23.6 2.7 %collective-permute-start.2 = (bf16[1,24,704]{2,1,0:T(8,128)(2,1)S(1)}, bf16[1,24,704]{2,1,0:T(8,128)(2,1)S(1)}, u32[]{:S(2)}, u32[]{:S(2)}) collective-permute-start(bf16[1,24,704]{2,1,0:T(8,128)(2,1)S(1)} %get-tuple-element.168), channel_id=1, source_target_pairs={{0,12},{4,0},{8,4},{12,8},{1,13},{5,1},{9,5},{13,9},{2,14},{6,2},{... | collective-permute-start | bytes 101384 | tf_op jit(solution)/shard_map/ppermute | solution.py:22
  26.3 2.8 %collective-permute-done.refs_1_ = bf16[1,24,704]{2,1,0:T(8,128)(2,1)S(1)} collective-permute-done((bf16[1,24,704]{2,1,0:T(8,128)(2,1)S(1)}, bf16[1,24,704]{2,1,0:T(8,128)(2,1)S(1)}, u32[]{:S(2)}, u32[]{:S(2)}) %collective-permute-start) | collective-permute-done | bytes 33824 | tf_op jit(solution)/shard_map/ppermute | solution.py:22
  31.6 4.6 %collective-permute-done.3.refs_1_ = bf16[1,4,1,24,704]{4,3,2,1,0:T(8,128)(2,1)S(1)} collective-permute-done((bf16[1,4,1,24,704]{4,3,2,1,0:T(8,128)(2,1)S(1)}, bf16[1,4,1,24,704]{4,3,2,1,0:T(8,128)(2,1)S(1)}, u32[]{:S(2)}, u32[]{:S(2)}) %collective-permute-start.3) | collective-permute-done | bytes 135200 | tf_op jit(solution)/shard_map/ppermute | solution.py:22
  36.2 1.6 collective-permute-start.5
  38.3 3.4 %collective-permute-start.7 = (bf16[128,768]{1,0:T(8,128)(2,1)S(1)}, bf16[128,768]{1,0:T(8,128)(2,1)S(1)}, u32[]{:S(2)}, u32[]{:S(2)}) collective-permute-start(bf16[128,768]{1,0:T(8,128)(2,1)S(1)} %bitcast.58), channel_id=1, source_target_pairs={{0,12},{4,0},{8,4},{12,8},{1,13},{5,1},{9,5},{13,9},{2,14},{6,2},{... | collective-permute-start | bytes 589832 | tf_op jit(solution)/shard_map/ppermute | solution.py:22
  41.6 11.0 %collective-permute-done.6.refs_2_.refs_3_ = bf16[128,768]{1,0:T(8,128)(2,1)S(1)} collective-permute-done((bf16[128,768]{1,0:T(8,128)(2,1)S(1)}, bf16[128,768]{1,0:T(8,128)(2,1)S(1)}, u32[]{:S(2)}, u32[]{:S(2)}) %collective-permute-start.6) | collective-permute-done | bytes 196640 | tf_op jit(solution)/shard_map/ppermute | solution.py:22
  52.8 2.0 collective-permute-done.8.refs_1_
  59.5 9.1 %collective-permute-done.9.refs_4_.refs_9_ = bf16[512,384]{1,0:T(8,128)(2,1)S(1)} collective-permute-done((bf16[512,384]{1,0:T(8,128)(2,1)S(1)}, bf16[512,384]{1,0:T(8,128)(2,1)S(1)}, u32[]{:S(2)}, u32[]{:S(2)}) %collective-permute-start.9) | collective-permute-done | bytes 393248 | tf_op jit(solution)/shard_map/ppermute | solution.py:22
  70.4 4.3 %attend.1 = (bf16[128,192]{1,0:T(8,128)(2,1)S(1)}, bf16[128,192]{1,0:T(8,128)(2,1)S(1)}, bf16[128,192]{1,0:T(8,128)(2,1)S(1)}, bf16[128,192]{1,0:T(8,128)(2,1)S(1)}, f32[2,512,256]{2,1,0:T(8,128)S(1)}) custom-call(s32[5]{0:T(128)S(1)} %stack.79.refs_0_, bf16[512,256]{1,0:T(8,128)(2,1)S(1)} %get-tuple-element.85.refs_1_, ...), custom_call_target="tpu_custom_call" | custom-call | flops 1 | bytes 1 | tf_op jit(solution)/shard_map/attend/pallas_call | solution.py:417
  75.9 4.5 %collective-permute-start.12 = (bf16[128,192]{1,0:T(8,128)(2,1)S(1)}, bf16[128,192]{1,0:T(8,128)(2,1)S(1)}, u32[]{:S(2)}, u32[]{:S(2)}) collective-permute-start(bf16[128,192]{1,0:T(8,128)(2,1)S(1)} %get-tuple-element.88), channel_id=1, source_target_pairs={{0,4},{4,8},{8,12},{12,0},{1,5},{5,9},{9,13},{13,1},{2,6},{6,10},{... | collective-permute-start | bytes 147464 | tf_op jit(solution)/shard_map/ppermute | solution.py:22
  82.7 2.2 collective-permute-done.12.refs_1_
  84.9 5.1 %collective-permute-done.13.refs_2_ = bf16[128,192]{1,0:T(8,128)(2,1)S(1)} collective-permute-done((bf16[128,192]{1,0:T(8,128)(2,1)S(1)}, bf16[128,192]{1,0:T(8,128)(2,1)S(1)}, u32[]{:S(2)}, u32[]{:S(2)}) %collective-permute-start.13) | collective-permute-done | bytes 49184 | tf_op jit(solution)/shard_map/ppermute | solution.py:22
  90.9 3.8 %all-gather.2.cloned.1.call-done.refs_0_.refs_5_.refs_6_ = bf16[768,1920]{1,0:T(8,128)(2,1)} async-done(((bf16[96,1920]{1,0:T(8,128)(2,1)}), bf16[768,1920]{1,0:T(8,128)(2,1)}) %all-gather.2.cloned.1.call-update) | async-done | bytes 2949136 | tf_op jit(solution)/shard_map/all_gather | solution.py:843
  94.7 1.8 copy-done
  97.7 1.9 collective-permute-done.18.refs_3_.refs_7_
  103.2 5.5 %collective-permute-done.19.refs_1_ = bf16[128,768]{1,0:T(8,128)(2,1)S(1)} collective-permute-done((bf16[128,768]{1,0:T(8,128)(2,1)S(1)}, bf16[128,768]{1,0:T(8,128)(2,1)S(1)}, u32[]{:S(2)}, u32[]{:S(2)}) %collective-permute-start.19) | collective-permute-done | bytes 196640 | tf_op jit(solution)/shard_map/ppermute | solution.py:22
  110.1 2.3 mlp_up.1
  114.5 1.6 collective-permute-done.22.refs_1_
  120.6 4.3 %collective-permute-done.23.refs_2_ = bf16[128,768]{1,0:T(8,128)(2,1)} collective-permute-done((bf16[128,768]{1,0:T(8,128)(2,1)}, bf16[128,768]{1,0:T(8,128)(2,1)}, u32[]{:S(2)}, u32[]{:S(2)}) %collective-permute-start.23) | collective-permute-done | bytes 196640 | tf_op jit(solution)/shard_map/ppermute | solution.py:22
  127.9 2.0 finish.1
  131.4 4.6 %collective-permute-done.24.refs_1_ = bf16[128,768]{1,0:T(8,128)(2,1)S(1)} collective-permute-done((bf16[128,768]{1,0:T(8,128)(2,1)S(1)}, bf16[128,768]{1,0:T(8,128)(2,1)S(1)}, u32[]{:S(2)}, u32[]{:S(2)}) %collective-permute-start.24) | collective-permute-done | bytes 196640 | tf_op jit(solution)/shard_map/ppermute | solution.py:22
  137.4 2.8 %mlp_back.1 = (f32[2,128,768]{2,1,0:T(8,128)S(1)}, bf16[2,128,768]{2,1,0:T(8,128)(2,1)S(1)}, bf16[512,768]{1,0:T(8,128)(2,1)S(1)}, bf16[512,768]{1,0:T(8,128)(2,1)S(1)}) custom-call(bf16[128,768]{1,0:T(8,128)(2,1)S(1)} %get-tuple-element.103.refs_0_, bf16[128,768]{1,0:T(8,128)(2,1)S(1)} %collective-permute-done.24.refs_1_, ...), custom_call_target="tpu_custom_call" | custom-call | flops 1 | bytes 1 | tf_op jit(solution)/shard_map/mlp_back/pallas_call | solution.py:417
  140.5 1.6 collective-permute-done.27.refs_1_
  144.3 1.6 collective-permute-start.28
  145.9 5.1 %collective-permute-done.28.refs_2_ = bf16[128,768]{1,0:T(8,128)(2,1)S(1)} collective-permute-done((bf16[128,768]{1,0:T(8,128)(2,1)S(1)}, bf16[128,768]{1,0:T(8,128)(2,1)S(1)}, u32[]{:S(2)}, u32[]{:S(2)}) %collective-permute-start.28) | collective-permute-done | bytes 196640 | tf_op jit(solution)/shard_map/ppermute | solution.py:22
  151.1 1.8 out_back.1
  156.8 1.7 collective-permute-start.31
  158.5 2.5 %collective-permute-done.29.refs_3_ = bf16[128,192]{1,0:T(8,128)(2,1)S(1)} collective-permute-done((bf16[128,192]{1,0:T(8,128)(2,1)S(1)}, bf16[128,192]{1,0:T(8,128)(2,1)S(1)}, u32[]{:S(2)}, u32[]{:S(2)}) %collective-permute-start.29) | collective-permute-done | bytes 49184 | tf_op jit(solution)/shard_map/ppermute | solution.py:22
  161.0 1.6 collective-permute-done.30.refs_4_
  162.7 7.4 %attend_back.1 = (bf16[512,192]{1,0:T(8,128)(2,1)S(1)}, f32[2,512,384]{2,1,0:T(8,128)S(1)}, bf16[2,512,384]{2,1,0:T(8,128)(2,1)}, f32[8,128]{1,0:T(8,128)S(1)}) custom-call(s32[5]{0:T(128)S(1)} %copy-done.58, bf16[512,256]{1,0:T(8,128)(2,1)S(1)} %copy-done.35, bf16[128,192]{1,0:T(8,128)(2,1)S(1)} %get-tuple-element.114.refs_2_, ...), custom_call_target="tpu_custom_call" | custom-call | flops 1 | bytes 1 | tf_op jit(solution)/shard_map/attend_back/pallas_call | solution.py:417
  170.1 1.7 collective-permute-done.44.refs_1_
  178.4 1.7 dynamic_update_slice.3
  181.0 6.0 %collective-permute-done.33.refs_2_ = bf16[512,384]{1,0:T(8,128)(2,1)} collective-permute-done((bf16[512,384]{1,0:T(8,128)(2,1)}, bf16[512,384]{1,0:T(8,128)(2,1)}, u32[]{:S(2)}, u32[]{:S(2)}) %collective-permute-start.33) | collective-permute-done | bytes 393248 | tf_op jit(solution)/shard_map/ppermute | solution.py:22
  187.0 2.7 %join_back.1 = (bf16[512,576]{1,0:T(8,128)(2,1)S(1)}, f32[512,768]{1,0:T(8,128)S(1)}, f32[128,768]{1,0:T(8,128)S(1)}, bf16[128,768]{1,0:T(8,128)(2,1)S(1)}, bf16...) custom-call(s32[1]{0:T(128)} %bitcast.3.place_ref.refs_0_, bf16[512,384]{1,0:T(8,128)(2,1)S(1)} %get-tuple-element.121.refs_1_, ...), custom_call_target="tpu_custom_call" | custom-call | flops 1 | bytes 1 | tf_op jit(solution)/shard_map/join_back/pallas_call | solution.py:417
  192.4 2.2 weights_back.1
  194.8 2.8 %collective-permute-done.34 = bf16[16,24,1536]{2,1,0:T(8,128)(2,1)S(1)} collective-permute-done((bf16[16,24,1536]{2,1,0:T(8,128)(2,1)S(1)}, bf16[16,24,1536]{2,1,0:T(8,128)(2,1)S(1)}, u32[]{:S(2)}, u32[]{:S(2)}) %collective-permute-start.34) | collective-permute-done | bytes 1179680 | tf_op jit(solution)/shard_map/ppermute | solution.py:22
  198.4 1.6 collective-permute-start.35
  201.7 3.2 %collective-permute-start.40 = (bf16[128,768]{1,0:T(8,128)(2,1)}, bf16[128,768]{1,0:T(8,128)(2,1)S(1)}, u32[]{:S(2)}, u32[]{:S(2)}) collective-permute-start(bf16[128,768]{1,0:T(8,128)(2,1)} %get-tuple-element.140), channel_id=1, source_target_pairs={{0,12},{4,0},{8,4},{12,8},{1,13},{5,1},{9,5},{13,9},{2,14},{6,2},{... | collective-permute-start | bytes 589832 | tf_op jit(solution)/shard_map/ppermute | solution.py:22
  204.9 2.6 %collective-permute-done.35.refs_2_ = bf16[2,4,1,24,768]{4,3,2,1,0:T(8,128)(2,1)S(1)} collective-permute-done((bf16[2,4,1,24,768]{4,3,2,1,0:T(8,128)(2,1)S(1)}, bf16[2,4,1,24,768]{4,3,2,1,0:T(8,128)(2,1)S(1)}, u32[]{:S(2)}, u32[]{:S(2)}) %collective-permute-start.35) | collective-permute-done | bytes 294944 | tf_op jit(solution)/shard_map/ppermute | solution.py:22
  211.3 2.5 %collective-permute-done.39.refs_5_.refs_2_ = bf16[128,768]{1,0:T(8,128)(2,1)S(1)} collective-permute-done((bf16[128,768]{1,0:T(8,128)(2,1)}, bf16[128,768]{1,0:T(8,128)(2,1)S(1)}, u32[]{:S(2)}, u32[]{:S(2)}) %collective-permute-start.39) | collective-permute-done | bytes 196640 | tf_op jit(solution)/shard_map/ppermute | solution.py:22
  218.5 1.8 collective-permute-start.47
  220.3 2.0 collective-permute-done.45.refs_1_
  222.4 1.9 collective-permute-start.41
  229.4 2.7 %collective-permute-done.42.refs_3_ = bf16[1,1,1,24,1536]{4,3,2,1,0:T(8,128)(2,1)S(1)} collective-permute-done((bf16[1,1,1,24,1536]{4,3,2,1,0:T(8,128)(2,1)S(1)}, bf16[1,1,1,24,1536]{4,3,2,1,0:T(8,128)(2,1)S(1)}, u32[]{:S(2)}, u32[]{:S(2)}) %collective-permute-start.42) | collective-permute-done | bytes 73760 | tf_op jit(solution)/shard_map/ppermute | solution.py:22
  (282 shorter events, 75.5 us)
Async XLA Ops:
  7.2 87.5 %all-gather.2.cloned.1.call-start = ((), (), s32[]{:S(2)}) async-start(), calls=%async_computation.1 | async-start | bytes 3317760 | tf_op jit(solution)/shard_map/all_gather | solution.py:843
  9.8 5.1 %collective-permute-start.15 = (bf16[24,1152]{1,0:T(8,128)(2,1)S(1)}, bf16[24,1152]{1,0:T(8,128)(2,1)S(1)}, u32[]{:S(2)}, u32[]{:S(2)}) collective-permute-start(bf16[24,1152]{1,0:T(8,128)(2,1)S(1)} %get-tuple-element.92), channel_id=1, source_target_pairs={{0,2},{1,3},{2,0},{3,1},{4,6},{5,7},{6,4},{7,5},{8,10},{9,11},{10,... | collective-permute-start | bytes 165896 | tf_op jit(solution)/shard_map/ppermute | solution.py:839
  12.8 2.1 collective-permute-start.16
  12.8 3.6 %collective-permute-start.17 = (bf16[24,1152]{1,0:T(8,128)(2,1)S(1)}, bf16[24,1152]{1,0:T(8,128)(2,1)S(1)}, u32[]{:S(2)}, u32[]{:S(2)}) collective-permute-start(bf16[24,1152]{1,0:T(8,128)(2,1)S(1)} %get-tuple-element.94), channel_id=1, source_target_pairs={{0,3},{1,2},{2,1},{3,0},{4,7},{5,6},{6,5},{7,4},{8,11},{9,10},{10,... | collective-permute-start | bytes 165896 | tf_op jit(solution)/shard_map/ppermute | solution.py:839
  18.6 197.4 %reduce-scatter.2.cloned.1.call-start = ((), (), s32[]{:S(2)}) async-start(), calls=%async_computation.2 | async-start | bytes 1474560 | tf_op jit(solution)/shard_map/reduce_scatter | solution.py:873
  18.7 17.5 %collective-permute-start.4 = (bf16[128,768]{1,0:T(8,128)(2,1)S(1)}, bf16[128,768]{1,0:T(8,128)(2,1)S(1)}, u32[]{:S(2)}, u32[]{:S(2)}) collective-permute-start(bf16[128,768]{1,0:T(8,128)(2,1)S(1)} %bitcast.56), channel_id=1, source_target_pairs={{0,4},{4,8},{8,12},{12,0},{1,5},{5,9},{9,13},{13,1},{2,6},{6,10},{... | collective-permute-start | bytes 589832 | tf_op jit(solution)/shard_map/ppermute | solution.py:22
  20.8 8.4 %collective-permute-start = (bf16[1,24,704]{2,1,0:T(8,128)(2,1)S(1)}, bf16[1,24,704]{2,1,0:T(8,128)(2,1)S(1)}, u32[]{:S(2)}, u32[]{:S(2)}) collective-permute-start(bf16[1,24,704]{2,1,0:T(8,128)(2,1)S(1)} %get-tuple-element.170), channel_id=1, source_target_pairs={{0,4},{4,8},{8,12},{12,0},{1,5},{5,9},{9,13},{13,1},{2,6},{6,10},{... | collective-permute-start | bytes 101384 | tf_op jit(solution)/shard_map/ppermute | solution.py:22
  22.4 8.0 %collective-permute-start.1 = (bf16[1,24,704]{2,1,0:T(8,128)(2,1)S(1)}, bf16[1,24,704]{2,1,0:T(8,128)(2,1)S(1)}, u32[]{:S(2)}, u32[]{:S(2)}) collective-permute-start(bf16[1,24,704]{2,1,0:T(8,128)(2,1)S(1)} %get-tuple-element.169), channel_id=1, source_target_pairs={{0,8},{4,12},{8,0},{12,4},{1,9},{5,13},{9,1},{13,5},{2,10},{6,14},... | collective-permute-start | bytes 101384 | tf_op jit(solution)/shard_map/ppermute | solution.py:22
  23.6 6.8 %collective-permute-start.2 = (bf16[1,24,704]{2,1,0:T(8,128)(2,1)S(1)}, bf16[1,24,704]{2,1,0:T(8,128)(2,1)S(1)}, u32[]{:S(2)}, u32[]{:S(2)}) collective-permute-start(bf16[1,24,704]{2,1,0:T(8,128)(2,1)S(1)} %get-tuple-element.168), channel_id=1, source_target_pairs={{0,12},{4,0},{8,4},{12,8},{1,13},{5,1},{9,5},{13,9},{2,14},{6,2},{... | collective-permute-start | bytes 101384 | tf_op jit(solution)/shard_map/ppermute | solution.py:22
  30.5 5.8 %collective-permute-start.3 = (bf16[1,4,1,24,704]{4,3,2,1,0:T(8,128)(2,1)S(1)}, bf16[1,4,1,24,704]{4,3,2,1,0:T(8,128)(2,1)S(1)}, u32[]{:S(2)}, u32[]{:S(2)}) collective-permute-start(bf16[1,4,1,24,704]{4,3,2,1,0:T(8,128)(2,1)S(1)} %bitcast.67), channel_id=1, source_target_pairs={{0,2},{2,0},{1,3},{3,1},{4,6},{6,4},{5,7},{7,5},{8,10},{10,8},{9,1... | collective-permute-start | bytes 405512 | tf_op jit(solution)/shard_map/ppermute | solution.py:22
  36.2 16.4 %collective-permute-start.5 = (bf16[1,4,2,24,704]{4,3,2,1,0:T(8,128)(2,1)S(1)}, bf16[1,4,2,24,704]{4,3,2,1,0:T(8,128)(2,1)S(1)}, u32[]{:S(2)}, u32[]{:S(2)}) collective-permute-start(bf16[1,4,2,24,704]{4,3,2,1,0:T(8,128)(2,1)S(1)} %arrange.7.refs_0_), channel_id=1, source_target_pairs={{0,16},{16,0},{1,17},{17,1},{2,18},{18,2},{3,19},{19,3},{4,20},{20... | collective-permute-start | bytes 811016 | tf_op jit(solution)/shard_map/ppermute | solution.py:22
  37.8 14.8 %collective-permute-start.6 = (bf16[128,768]{1,0:T(8,128)(2,1)S(1)}, bf16[128,768]{1,0:T(8,128)(2,1)S(1)}, u32[]{:S(2)}, u32[]{:S(2)}) collective-permute-start(bf16[128,768]{1,0:T(8,128)(2,1)S(1)} %bitcast.57), channel_id=1, source_target_pairs={{0,8},{4,12},{8,0},{12,4},{1,9},{5,13},{9,1},{13,5},{2,10},{6,14},... | collective-permute-start | bytes 589832 | tf_op jit(solution)/shard_map/ppermute | solution.py:22
  38.3 14.3 %collective-permute-start.7 = (bf16[128,768]{1,0:T(8,128)(2,1)S(1)}, bf16[128,768]{1,0:T(8,128)(2,1)S(1)}, u32[]{:S(2)}, u32[]{:S(2)}) collective-permute-start(bf16[128,768]{1,0:T(8,128)(2,1)S(1)} %bitcast.58), channel_id=1, source_target_pairs={{0,12},{4,0},{8,4},{12,8},{1,13},{5,1},{9,5},{13,9},{2,14},{6,2},{... | collective-permute-start | bytes 589832 | tf_op jit(solution)/shard_map/ppermute | solution.py:22
  52.7 2.1 collective-permute-start.8
  57.5 11.2 %collective-permute-start.9 = (bf16[512,384]{1,0:T(8,128)(2,1)S(1)}, bf16[512,384]{1,0:T(8,128)(2,1)S(1)}, u32[]{:S(2)}, u32[]{:S(2)}) collective-permute-start(bf16[512,384]{1,0:T(8,128)(2,1)S(1)} %get-tuple-element.86.refs_3_.refs_8_), channel_id=1, source_target_pairs={{0,2},{2,0},{1,3},{3,1},{4,6},{6,4},{5,7},{7,5},{8,10},{10,8},{9,1... | collective-permute-start | bytes 1179656 | tf_op jit(solution)/shard_map/ppermute | solution.py:22
  59.1 10.4 %collective-permute-start.10 = (bf16[512,384]{1,0:T(8,128)(2,1)S(1)}, bf16[512,384]{1,0:T(8,128)(2,1)S(1)}, u32[]{:S(2)}, u32[]{:S(2)}) collective-permute-start(bf16[512,384]{1,0:T(8,128)(2,1)S(1)} %get-tuple-element.86.refs_3_.refs_8_), channel_id=1, source_target_pairs={{0,1},{1,0},{2,3},{3,2},{4,5},{5,4},{6,7},{7,6},{8,9},{9,8},{10,11... | collective-permute-start | bytes 1179656 | tf_op jit(solution)/shard_map/ppermute | solution.py:22
  68.7 1.7 collective-permute-start.11
  75.9 9.0 %collective-permute-start.12 = (bf16[128,192]{1,0:T(8,128)(2,1)S(1)}, bf16[128,192]{1,0:T(8,128)(2,1)S(1)}, u32[]{:S(2)}, u32[]{:S(2)}) collective-permute-start(bf16[128,192]{1,0:T(8,128)(2,1)S(1)} %get-tuple-element.88), channel_id=1, source_target_pairs={{0,4},{4,8},{8,12},{12,0},{1,5},{5,9},{9,13},{13,1},{2,6},{6,10},{... | collective-permute-start | bytes 147464 | tf_op jit(solution)/shard_map/ppermute | solution.py:22
  80.3 9.7 %collective-permute-start.13 = (bf16[128,192]{1,0:T(8,128)(2,1)S(1)}, bf16[128,192]{1,0:T(8,128)(2,1)S(1)}, u32[]{:S(2)}, u32[]{:S(2)}) collective-permute-start(bf16[128,192]{1,0:T(8,128)(2,1)S(1)} %get-tuple-element.89), channel_id=1, source_target_pairs={{0,8},{4,12},{8,0},{12,4},{1,9},{5,13},{9,1},{13,5},{2,10},{6,14},... | collective-permute-start | bytes 147464 | tf_op jit(solution)/shard_map/ppermute | solution.py:22
  81.3 8.7 %collective-permute-start.14 = (bf16[128,192]{1,0:T(8,128)(2,1)S(1)}, bf16[128,192]{1,0:T(8,128)(2,1)S(1)}, u32[]{:S(2)}, u32[]{:S(2)}) collective-permute-start(bf16[128,192]{1,0:T(8,128)(2,1)S(1)} %get-tuple-element.90), channel_id=1, source_target_pairs={{0,12},{4,0},{8,4},{12,8},{1,13},{5,1},{9,5},{13,9},{2,14},{6,2},{... | collective-permute-start | bytes 147464 | tf_op jit(solution)/shard_map/ppermute | solution.py:22
  97.5 2.1 collective-permute-start.18
  101.7 6.9 %collective-permute-start.19 = (bf16[128,768]{1,0:T(8,128)(2,1)S(1)}, bf16[128,768]{1,0:T(8,128)(2,1)S(1)}, u32[]{:S(2)}, u32[]{:S(2)}) collective-permute-start(bf16[128,768]{1,0:T(8,128)(2,1)S(1)} %get-tuple-element.95.refs_0_), channel_id=1, source_target_pairs={{0,2},{2,0},{1,3},{3,1},{4,6},{6,4},{5,7},{7,5},{8,10},{10,8},{9,1... | collective-permute-start | bytes 589832 | tf_op jit(solution)/shard_map/ppermute | solution.py:22
  103.2 5.5 %collective-permute-start.20 = (bf16[128,768]{1,0:T(8,128)(2,1)S(1)}, bf16[128,768]{1,0:T(8,128)(2,1)S(1)}, u32[]{:S(2)}, u32[]{:S(2)}) collective-permute-start(bf16[128,768]{1,0:T(8,128)(2,1)S(1)} %get-tuple-element.95.refs_0_), channel_id=1, source_target_pairs={{0,1},{1,0},{2,3},{3,2},{4,5},{5,4},{6,7},{7,6},{8,9},{9,8},{10,11... | collective-permute-start | bytes 589832 | tf_op jit(solution)/shard_map/ppermute | solution.py:22
  114.4 1.7 collective-permute-start.22
  117.6 7.3 %collective-permute-start.23 = (bf16[128,768]{1,0:T(8,128)(2,1)}, bf16[128,768]{1,0:T(8,128)(2,1)}, u32[]{:S(2)}, u32[]{:S(2)}) collective-permute-start(bf16[128,768]{1,0:T(8,128)(2,1)} %get-tuple-element.99), channel_id=1, source_target_pairs={{0,2},{2,0},{1,3},{3,1},{4,6},{6,4},{5,7},{7,5},{8,10},{10,8},{9,1... | collective-permute-start | bytes 589832 | tf_op jit(solution)/shard_map/ppermute | solution.py:22
  129.9 6.1 %collective-permute-start.24 = (bf16[128,768]{1,0:T(8,128)(2,1)S(1)}, bf16[128,768]{1,0:T(8,128)(2,1)S(1)}, u32[]{:S(2)}, u32[]{:S(2)}) collective-permute-start(bf16[128,768]{1,0:T(8,128)(2,1)S(1)} %get-tuple-element.103.refs_0_), channel_id=1, source_target_pairs={{0,2},{2,0},{1,3},{3,1},{4,6},{6,4},{5,7},{7,5},{8,10},{10,8},{9,1... | collective-permute-start | bytes 589832 | tf_op jit(solution)/shard_map/ppermute | solution.py:22
  131.4 4.6 %collective-permute-start.25 = (bf16[128,768]{1,0:T(8,128)(2,1)S(1)}, bf16[128,768]{1,0:T(8,128)(2,1)S(1)}, u32[]{:S(2)}, u32[]{:S(2)}) collective-permute-start(bf16[128,768]{1,0:T(8,128)(2,1)S(1)} %get-tuple-element.103.refs_0_), channel_id=1, source_target_pairs={{0,1},{1,0},{2,3},{3,2},{4,5},{5,4},{6,7},{7,6},{8,9},{9,8},{10,11... | collective-permute-start | bytes 589832 | tf_op jit(solution)/shard_map/ppermute | solution.py:22
  140.3 1.8 collective-permute-start.27
  143.7 28.1 %collective-permute-start.44 = (bf16[384,1536]{1,0:T(8,128)(2,1)S(1)}, bf16[384,1536]{1,0:T(8,128)(2,1)S(1)}, u32[]{:S(2)}, u32[]{:S(2)}) collective-permute-start(bf16[384,1536]{1,0:T(8,128)(2,1)S(1)} %get-tuple-element.146), channel_id=1, source_target_pairs={{0,16},{16,0},{1,17},{17,1},{2,18},{18,2},{3,19},{19,3},{4,20},{20... | collective-permute-start | bytes 3538952 | tf_op jit(solution)/shard_map/ppermute | solution.py:22
  144.3 6.7 %collective-permute-start.28 = (bf16[128,768]{1,0:T(8,128)(2,1)S(1)}, bf16[128,768]{1,0:T(8,128)(2,1)S(1)}, u32[]{:S(2)}, u32[]{:S(2)}) collective-permute-start(bf16[128,768]{1,0:T(8,128)(2,1)S(1)} %get-tuple-element.108), channel_id=1, source_target_pairs={{0,2},{2,0},{1,3},{3,1},{4,6},{6,4},{5,7},{7,5},{8,10},{10,8},{9,1... | collective-permute-start | bytes 589832 | tf_op jit(solution)/shard_map/ppermute | solution.py:22
  154.7 6.4 %collective-permute-start.29 = (bf16[128,192]{1,0:T(8,128)(2,1)S(1)}, bf16[128,192]{1,0:T(8,128)(2,1)S(1)}, u32[]{:S(2)}, u32[]{:S(2)}) collective-permute-start(bf16[128,192]{1,0:T(8,128)(2,1)S(1)} %get-tuple-element.115), channel_id=1, source_target_pairs={{0,4},{4,8},{8,12},{12,0},{1,5},{5,9},{9,13},{13,1},{2,6},{6,10},{... | collective-permute-start | bytes 147464 | tf_op jit(solution)/shard_map/ppermute | solution.py:22
  155.5 7.1 %collective-permute-start.30 = (bf16[128,192]{1,0:T(8,128)(2,1)S(1)}, bf16[128,192]{1,0:T(8,128)(2,1)S(1)}, u32[]{:S(2)}, u32[]{:S(2)}) collective-permute-start(bf16[128,192]{1,0:T(8,128)(2,1)S(1)} %get-tuple-element.116), channel_id=1, source_target_pairs={{0,8},{4,12},{8,0},{12,4},{1,9},{5,13},{9,1},{13,5},{2,10},{6,14},... | collective-permute-start | bytes 147464 | tf_op jit(solution)/shard_map/ppermute | solution.py:22
  156.8 5.8 %collective-permute-start.31 = (bf16[128,192]{1,0:T(8,128)(2,1)S(1)}, bf16[128,192]{1,0:T(8,128)(2,1)S(1)}, u32[]{:S(2)}, u32[]{:S(2)}) collective-permute-start(bf16[128,192]{1,0:T(8,128)(2,1)S(1)} %get-tuple-element.117), channel_id=1, source_target_pairs={{0,12},{4,0},{8,4},{12,8},{1,13},{5,1},{9,5},{13,9},{2,14},{6,2},{... | collective-permute-start | bytes 147464 | tf_op jit(solution)/shard_map/ppermute | solution.py:22
  170.1 3.0 %collective-permute-start.32 = (bf16[2,512,384]{2,1,0:T(8,128)(2,1)}, bf16[2,512,384]{2,1,0:T(8,128)(2,1)S(1)}, u32[]{:S(2)}, u32[]{:S(2)}) collective-permute-start(bf16[2,512,384]{2,1,0:T(8,128)(2,1)} %get-tuple-element.120), channel_id=1, source_target_pairs={{0,1},{1,0},{2,3},{3,2},{4,5},{5,4},{6,7},{7,6},{8,9},{9,8},{10,11... | collective-permute-start | bytes 2359304 | tf_op jit(solution)/shard_map/ppermute | solution.py:22
  176.1 10.9 %collective-permute-start.33 = (bf16[512,384]{1,0:T(8,128)(2,1)}, bf16[512,384]{1,0:T(8,128)(2,1)}, u32[]{:S(2)}, u32[]{:S(2)}) collective-permute-start(bf16[512,384]{1,0:T(8,128)(2,1)} %get-tuple-element.122), channel_id=1, source_target_pairs={{0,2},{2,0},{1,3},{3,1},{4,6},{6,4},{5,7},{7,5},{8,10},{10,8},{9,1... | collective-permute-start | bytes 1179656 | tf_op jit(solution)/shard_map/ppermute | solution.py:22
  194.6 2.9 %collective-permute-start.34 = (bf16[16,24,1536]{2,1,0:T(8,128)(2,1)S(1)}, bf16[16,24,1536]{2,1,0:T(8,128)(2,1)S(1)}, u32[]{:S(2)}, u32[]{:S(2)}) collective-permute-start(bf16[16,24,1536]{2,1,0:T(8,128)(2,1)S(1)} %get-tuple-element.130), channel_id=1, source_target_pairs={{0,1},{1,0},{2,3},{3,2},{4,5},{5,4},{6,7},{7,6},{8,9},{9,8},{10,11... | collective-permute-start | bytes 3538952 | tf_op jit(solution)/shard_map/ppermute | solution.py:22
  198.4 9.1 %collective-permute-start.35 = (bf16[2,4,1,24,768]{4,3,2,1,0:T(8,128)(2,1)S(1)}, bf16[2,4,1,24,768]{4,3,2,1,0:T(8,128)(2,1)S(1)}, u32[]{:S(2)}, u32[]{:S(2)}) collective-permute-start(bf16[2,4,1,24,768]{4,3,2,1,0:T(8,128)(2,1)S(1)} %get-tuple-element.132), channel_id=1, source_target_pairs={{0,2},{2,0},{1,3},{3,1},{4,6},{6,4},{5,7},{7,5},{8,10},{10,8},{9,1... | collective-permute-start | bytes 884744 | tf_op jit(solution)/shard_map/ppermute | solution.py:22
  200.0 8.8 %collective-permute-start.36 = (bf16[1,4,2,24,768]{4,3,2,1,0:T(8,128)(2,1)S(1)}, bf16[1,4,2,24,768]{4,3,2,1,0:T(8,128)(2,1)S(1)}, u32[]{:S(2)}, u32[]{:S(2)}) collective-permute-start(bf16[1,4,2,24,768]{4,3,2,1,0:T(8,128)(2,1)S(1)} %get-tuple-element.134), channel_id=1, source_target_pairs={{0,16},{16,0},{1,17},{17,1},{2,18},{18,2},{3,19},{19,3},{4,20},{20... | collective-permute-start | bytes 884744 | tf_op jit(solution)/shard_map/ppermute | solution.py:22
  201.2 12.6 %collective-permute-start.39 = (bf16[128,768]{1,0:T(8,128)(2,1)}, bf16[128,768]{1,0:T(8,128)(2,1)S(1)}, u32[]{:S(2)}, u32[]{:S(2)}) collective-permute-start(bf16[128,768]{1,0:T(8,128)(2,1)} %get-tuple-element.139), channel_id=1, source_target_pairs={{0,8},{4,12},{8,0},{12,4},{1,9},{5,13},{9,1},{13,5},{2,10},{6,14},... | collective-permute-start | bytes 589832 | tf_op jit(solution)/shard_map/ppermute | solution.py:22
  201.7 12.1 %collective-permute-start.40 = (bf16[128,768]{1,0:T(8,128)(2,1)}, bf16[128,768]{1,0:T(8,128)(2,1)S(1)}, u32[]{:S(2)}, u32[]{:S(2)}) collective-permute-start(bf16[128,768]{1,0:T(8,128)(2,1)} %get-tuple-element.140), channel_id=1, source_target_pairs={{0,12},{4,0},{8,4},{12,8},{1,13},{5,1},{9,5},{13,9},{2,14},{6,2},{... | collective-permute-start | bytes 589832 | tf_op jit(solution)/shard_map/ppermute | solution.py:22
  209.5 5.2 %collective-permute-start.37 = (bf16[1,4,1,24,768]{4,3,2,1,0:T(8,128)(2,1)S(1)}, bf16[1,4,1,24,768]{4,3,2,1,0:T(8,128)(2,1)S(1)}, u32[]{:S(2)}, u32[]{:S(2)}) collective-permute-start(bf16[1,4,1,24,768]{4,3,2,1,0:T(8,128)(2,1)S(1)} %get-tuple-element.136), channel_id=1, source_target_pairs={{0,16},{16,0},{1,17},{17,1},{2,18},{18,2},{3,19},{19,3},{4,20},{20... | collective-permute-start | bytes 442376 | tf_op jit(solution)/shard_map/ppermute | solution.py:22
  210.8 5.1 %collective-permute-start.38 = (bf16[1,4,1,24,768]{4,3,2,1,0:T(8,128)(2,1)S(1)}, bf16[1,4,1,24,768]{4,3,2,1,0:T(8,128)(2,1)S(1)}, u32[]{:S(2)}, u32[]{:S(2)}) collective-permute-start(bf16[1,4,1,24,768]{4,3,2,1,0:T(8,128)(2,1)S(1)} %get-tuple-element.138), channel_id=1, source_target_pairs={{0,2},{2,0},{1,3},{3,1},{4,6},{6,4},{5,7},{7,5},{8,10},{10,8},{9,1... | collective-permute-start | bytes 442376 | tf_op jit(solution)/shard_map/ppermute | solution.py:22
  217.9 4.4 %collective-permute-start.45 = (bf16[1,1,1,2,24,768]{5,4,3,2,1,0:T(8,128)(2,1)S(1)}, bf16[1,1,1,2,24,768]{5,4,3,2,1,0:T(8,128)(2,1)S(1)}, u32[]{:S(2)}, u32[]{:S(2)}) collective-permute-start(bf16[1,1,1,2,24,768]{5,4,3,2,1,0:T(8,128)(2,1)S(1)} %get-tuple-element.166), channel_id=1, source_target_pairs={{0,2},{2,0},{1,3},{3,1},{4,6},{6,4},{5,7},{7,5},{8,10},{10,8},{9,1... | collective-permute-start | bytes 221192 | tf_op jit(solution)/shard_map/ppermute | solution.py:22
  218.5 8.3 %collective-permute-start.47 = (bf16[128,768]{1,0:T(8,128)(2,1)S(1)}, bf16[128,768]{1,0:T(8,128)(2,1)S(1)}, u32[]{:S(2)}, u32[]{:S(2)}) collective-permute-start(bf16[128,768]{1,0:T(8,128)(2,1)S(1)} %copy-done.62), channel_id=1, source_target_pairs={{0,4},{4,8},{8,12},{12,0},{1,5},{5,9},{9,13},{13,1},{2,6},{6,10},{... | collective-permute-start | bytes 589832 | tf_op jit(solution)/shard_map/ppermute | solution.py:22
  222.3 5.6 %collective-permute-start.46 = (bf16[1,1,2,1,24,768]{5,4,3,2,1,0:T(8,128)(2,1)S(1)}, bf16[1,1,2,1,24,768]{5,4,3,2,1,0:T(8,128)(2,1)S(1)}, u32[]{:S(2)}, u32[]{:S(2)}) collective-permute-start(bf16[1,1,2,1,24,768]{5,4,3,2,1,0:T(8,128)(2,1)S(1)} %get-tuple-element.164), channel_id=1, source_target_pairs={{0,1},{1,0},{2,3},{3,2},{4,5},{5,4},{6,7},{7,6},{8,9},{9,8},{10,11... | collective-permute-start | bytes 221192 | tf_op jit(solution)/shard_map/ppermute | solution.py:22
  222.4 7.0 %collective-permute-start.41 = (bf16[1,1,1,24,1536]{4,3,2,1,0:T(8,128)(2,1)S(1)}, bf16[1,1,1,24,1536]{4,3,2,1,0:T(8,128)(2,1)S(1)}, u32[]{:S(2)}, u32[]{:S(2)}) collective-permute-start(bf16[1,1,1,24,1536]{4,3,2,1,0:T(8,128)(2,1)S(1)} %get-tuple-element.142), channel_id=1, source_target_pairs={{0,4},{4,8},{8,12},{12,0},{1,5},{5,9},{9,13},{13,1},{2,6},{6,10},{... | collective-permute-start | bytes 221192 | tf_op jit(solution)/shard_map/ppermute | solution.py:22
  224.3 7.8 %collective-permute-start.42 = (bf16[1,1,1,24,1536]{4,3,2,1,0:T(8,128)(2,1)S(1)}, bf16[1,1,1,24,1536]{4,3,2,1,0:T(8,128)(2,1)S(1)}, u32[]{:S(2)}, u32[]{:S(2)}) collective-permute-start(bf16[1,1,1,24,1536]{4,3,2,1,0:T(8,128)(2,1)S(1)} %get-tuple-element.143), channel_id=1, source_target_pairs={{0,8},{4,12},{8,0},{12,4},{1,9},{5,13},{9,1},{13,5},{2,10},{6,14},... | collective-permute-start | bytes 221192 | tf_op jit(solution)/shard_map/ppermute | solution.py:22
  225.7 6.5 %collective-permute-start.43 = (bf16[1,1,1,24,1536]{4,3,2,1,0:T(8,128)(2,1)S(1)}, bf16[1,1,1,24,1536]{4,3,2,1,0:T(8,128)(2,1)S(1)}, u32[]{:S(2)}, u32[]{:S(2)}) collective-permute-start(bf16[1,1,1,24,1536]{4,3,2,1,0:T(8,128)(2,1)S(1)} %get-tuple-element.144), channel_id=1, source_target_pairs={{0,12},{4,0},{8,4},{12,8},{1,13},{5,1},{9,5},{13,9},{2,14},{6,2},{... | collective-permute-start | bytes 221192 | tf_op jit(solution)/shard_map/ppermute | solution.py:22
  (78 other events, 585.1 us)
Sparse Core Ops, SparseCore 0:
  18.8 75.9 all-gather.1
  173.3 27.4 reduce-scatter.1

commit v4 on v3

--- a/solution.py
+++ b/solution.py
@@ -161,6 +161,48 @@
 
     args = (place, *pieces, w_down.reshape(2 * sx, rows, -1)) if joined else (place, *pieces)
     return call(body, args, [((2 * sx, rows, wide), BF)], "join_up", 1)[0].reshape(2 * sx * rows, wide)
+
+
+def open_sums(place, sums, width, sx, wr, after):
+    joined = len(sums) == 1
+    rows = sums[0].shape[0]
+    ff = sums[-1].shape[1] - width if joined else sums[-1].shape[1]
+    first = width if joined else 0
+
+    def body(at_ref, *refs):
+        ups, down_ref, outs = refs[len(sums) - 1], refs[len(sums)], refs[len(sums) + 1:]
+        if joined:
+            for i in range(2 * sx):
+                down_ref[i * wr:(i + 1) * wr, :] = ups[i, :, 0:width].astype(F32)
+        else:
+            down_ref[...] = refs[0][...].astype(F32)
+        for dc in range(2):
+            core = at_ref[1] if dc == 0 else 1 - at_ref[1]
+            for dx in range(sx):
+                outs[dc * sx + dx][...] = ups[lax.rem(at_ref[0] + dx, sx) * 2 + core][:, first:]
+
+    outs = [((rows, width), F32)] + [((wr, ff), BF)] * (2 * sx)
+    args = (place, *sums[:-1], sums[-1].reshape(2 * sx, wr, -1))
+    down, *pieces = call(body, args, outs, "open_sums", 1, after)
+    return down, pieces
+
+
+def close_up(place, pieces, ffd):
+    sx = len(pieces) // 2
+    wr, ff = pieces[0].shape
+
+    def body(at_ref, *refs):
+        out, every = refs[-2:]
+        for dc in range(2):
+            core = at_ref[1] if dc == 0 else 1 - at_ref[1]
+            for dx in range(sx):
+                every[lax.rem(at_ref[0] + sx - dx, sx) * 2 + core] = refs[dc * sx + dx][...].astype(F32)
+        for i in range(2 * sx):
+            for b in range(ff // ffd):
+                at = (b * 2 * sx + i) * ffd
+                out[:, at:at + ffd] = every[i, :, b * ffd:(b + 1) * ffd]
+
+    return call(body, (place, *pieces), [((wr, 2 * sx * ff), F32)], "close_up", 1, scratch=[pltpu.VMEM((2 * sx, wr, ff), F32)])[0]
 
 
 def held(value, after):
@@ -822,6 +864,14 @@
     def cut_z(value):
         return [lax.dynamic_slice_in_dim(value, lax.rem(iz + d, sz), 1, 0) for d in range(sz)]
 
+    def to_group(pieces):
+        sent = [pieces[0]]
+        for d in range(1, 2 * sx):
+            dc, dx = d // sx, d % sx
+            pairs = [(x * 2 + c, (x + dx) % sx * 2 + (c + dc) % 2) for x in range(sx) for c in range(2)]
+            sent.append(lax.ppermute(pieces[d], ("x", "core"), pairs))
+        return sent
+
     flat = jnp.concatenate([jnp.stack([q_bias, v_bias, out_bias, down_bias, ln1_gain, ln1_bias, ln2_gain, ln2_bias]), up_bias.reshape(upc, wr)])
     hidden = hidden_in[0]
     pieces = from_z(hidden)
@@ -833,10 +883,7 @@
 
     at_xc = jnp.stack([ix, core]).astype(jnp.int32)
     ups = list(pack_up(at_xc, w_up, w_out, ffd, sx))
-    for d in range(1, 2 * sx):
-        dc, dx = d // sx, d % sx
-        pairs = [(x * 2 + c, (x + dx) % sx * 2 + (c + dc) % 2) for x in range(sx) for c in range(2)]
-        ups[d] = lax.ppermute(ups[d], ("x", "core"), pairs)
+    ups = to_group(ups)
     weights = [join_up(at_xc, ups, w_down)]
     if ffd != 2 * sx * wr:
         weights = weights + [w_down]
@@ -882,18 +929,14 @@
     third = fold_both(kept.reshape(sy, sz, sx, wr, -1), shift(sent, "core", 1).reshape(sy, sz, sx, wr, -1), ix, iy, width)
     third = fold_cross(third[:sx], passed(third[:sx], "x"), third[sx:], passed(third[sx:], "y"), ix, iy)
     third = fold_last(third[:sy], passed(third[:sy], "y"), third[sy:], passed(third[sy:], "x"), iz, after=[gn1_parts[2], gn1_parts[3]])
-    ready = third[0][0, 0, 0, :, :LANES]
-    gw_sums = [held(member, [ready]) for member in gw_sums]
     third = [third[0]] + passed(third, "z")
-
-    gw_down = gw_sums[0][:, :width].astype(F32)
-    gw_up = gw_sums[-1][:, -ff:].reshape(1, 1, sx, 2, wr, ff)
-    up_x = [lax.dynamic_slice_in_dim(gw_up, lax.rem(ix + d, sx), 1, 2) for d in range(sx)]
-    gw_up = arrange([up_x[0]] + [shift(up_x[d], "x", d) for d in range(1, sx)], ix, 2)
-    gw_up = arrange([lax.dynamic_slice_in_dim(gw_up, core, 1, 3), shift(lax.dynamic_slice_in_dim(gw_up, 1 - core, 1, 3), "core", 1)], core, 3)
-    gw_up = gw_up.reshape(sx, 2, wr, sy * sz, ffd).transpose(2, 3, 0, 1, 4).reshape(wr, -1).astype(F32)
-
-    grad_w_qkv, sums, gw_out = unpack_one(place, third, after=[gw_up])
+    ready = third[1:2]
+
+    gw_down, ups = open_sums(at_xc, gw_sums, width, sx, wr, ready)
+    ups = to_group(ups)
+    gw_up = close_up(at_xc, ups, ffd)
+
+    grad_w_qkv, sums, gw_out = unpack_one(place, third, after=ups[-1:])
     sums = sums.T
     loss = jnp.sum(sums[16:17 + -(-devices // wr)]) / (count * width)
     return (

time: 244 us -> 245 us (level)
  starting transfers between devices: 52.9 us -> 59.2 us
  waiting for transfers between devices: 102 us -> 96 us
  Pallas kernels: 38.6 us -> 41.2 us
    ppermute x45 -> x43, waiting for transfers between devices: 94.8 us -> 88.4 us  [shift(): lax.ppermute(value, axis, [(a, (a + step) % size) for a in range(size)])]
    ppermute x45 -> x43, starting transfers between devices: 49.6 us -> 54 us  [shift(): lax.ppermute(value, axis, [(a, (a + step) % size) for a in range(size)])]
    pallas_call x26 -> x27, Pallas kernels: 38.4 us -> 41.1 us  [call(): pl.pallas_call(whole, in_specs=specs + [pl.BlockSpec(memory_space=pl.ANY)...]
    ppermute x3 -> x6, starting transfers between devices: 3.21 us -> 5.06 us  [to_group(): sent.append(lax.ppermute(pieces[d], ('x', 'core'), pairs))]
    unnamed x153 -> x151, local copies, waits for them, and re-layouts: 22.7 us -> 21.9 us
  transfers between devices with their start and end apart: 50 -> 51, of which waited for: 35 -> 33; matrix products, arithmetic and copies ran while one was open for 3% -> 3% of each run, Pallas kernels for 10% -> 11%
where the time goes in v4:
time: 245 us; the launch traced here: 244 us
  waiting for transfers between devices  96 us (39%)
  starting transfers between devices  59.2 us (24%)
  Pallas kernels  41.2 us (17%)
  local copies, waits for them, and re-layouts  27.6 us (11%)
  between operations  17.4 us (7%)
  other arithmetic  2.5 us (1%)
    ppermute x43, waiting for transfers between devices, shift(): lax.ppermute(value, axis, [(a, (a + step) % size) for a in range(size)])  88.4 us
    ppermute x43, starting transfers between devices, shift(): lax.ppermute(value, axis, [(a, (a + step) % size) for a in range(size)])  54 us
    pallas_call x27, Pallas kernels, call(): pl.pallas_call(whole, in_specs=specs + [pl.BlockSpec(memory_space=pl.ANY)...  41.1 us
    unnamed x151, local copies, waits for them, and re-layouts  21.9 us
    ppermute x6, starting transfers between devices, to_group(): sent.append(lax.ppermute(pieces[d], ('x', 'core'), pairs))  5.06 us
  transfers between devices with their start and end apart: 51, of which 33 were waited for; matrix products, arithmetic and copies ran while one was open for 3% of the time, Pallas kernels for 11%

profile of v4, /device:TPU:0, one launch (start us, length us, event | category | flops | bytes accessed | tf_op | source)
XLA Modules:
  0.0 243.9 jit_solution(6367256489673226161)
XLA Ops:
  9.8 3.0 %collective-permute-start.15 = (bf16[24,1152]{1,0:T(8,128)(2,1)S(1)}, bf16[24,1152]{1,0:T(8,128)(2,1)S(1)}, u32[]{:S(2)}, u32[]{:S(2)}) collective-permute-start(bf16[24,1152]{1,0:T(8,128)(2,1)S(1)} %get-tuple-element.97), channel_id=1, source_target_pairs={{0,2},{1,3},{2,0},{3,1},{4,6},{5,7},{6,4},{7,5},{8,10},{9,11},{10,... | collective-permute-start | bytes 165896 | tf_op jit(solution)/shard_map/ppermute | solution.py:872
  13.0 1.9 collective-permute-done.15.refs_2_
  18.7 1.6 collective-permute-start.4
  20.8 1.6 collective-permute-start
  23.6 2.7 %collective-permute-start.2 = (bf16[1,24,704]{2,1,0:T(8,128)(2,1)S(1)}, bf16[1,24,704]{2,1,0:T(8,128)(2,1)S(1)}, u32[]{:S(2)}, u32[]{:S(2)}) collective-permute-start(bf16[1,24,704]{2,1,0:T(8,128)(2,1)S(1)} %get-tuple-element.172), channel_id=1, source_target_pairs={{0,12},{4,0},{8,4},{12,8},{1,13},{5,1},{9,5},{13,9},{2,14},{6,2},{... | collective-permute-start | bytes 101384 | tf_op jit(solution)/shard_map/ppermute | solution.py:22
  26.3 2.8 %collective-permute-done.refs_1_ = bf16[1,24,704]{2,1,0:T(8,128)(2,1)S(1)} collective-permute-done((bf16[1,24,704]{2,1,0:T(8,128)(2,1)S(1)}, bf16[1,24,704]{2,1,0:T(8,128)(2,1)S(1)}, u32[]{:S(2)}, u32[]{:S(2)}) %collective-permute-start) | collective-permute-done | bytes 33824 | tf_op jit(solution)/shard_map/ppermute | solution.py:22
  31.6 4.6 %collective-permute-done.3.refs_1_ = bf16[1,4,1,24,704]{4,3,2,1,0:T(8,128)(2,1)S(1)} collective-permute-done((bf16[1,4,1,24,704]{4,3,2,1,0:T(8,128)(2,1)S(1)}, bf16[1,4,1,24,704]{4,3,2,1,0:T(8,128)(2,1)S(1)}, u32[]{:S(2)}, u32[]{:S(2)}) %collective-permute-start.3) | collective-permute-done | bytes 135200 | tf_op jit(solution)/shard_map/ppermute | solution.py:22
  36.3 1.6 collective-permute-start.5
  38.3 3.4 %collective-permute-start.7 = (bf16[128,768]{1,0:T(8,128)(2,1)S(1)}, bf16[128,768]{1,0:T(8,128)(2,1)S(1)}, u32[]{:S(2)}, u32[]{:S(2)}) collective-permute-start(bf16[128,768]{1,0:T(8,128)(2,1)S(1)} %bitcast.51), channel_id=1, source_target_pairs={{0,12},{4,0},{8,4},{12,8},{1,13},{5,1},{9,5},{13,9},{2,14},{6,2},{... | collective-permute-start | bytes 589832 | tf_op jit(solution)/shard_map/ppermute | solution.py:22
  41.7 11.0 %collective-permute-done.6.refs_2_.refs_3_ = bf16[128,768]{1,0:T(8,128)(2,1)S(1)} collective-permute-done((bf16[128,768]{1,0:T(8,128)(2,1)S(1)}, bf16[128,768]{1,0:T(8,128)(2,1)S(1)}, u32[]{:S(2)}, u32[]{:S(2)}) %collective-permute-start.6) | collective-permute-done | bytes 196640 | tf_op jit(solution)/shard_map/ppermute | solution.py:22
  52.8 2.0 collective-permute-done.8.refs_1_
  59.6 9.1 %collective-permute-done.9.refs_4_.refs_9_ = bf16[512,384]{1,0:T(8,128)(2,1)S(1)} collective-permute-done((bf16[512,384]{1,0:T(8,128)(2,1)S(1)}, bf16[512,384]{1,0:T(8,128)(2,1)S(1)}, u32[]{:S(2)}, u32[]{:S(2)}) %collective-permute-start.9) | collective-permute-done | bytes 393248 | tf_op jit(solution)/shard_map/ppermute | solution.py:22
  70.4 4.3 %attend.1 = (bf16[128,192]{1,0:T(8,128)(2,1)S(1)}, bf16[128,192]{1,0:T(8,128)(2,1)S(1)}, bf16[128,192]{1,0:T(8,128)(2,1)S(1)}, bf16[128,192]{1,0:T(8,128)(2,1)S(1)}, f32[2,512,256]{2,1,0:T(8,128)S(1)}) custom-call(s32[5]{0:T(128)S(1)} %stack.79.refs_0_, bf16[512,256]{1,0:T(8,128)(2,1)S(1)} %get-tuple-element.90.refs_1_, ...), custom_call_target="tpu_custom_call" | custom-call | flops 1 | bytes 1 | tf_op jit(solution)/shard_map/attend/pallas_call | solution.py:459
  75.8 4.5 %collective-permute-start.12 = (bf16[128,192]{1,0:T(8,128)(2,1)S(1)}, bf16[128,192]{1,0:T(8,128)(2,1)S(1)}, u32[]{:S(2)}, u32[]{:S(2)}) collective-permute-start(bf16[128,192]{1,0:T(8,128)(2,1)S(1)} %get-tuple-element.93), channel_id=1, source_target_pairs={{0,4},{4,8},{8,12},{12,0},{1,5},{5,9},{9,13},{13,1},{2,6},{6,10},{... | collective-permute-start | bytes 147464 | tf_op jit(solution)/shard_map/ppermute | solution.py:22
  82.7 2.2 collective-permute-done.12.refs_1_
  84.8 5.1 %collective-permute-done.13.refs_2_ = bf16[128,192]{1,0:T(8,128)(2,1)S(1)} collective-permute-done((bf16[128,192]{1,0:T(8,128)(2,1)S(1)}, bf16[128,192]{1,0:T(8,128)(2,1)S(1)}, u32[]{:S(2)}, u32[]{:S(2)}) %collective-permute-start.13) | collective-permute-done | bytes 49184 | tf_op jit(solution)/shard_map/ppermute | solution.py:22
  90.9 3.8 %all-gather.2.cloned.1.call-done.refs_0_.refs_5_.refs_6_ = bf16[768,1920]{1,0:T(8,128)(2,1)} async-done(((bf16[96,1920]{1,0:T(8,128)(2,1)}), bf16[768,1920]{1,0:T(8,128)(2,1)}) %all-gather.2.cloned.1.call-update) | async-done | bytes 2949136 | tf_op jit(solution)/shard_map/all_gather | solution.py:890
  94.7 1.8 copy-done
  97.7 1.9 collective-permute-done.18.refs_3_.refs_7_
  103.2 5.5 %collective-permute-done.19.refs_1_ = bf16[128,768]{1,0:T(8,128)(2,1)S(1)} collective-permute-done((bf16[128,768]{1,0:T(8,128)(2,1)S(1)}, bf16[128,768]{1,0:T(8,128)(2,1)S(1)}, u32[]{:S(2)}, u32[]{:S(2)}) %collective-permute-start.19) | collective-permute-done | bytes 196640 | tf_op jit(solution)/shard_map/ppermute | solution.py:22
  110.1 2.3 mlp_up.1
  114.6 1.6 collective-permute-done.22.refs_1_
  117.6 1.5 collective-permute-start.23
  120.6 4.3 %collective-permute-done.23.refs_2_ = bf16[128,768]{1,0:T(8,128)(2,1)} collective-permute-done((bf16[128,768]{1,0:T(8,128)(2,1)}, bf16[128,768]{1,0:T(8,128)(2,1)}, u32[]{:S(2)}, u32[]{:S(2)}) %collective-permute-start.23) | collective-permute-done | bytes 196640 | tf_op jit(solution)/shard_map/ppermute | solution.py:22
  127.9 2.0 finish.1
  129.9 1.5 collective-permute-start.24
  131.4 4.6 %collective-permute-done.24.refs_1_ = bf16[128,768]{1,0:T(8,128)(2,1)S(1)} collective-permute-done((bf16[128,768]{1,0:T(8,128)(2,1)S(1)}, bf16[128,768]{1,0:T(8,128)(2,1)S(1)}, u32[]{:S(2)}, u32[]{:S(2)}) %collective-permute-start.24) | collective-permute-done | bytes 196640 | tf_op jit(solution)/shard_map/ppermute | solution.py:22
  137.4 2.8 %mlp_back.1 = (f32[2,128,768]{2,1,0:T(8,128)S(1)}, bf16[2,128,768]{2,1,0:T(8,128)(2,1)S(1)}, bf16[512,768]{1,0:T(8,128)(2,1)S(1)}, bf16[512,768]{1,0:T(8,128)(2,1)S(1)}) custom-call(bf16[128,768]{1,0:T(8,128)(2,1)S(1)} %get-tuple-element.108.refs_0_, bf16[128,768]{1,0:T(8,128)(2,1)S(1)} %collective-permute-done.24.refs_1_, ...), custom_call_target="tpu_custom_call" | custom-call | flops 1 | bytes 1 | tf_op jit(solution)/shard_map/mlp_back/pallas_call | solution.py:459
  140.5 1.6 collective-permute-done.27.refs_1_
  144.3 1.6 collective-permute-start.28
  145.9 5.1 %collective-permute-done.28.refs_2_ = bf16[128,768]{1,0:T(8,128)(2,1)S(1)} collective-permute-done((bf16[128,768]{1,0:T(8,128)(2,1)S(1)}, bf16[128,768]{1,0:T(8,128)(2,1)S(1)}, u32[]{:S(2)}, u32[]{:S(2)}) %collective-permute-start.28) | collective-permute-done | bytes 196640 | tf_op jit(solution)/shard_map/ppermute | solution.py:22
  151.1 1.8 out_back.1
  156.8 1.7 collective-permute-start.31
  158.5 2.5 %collective-permute-done.29.refs_3_ = bf16[128,192]{1,0:T(8,128)(2,1)S(1)} collective-permute-done((bf16[128,192]{1,0:T(8,128)(2,1)S(1)}, bf16[128,192]{1,0:T(8,128)(2,1)S(1)}, u32[]{:S(2)}, u32[]{:S(2)}) %collective-permute-start.29) | collective-permute-done | bytes 49184 | tf_op jit(solution)/shard_map/ppermute | solution.py:22
  161.1 1.6 collective-permute-done.30.refs_4_
  162.7 7.4 %attend_back.1 = (bf16[512,192]{1,0:T(8,128)(2,1)S(1)}, f32[2,512,384]{2,1,0:T(8,128)S(1)}, bf16[2,512,384]{2,1,0:T(8,128)(2,1)}, f32[8,128]{1,0:T(8,128)S(1)}) custom-call(s32[5]{0:T(128)S(1)} %copy-done.59, bf16[512,256]{1,0:T(8,128)(2,1)S(1)} %copy-done.34, bf16[128,192]{1,0:T(8,128)(2,1)S(1)} %get-tuple-element.119.refs_2_, ...), custom_call_target="tpu_custom_call" | custom-call | flops 1 | bytes 1 | tf_op jit(solution)/shard_map/attend_back/pallas_call | solution.py:459
  170.1 1.7 collective-permute-done.44.refs_1_
  176.0 1.5 collective-permute-start.33
  178.3 1.7 dynamic_update_slice.3
  181.0 6.0 %collective-permute-done.33.refs_2_ = bf16[512,384]{1,0:T(8,128)(2,1)} collective-permute-done((bf16[512,384]{1,0:T(8,128)(2,1)}, bf16[512,384]{1,0:T(8,128)(2,1)}, u32[]{:S(2)}, u32[]{:S(2)}) %collective-permute-start.33) | collective-permute-done | bytes 393248 | tf_op jit(solution)/shard_map/ppermute | solution.py:22
  187.0 2.6 %join_back.1 = (bf16[512,576]{1,0:T(8,128)(2,1)S(1)}, f32[512,768]{1,0:T(8,128)S(1)}, f32[128,768]{1,0:T(8,128)S(1)}, bf16[128,768]{1,0:T(8,128)(2,1)}, bf16[128...) custom-call(s32[1]{0:T(128)} %bitcast.3.place_ref.refs_0_, bf16[512,384]{1,0:T(8,128)(2,1)S(1)} %get-tuple-element.126.refs_1_, ...), custom_call_target="tpu_custom_call" | custom-call | flops 1 | bytes 1 | tf_op jit(solution)/shard_map/join_back/pallas_call | solution.py:459
  191.6 2.2 weights_back.1
  194.0 2.8 %collective-permute-done.34 = bf16[16,24,1536]{2,1,0:T(8,128)(2,1)S(1)} collective-permute-done((bf16[16,24,1536]{2,1,0:T(8,128)(2,1)S(1)}, bf16[16,24,1536]{2,1,0:T(8,128)(2,1)S(1)}, u32[]{:S(2)}, u32[]{:S(2)}) %collective-permute-start.34) | collective-permute-done | bytes 1179680 | tf_op jit(solution)/shard_map/ppermute | solution.py:22
  197.6 1.6 collective-permute-start.35
  200.9 3.2 %collective-permute-start.40 = (bf16[128,768]{1,0:T(8,128)(2,1)S(1)}, bf16[128,768]{1,0:T(8,128)(2,1)S(1)}, u32[]{:S(2)}, u32[]{:S(2)}) collective-permute-start(bf16[128,768]{1,0:T(8,128)(2,1)S(1)} %get-tuple-element.145), channel_id=1, source_target_pairs={{0,12},{4,0},{8,4},{12,8},{1,13},{5,1},{9,5},{13,9},{2,14},{6,2},{... | collective-permute-start | bytes 589832 | tf_op jit(solution)/shard_map/ppermute | solution.py:22
  204.1 2.7 %collective-permute-done.35.refs_2_ = bf16[2,4,1,24,768]{4,3,2,1,0:T(8,128)(2,1)S(1)} collective-permute-done((bf16[2,4,1,24,768]{4,3,2,1,0:T(8,128)(2,1)S(1)}, bf16[2,4,1,24,768]{4,3,2,1,0:T(8,128)(2,1)S(1)}, u32[]{:S(2)}, u32[]{:S(2)}) %collective-permute-start.35) | collective-permute-done | bytes 294944 | tf_op jit(solution)/shard_map/ppermute | solution.py:22
  215.2 7.5 %collective-permute-start.41 = (bf16[1,1,1,24,1536]{4,3,2,1,0:T(8,128)(2,1)S(1)}, bf16[1,1,1,24,1536]{4,3,2,1,0:T(8,128)(2,1)S(1)}, u32[]{:S(2)}, u32[]{:S(2)}) collective-permute-start(bf16[1,1,1,24,1536]{4,3,2,1,0:T(8,128)(2,1)S(1)} %get-tuple-element.147), channel_id=1, source_target_pairs={{0,4},{4,8},{8,12},{12,0},{1,5},{5,9},{9,13},{13,1},{2,6},{6,10},{... | collective-permute-start | bytes 221192 | tf_op jit(solution)/shard_map/ppermute | solution.py:22
  222.7 2.4 collective-permute-start.43
  (274 shorter events, 72.3 us)
Async XLA Ops:
  7.2 87.5 %all-gather.2.cloned.1.call-start = ((), (), s32[]{:S(2)}) async-start(), calls=%async_computation.1 | async-start | bytes 3317760 | tf_op jit(solution)/shard_map/all_gather | solution.py:890
  9.8 5.1 %collective-permute-start.15 = (bf16[24,1152]{1,0:T(8,128)(2,1)S(1)}, bf16[24,1152]{1,0:T(8,128)(2,1)S(1)}, u32[]{:S(2)}, u32[]{:S(2)}) collective-permute-start(bf16[24,1152]{1,0:T(8,128)(2,1)S(1)} %get-tuple-element.97), channel_id=1, source_target_pairs={{0,2},{1,3},{2,0},{3,1},{4,6},{5,7},{6,4},{7,5},{8,10},{9,11},{10,... | collective-permute-start | bytes 165896 | tf_op jit(solution)/shard_map/ppermute | solution.py:872
  12.8 2.1 collective-permute-start.16
  12.8 3.6 %collective-permute-start.17 = (bf16[24,1152]{1,0:T(8,128)(2,1)S(1)}, bf16[24,1152]{1,0:T(8,128)(2,1)S(1)}, u32[]{:S(2)}, u32[]{:S(2)}) collective-permute-start(bf16[24,1152]{1,0:T(8,128)(2,1)S(1)} %get-tuple-element.99), channel_id=1, source_target_pairs={{0,3},{1,2},{2,1},{3,0},{4,7},{5,6},{6,5},{7,4},{8,11},{9,10},{10,... | collective-permute-start | bytes 165896 | tf_op jit(solution)/shard_map/ppermute | solution.py:872
  18.7 206.4 %reduce-scatter.2.cloned.1.call-start = ((), (), s32[]{:S(2)}) async-start(), calls=%async_computation.2 | async-start | bytes 1474560 | tf_op jit(solution)/shard_map/reduce_scatter | solution.py:920
  18.7 17.5 %collective-permute-start.4 = (bf16[128,768]{1,0:T(8,128)(2,1)S(1)}, bf16[128,768]{1,0:T(8,128)(2,1)S(1)}, u32[]{:S(2)}, u32[]{:S(2)}) collective-permute-start(bf16[128,768]{1,0:T(8,128)(2,1)S(1)} %bitcast.49), channel_id=1, source_target_pairs={{0,4},{4,8},{8,12},{12,0},{1,5},{5,9},{9,13},{13,1},{2,6},{6,10},{... | collective-permute-start | bytes 589832 | tf_op jit(solution)/shard_map/ppermute | solution.py:22
  20.8 8.4 %collective-permute-start = (bf16[1,24,704]{2,1,0:T(8,128)(2,1)S(1)}, bf16[1,24,704]{2,1,0:T(8,128)(2,1)S(1)}, u32[]{:S(2)}, u32[]{:S(2)}) collective-permute-start(bf16[1,24,704]{2,1,0:T(8,128)(2,1)S(1)} %get-tuple-element.174), channel_id=1, source_target_pairs={{0,4},{4,8},{8,12},{12,0},{1,5},{5,9},{9,13},{13,1},{2,6},{6,10},{... | collective-permute-start | bytes 101384 | tf_op jit(solution)/shard_map/ppermute | solution.py:22
  22.4 8.0 %collective-permute-start.1 = (bf16[1,24,704]{2,1,0:T(8,128)(2,1)S(1)}, bf16[1,24,704]{2,1,0:T(8,128)(2,1)S(1)}, u32[]{:S(2)}, u32[]{:S(2)}) collective-permute-start(bf16[1,24,704]{2,1,0:T(8,128)(2,1)S(1)} %get-tuple-element.173), channel_id=1, source_target_pairs={{0,8},{4,12},{8,0},{12,4},{1,9},{5,13},{9,1},{13,5},{2,10},{6,14},... | collective-permute-start | bytes 101384 | tf_op jit(solution)/shard_map/ppermute | solution.py:22
  23.6 6.8 %collective-permute-start.2 = (bf16[1,24,704]{2,1,0:T(8,128)(2,1)S(1)}, bf16[1,24,704]{2,1,0:T(8,128)(2,1)S(1)}, u32[]{:S(2)}, u32[]{:S(2)}) collective-permute-start(bf16[1,24,704]{2,1,0:T(8,128)(2,1)S(1)} %get-tuple-element.172), channel_id=1, source_target_pairs={{0,12},{4,0},{8,4},{12,8},{1,13},{5,1},{9,5},{13,9},{2,14},{6,2},{... | collective-permute-start | bytes 101384 | tf_op jit(solution)/shard_map/ppermute | solution.py:22
  30.5 5.8 %collective-permute-start.3 = (bf16[1,4,1,24,704]{4,3,2,1,0:T(8,128)(2,1)S(1)}, bf16[1,4,1,24,704]{4,3,2,1,0:T(8,128)(2,1)S(1)}, u32[]{:S(2)}, u32[]{:S(2)}) collective-permute-start(bf16[1,4,1,24,704]{4,3,2,1,0:T(8,128)(2,1)S(1)} %bitcast.60), channel_id=1, source_target_pairs={{0,2},{2,0},{1,3},{3,1},{4,6},{6,4},{5,7},{7,5},{8,10},{10,8},{9,1... | collective-permute-start | bytes 405512 | tf_op jit(solution)/shard_map/ppermute | solution.py:22
  36.3 16.4 %collective-permute-start.5 = (bf16[1,4,2,24,704]{4,3,2,1,0:T(8,128)(2,1)S(1)}, bf16[1,4,2,24,704]{4,3,2,1,0:T(8,128)(2,1)S(1)}, u32[]{:S(2)}, u32[]{:S(2)}) collective-permute-start(bf16[1,4,2,24,704]{4,3,2,1,0:T(8,128)(2,1)S(1)} %arrange.5.refs_0_), channel_id=1, source_target_pairs={{0,16},{16,0},{1,17},{17,1},{2,18},{18,2},{3,19},{19,3},{4,20},{20... | collective-permute-start | bytes 811016 | tf_op jit(solution)/shard_map/ppermute | solution.py:22
  37.8 14.8 %collective-permute-start.6 = (bf16[128,768]{1,0:T(8,128)(2,1)S(1)}, bf16[128,768]{1,0:T(8,128)(2,1)S(1)}, u32[]{:S(2)}, u32[]{:S(2)}) collective-permute-start(bf16[128,768]{1,0:T(8,128)(2,1)S(1)} %bitcast.50), channel_id=1, source_target_pairs={{0,8},{4,12},{8,0},{12,4},{1,9},{5,13},{9,1},{13,5},{2,10},{6,14},... | collective-permute-start | bytes 589832 | tf_op jit(solution)/shard_map/ppermute | solution.py:22
  38.3 14.3 %collective-permute-start.7 = (bf16[128,768]{1,0:T(8,128)(2,1)S(1)}, bf16[128,768]{1,0:T(8,128)(2,1)S(1)}, u32[]{:S(2)}, u32[]{:S(2)}) collective-permute-start(bf16[128,768]{1,0:T(8,128)(2,1)S(1)} %bitcast.51), channel_id=1, source_target_pairs={{0,12},{4,0},{8,4},{12,8},{1,13},{5,1},{9,5},{13,9},{2,14},{6,2},{... | collective-permute-start | bytes 589832 | tf_op jit(solution)/shard_map/ppermute | solution.py:22
  52.7 2.1 collective-permute-start.8
  57.5 11.2 %collective-permute-start.9 = (bf16[512,384]{1,0:T(8,128)(2,1)S(1)}, bf16[512,384]{1,0:T(8,128)(2,1)S(1)}, u32[]{:S(2)}, u32[]{:S(2)}) collective-permute-start(bf16[512,384]{1,0:T(8,128)(2,1)S(1)} %get-tuple-element.91.refs_3_.refs_8_), channel_id=1, source_target_pairs={{0,2},{2,0},{1,3},{3,1},{4,6},{6,4},{5,7},{7,5},{8,10},{10,8},{9,1... | collective-permute-start | bytes 1179656 | tf_op jit(solution)/shard_map/ppermute | solution.py:22
  59.2 10.3 %collective-permute-start.10 = (bf16[512,384]{1,0:T(8,128)(2,1)S(1)}, bf16[512,384]{1,0:T(8,128)(2,1)S(1)}, u32[]{:S(2)}, u32[]{:S(2)}) collective-permute-start(bf16[512,384]{1,0:T(8,128)(2,1)S(1)} %get-tuple-element.91.refs_3_.refs_8_), channel_id=1, source_target_pairs={{0,1},{1,0},{2,3},{3,2},{4,5},{5,4},{6,7},{7,6},{8,9},{9,8},{10,11... | collective-permute-start | bytes 1179656 | tf_op jit(solution)/shard_map/ppermute | solution.py:22
  68.7 1.7 collective-permute-start.11
  75.8 9.0 %collective-permute-start.12 = (bf16[128,192]{1,0:T(8,128)(2,1)S(1)}, bf16[128,192]{1,0:T(8,128)(2,1)S(1)}, u32[]{:S(2)}, u32[]{:S(2)}) collective-permute-start(bf16[128,192]{1,0:T(8,128)(2,1)S(1)} %get-tuple-element.93), channel_id=1, source_target_pairs={{0,4},{4,8},{8,12},{12,0},{1,5},{5,9},{9,13},{13,1},{2,6},{6,10},{... | collective-permute-start | bytes 147464 | tf_op jit(solution)/shard_map/ppermute | solution.py:22
  80.3 9.7 %collective-permute-start.13 = (bf16[128,192]{1,0:T(8,128)(2,1)S(1)}, bf16[128,192]{1,0:T(8,128)(2,1)S(1)}, u32[]{:S(2)}, u32[]{:S(2)}) collective-permute-start(bf16[128,192]{1,0:T(8,128)(2,1)S(1)} %get-tuple-element.94), channel_id=1, source_target_pairs={{0,8},{4,12},{8,0},{12,4},{1,9},{5,13},{9,1},{13,5},{2,10},{6,14},... | collective-permute-start | bytes 147464 | tf_op jit(solution)/shard_map/ppermute | solution.py:22
  81.3 8.8 %collective-permute-start.14 = (bf16[128,192]{1,0:T(8,128)(2,1)S(1)}, bf16[128,192]{1,0:T(8,128)(2,1)S(1)}, u32[]{:S(2)}, u32[]{:S(2)}) collective-permute-start(bf16[128,192]{1,0:T(8,128)(2,1)S(1)} %get-tuple-element.95), channel_id=1, source_target_pairs={{0,12},{4,0},{8,4},{12,8},{1,13},{5,1},{9,5},{13,9},{2,14},{6,2},{... | collective-permute-start | bytes 147464 | tf_op jit(solution)/shard_map/ppermute | solution.py:22
  97.6 2.1 collective-permute-start.18
  101.7 6.9 %collective-permute-start.19 = (bf16[128,768]{1,0:T(8,128)(2,1)S(1)}, bf16[128,768]{1,0:T(8,128)(2,1)S(1)}, u32[]{:S(2)}, u32[]{:S(2)}) collective-permute-start(bf16[128,768]{1,0:T(8,128)(2,1)S(1)} %get-tuple-element.100.refs_0_), channel_id=1, source_target_pairs={{0,2},{2,0},{1,3},{3,1},{4,6},{6,4},{5,7},{7,5},{8,10},{10,8},{9,1... | collective-permute-start | bytes 589832 | tf_op jit(solution)/shard_map/ppermute | solution.py:22
  103.2 5.5 %collective-permute-start.20 = (bf16[128,768]{1,0:T(8,128)(2,1)S(1)}, bf16[128,768]{1,0:T(8,128)(2,1)S(1)}, u32[]{:S(2)}, u32[]{:S(2)}) collective-permute-start(bf16[128,768]{1,0:T(8,128)(2,1)S(1)} %get-tuple-element.100.refs_0_), channel_id=1, source_target_pairs={{0,1},{1,0},{2,3},{3,2},{4,5},{5,4},{6,7},{7,6},{8,9},{9,8},{10,11... | collective-permute-start | bytes 589832 | tf_op jit(solution)/shard_map/ppermute | solution.py:22
  117.6 7.3 %collective-permute-start.23 = (bf16[128,768]{1,0:T(8,128)(2,1)}, bf16[128,768]{1,0:T(8,128)(2,1)}, u32[]{:S(2)}, u32[]{:S(2)}) collective-permute-start(bf16[128,768]{1,0:T(8,128)(2,1)} %get-tuple-element.104), channel_id=1, source_target_pairs={{0,2},{2,0},{1,3},{3,1},{4,6},{6,4},{5,7},{7,5},{8,10},{10,8},{9,1... | collective-permute-start | bytes 589832 | tf_op jit(solution)/shard_map/ppermute | solution.py:22
  129.9 6.1 %collective-permute-start.24 = (bf16[128,768]{1,0:T(8,128)(2,1)S(1)}, bf16[128,768]{1,0:T(8,128)(2,1)S(1)}, u32[]{:S(2)}, u32[]{:S(2)}) collective-permute-start(bf16[128,768]{1,0:T(8,128)(2,1)S(1)} %get-tuple-element.108.refs_0_), channel_id=1, source_target_pairs={{0,2},{2,0},{1,3},{3,1},{4,6},{6,4},{5,7},{7,5},{8,10},{10,8},{9,1... | collective-permute-start | bytes 589832 | tf_op jit(solution)/shard_map/ppermute | solution.py:22
  131.4 4.6 %collective-permute-start.25 = (bf16[128,768]{1,0:T(8,128)(2,1)S(1)}, bf16[128,768]{1,0:T(8,128)(2,1)S(1)}, u32[]{:S(2)}, u32[]{:S(2)}) collective-permute-start(bf16[128,768]{1,0:T(8,128)(2,1)S(1)} %get-tuple-element.108.refs_0_), channel_id=1, source_target_pairs={{0,1},{1,0},{2,3},{3,2},{4,5},{5,4},{6,7},{7,6},{8,9},{9,8},{10,11... | collective-permute-start | bytes 589832 | tf_op jit(solution)/shard_map/ppermute | solution.py:22
  140.3 1.8 collective-permute-start.27
  143.7 28.1 %collective-permute-start.44 = (bf16[384,1536]{1,0:T(8,128)(2,1)S(1)}, bf16[384,1536]{1,0:T(8,128)(2,1)S(1)}, u32[]{:S(2)}, u32[]{:S(2)}) collective-permute-start(bf16[384,1536]{1,0:T(8,128)(2,1)S(1)} %get-tuple-element.151), channel_id=1, source_target_pairs={{0,16},{16,0},{1,17},{17,1},{2,18},{18,2},{3,19},{19,3},{4,20},{20... | collective-permute-start | bytes 3538952 | tf_op jit(solution)/shard_map/ppermute | solution.py:22
  144.3 6.7 %collective-permute-start.28 = (bf16[128,768]{1,0:T(8,128)(2,1)S(1)}, bf16[128,768]{1,0:T(8,128)(2,1)S(1)}, u32[]{:S(2)}, u32[]{:S(2)}) collective-permute-start(bf16[128,768]{1,0:T(8,128)(2,1)S(1)} %get-tuple-element.113), channel_id=1, source_target_pairs={{0,2},{2,0},{1,3},{3,1},{4,6},{6,4},{5,7},{7,5},{8,10},{10,8},{9,1... | collective-permute-start | bytes 589832 | tf_op jit(solution)/shard_map/ppermute | solution.py:22
  154.7 6.4 %collective-permute-start.29 = (bf16[128,192]{1,0:T(8,128)(2,1)S(1)}, bf16[128,192]{1,0:T(8,128)(2,1)S(1)}, u32[]{:S(2)}, u32[]{:S(2)}) collective-permute-start(bf16[128,192]{1,0:T(8,128)(2,1)S(1)} %get-tuple-element.120), channel_id=1, source_target_pairs={{0,4},{4,8},{8,12},{12,0},{1,5},{5,9},{9,13},{13,1},{2,6},{6,10},{... | collective-permute-start | bytes 147464 | tf_op jit(solution)/shard_map/ppermute | solution.py:22
  155.5 7.1 %collective-permute-start.30 = (bf16[128,192]{1,0:T(8,128)(2,1)S(1)}, bf16[128,192]{1,0:T(8,128)(2,1)S(1)}, u32[]{:S(2)}, u32[]{:S(2)}) collective-permute-start(bf16[128,192]{1,0:T(8,128)(2,1)S(1)} %get-tuple-element.121), channel_id=1, source_target_pairs={{0,8},{4,12},{8,0},{12,4},{1,9},{5,13},{9,1},{13,5},{2,10},{6,14},... | collective-permute-start | bytes 147464 | tf_op jit(solution)/shard_map/ppermute | solution.py:22
  156.8 5.8 %collective-permute-start.31 = (bf16[128,192]{1,0:T(8,128)(2,1)S(1)}, bf16[128,192]{1,0:T(8,128)(2,1)S(1)}, u32[]{:S(2)}, u32[]{:S(2)}) collective-permute-start(bf16[128,192]{1,0:T(8,128)(2,1)S(1)} %get-tuple-element.122), channel_id=1, source_target_pairs={{0,12},{4,0},{8,4},{12,8},{1,13},{5,1},{9,5},{13,9},{2,14},{6,2},{... | collective-permute-start | bytes 147464 | tf_op jit(solution)/shard_map/ppermute | solution.py:22
  170.1 3.0 %collective-permute-start.32 = (bf16[2,512,384]{2,1,0:T(8,128)(2,1)}, bf16[2,512,384]{2,1,0:T(8,128)(2,1)S(1)}, u32[]{:S(2)}, u32[]{:S(2)}) collective-permute-start(bf16[2,512,384]{2,1,0:T(8,128)(2,1)} %get-tuple-element.125), channel_id=1, source_target_pairs={{0,1},{1,0},{2,3},{3,2},{4,5},{5,4},{6,7},{7,6},{8,9},{9,8},{10,11... | collective-permute-start | bytes 2359304 | tf_op jit(solution)/shard_map/ppermute | solution.py:22
  176.0 10.9 %collective-permute-start.33 = (bf16[512,384]{1,0:T(8,128)(2,1)}, bf16[512,384]{1,0:T(8,128)(2,1)}, u32[]{:S(2)}, u32[]{:S(2)}) collective-permute-start(bf16[512,384]{1,0:T(8,128)(2,1)} %get-tuple-element.127), channel_id=1, source_target_pairs={{0,2},{2,0},{1,3},{3,1},{4,6},{6,4},{5,7},{7,5},{8,10},{10,8},{9,1... | collective-permute-start | bytes 1179656 | tf_op jit(solution)/shard_map/ppermute | solution.py:22
  193.9 2.9 %collective-permute-start.34 = (bf16[16,24,1536]{2,1,0:T(8,128)(2,1)S(1)}, bf16[16,24,1536]{2,1,0:T(8,128)(2,1)S(1)}, u32[]{:S(2)}, u32[]{:S(2)}) collective-permute-start(bf16[16,24,1536]{2,1,0:T(8,128)(2,1)S(1)} %get-tuple-element.135), channel_id=1, source_target_pairs={{0,1},{1,0},{2,3},{3,2},{4,5},{5,4},{6,7},{7,6},{8,9},{9,8},{10,11... | collective-permute-start | bytes 3538952 | tf_op jit(solution)/shard_map/ppermute | solution.py:22
  197.6 9.1 %collective-permute-start.35 = (bf16[2,4,1,24,768]{4,3,2,1,0:T(8,128)(2,1)S(1)}, bf16[2,4,1,24,768]{4,3,2,1,0:T(8,128)(2,1)S(1)}, u32[]{:S(2)}, u32[]{:S(2)}) collective-permute-start(bf16[2,4,1,24,768]{4,3,2,1,0:T(8,128)(2,1)S(1)} %get-tuple-element.137), channel_id=1, source_target_pairs={{0,2},{2,0},{1,3},{3,1},{4,6},{6,4},{5,7},{7,5},{8,10},{10,8},{9,1... | collective-permute-start | bytes 884744 | tf_op jit(solution)/shard_map/ppermute | solution.py:22
  199.2 8.8 %collective-permute-start.36 = (bf16[1,4,2,24,768]{4,3,2,1,0:T(8,128)(2,1)S(1)}, bf16[1,4,2,24,768]{4,3,2,1,0:T(8,128)(2,1)S(1)}, u32[]{:S(2)}, u32[]{:S(2)}) collective-permute-start(bf16[1,4,2,24,768]{4,3,2,1,0:T(8,128)(2,1)S(1)} %get-tuple-element.139), channel_id=1, source_target_pairs={{0,16},{16,0},{1,17},{17,1},{2,18},{18,2},{3,19},{19,3},{4,20},{20... | collective-permute-start | bytes 884744 | tf_op jit(solution)/shard_map/ppermute | solution.py:22
  200.4 12.4 %collective-permute-start.39 = (bf16[128,768]{1,0:T(8,128)(2,1)S(1)}, bf16[128,768]{1,0:T(8,128)(2,1)S(1)}, u32[]{:S(2)}, u32[]{:S(2)}) collective-permute-start(bf16[128,768]{1,0:T(8,128)(2,1)S(1)} %get-tuple-element.144), channel_id=1, source_target_pairs={{0,8},{4,12},{8,0},{12,4},{1,9},{5,13},{9,1},{13,5},{2,10},{6,14},... | collective-permute-start | bytes 589832 | tf_op jit(solution)/shard_map/ppermute | solution.py:22
  200.9 11.9 %collective-permute-start.40 = (bf16[128,768]{1,0:T(8,128)(2,1)S(1)}, bf16[128,768]{1,0:T(8,128)(2,1)S(1)}, u32[]{:S(2)}, u32[]{:S(2)}) collective-permute-start(bf16[128,768]{1,0:T(8,128)(2,1)S(1)} %get-tuple-element.145), channel_id=1, source_target_pairs={{0,12},{4,0},{8,4},{12,8},{1,13},{5,1},{9,5},{13,9},{2,14},{6,2},{... | collective-permute-start | bytes 589832 | tf_op jit(solution)/shard_map/ppermute | solution.py:22
  208.7 5.2 %collective-permute-start.37 = (bf16[1,4,1,24,768]{4,3,2,1,0:T(8,128)(2,1)S(1)}, bf16[1,4,1,24,768]{4,3,2,1,0:T(8,128)(2,1)S(1)}, u32[]{:S(2)}, u32[]{:S(2)}) collective-permute-start(bf16[1,4,1,24,768]{4,3,2,1,0:T(8,128)(2,1)S(1)} %get-tuple-element.141), channel_id=1, source_target_pairs={{0,16},{16,0},{1,17},{17,1},{2,18},{18,2},{3,19},{19,3},{4,20},{20... | collective-permute-start | bytes 442376 | tf_op jit(solution)/shard_map/ppermute | solution.py:22
  210.0 5.1 %collective-permute-start.38 = (bf16[1,4,1,24,768]{4,3,2,1,0:T(8,128)(2,1)S(1)}, bf16[1,4,1,24,768]{4,3,2,1,0:T(8,128)(2,1)S(1)}, u32[]{:S(2)}, u32[]{:S(2)}) collective-permute-start(bf16[1,4,1,24,768]{4,3,2,1,0:T(8,128)(2,1)S(1)} %get-tuple-element.143), channel_id=1, source_target_pairs={{0,2},{2,0},{1,3},{3,1},{4,6},{6,4},{5,7},{7,5},{8,10},{10,8},{9,1... | collective-permute-start | bytes 442376 | tf_op jit(solution)/shard_map/ppermute | solution.py:22
  210.5 16.8 %collective-permute-start.46 = (bf16[128,768]{1,0:T(8,128)(2,1)}, bf16[128,768]{1,0:T(8,128)(2,1)S(1)}, u32[]{:S(2)}, u32[]{:S(2)}) collective-permute-start(bf16[128,768]{1,0:T(8,128)(2,1)} %get-tuple-element.156), channel_id=1, source_target_pairs={{0,4},{4,8},{8,12},{12,0},{1,5},{5,9},{9,13},{13,1},{2,6},{6,10},{... | collective-permute-start | bytes 589832 | tf_op jit(solution)/shard_map/ppermute | solution.py:22
  215.2 9.9 %collective-permute-start.41 = (bf16[1,1,1,24,1536]{4,3,2,1,0:T(8,128)(2,1)S(1)}, bf16[1,1,1,24,1536]{4,3,2,1,0:T(8,128)(2,1)S(1)}, u32[]{:S(2)}, u32[]{:S(2)}) collective-permute-start(bf16[1,1,1,24,1536]{4,3,2,1,0:T(8,128)(2,1)S(1)} %get-tuple-element.147), channel_id=1, source_target_pairs={{0,4},{4,8},{8,12},{12,0},{1,5},{5,9},{9,13},{13,1},{2,6},{6,10},{... | collective-permute-start | bytes 221192 | tf_op jit(solution)/shard_map/ppermute | solution.py:22
  222.6 7.7 %collective-permute-start.42 = (bf16[1,1,1,24,1536]{4,3,2,1,0:T(8,128)(2,1)S(1)}, bf16[1,1,1,24,1536]{4,3,2,1,0:T(8,128)(2,1)S(1)}, u32[]{:S(2)}, u32[]{:S(2)}) collective-permute-start(bf16[1,1,1,24,1536]{4,3,2,1,0:T(8,128)(2,1)S(1)} %get-tuple-element.148), channel_id=1, source_target_pairs={{0,8},{4,12},{8,0},{12,4},{1,9},{5,13},{9,1},{13,5},{2,10},{6,14},... | collective-permute-start | bytes 221192 | tf_op jit(solution)/shard_map/ppermute | solution.py:22
  222.7 7.7 %collective-permute-start.43 = (bf16[1,1,1,24,1536]{4,3,2,1,0:T(8,128)(2,1)S(1)}, bf16[1,1,1,24,1536]{4,3,2,1,0:T(8,128)(2,1)S(1)}, u32[]{:S(2)}, u32[]{:S(2)}) collective-permute-start(bf16[1,1,1,24,1536]{4,3,2,1,0:T(8,128)(2,1)S(1)} %get-tuple-element.149), channel_id=1, source_target_pairs={{0,12},{4,0},{8,4},{12,8},{1,13},{5,1},{9,5},{13,9},{2,14},{6,2},{... | collective-permute-start | bytes 221192 | tf_op jit(solution)/shard_map/ppermute | solution.py:22
  227.3 3.4 %collective-permute-start.45 = (bf16[24,768]{1,0:T(8,128)(2,1)S(1)}, bf16[24,768]{1,0:T(8,128)(2,1)S(1)}, u32[]{:S(2)}, u32[]{:S(2)}) collective-permute-start(bf16[24,768]{1,0:T(8,128)(2,1)S(1)} %get-tuple-element.153), channel_id=1, source_target_pairs={{0,3},{1,2},{2,1},{3,0},{4,7},{5,6},{6,5},{7,4},{8,11},{9,10},{10,... | collective-permute-start | bytes 110600 | tf_op jit(solution)/shard_map/ppermute | solution.py:872
  228.5 6.0 %collective-permute-start.47 = (bf16[24,768]{1,0:T(8,128)(2,1)S(1)}, bf16[24,768]{1,0:T(8,128)(2,1)S(1)}, u32[]{:S(2)}, u32[]{:S(2)}) collective-permute-start(bf16[24,768]{1,0:T(8,128)(2,1)S(1)} %get-tuple-element.161), channel_id=1, source_target_pairs={{0,2},{1,3},{2,0},{3,1},{4,6},{5,7},{6,4},{7,5},{8,10},{9,11},{10,... | collective-permute-start | bytes 110600 | tf_op jit(solution)/shard_map/ppermute | solution.py:872
  229.1 5.4 %collective-permute-start.48 = (bf16[24,768]{1,0:T(8,128)(2,1)S(1)}, bf16[24,768]{1,0:T(8,128)(2,1)S(1)}, u32[]{:S(2)}, u32[]{:S(2)}) collective-permute-start(bf16[24,768]{1,0:T(8,128)(2,1)S(1)} %get-tuple-element.162), channel_id=1, source_target_pairs={{0,1},{1,0},{2,3},{3,2},{4,5},{5,4},{6,7},{7,6},{8,9},{9,8},{10,11... | collective-permute-start | bytes 110600 | tf_op jit(solution)/shard_map/ppermute | solution.py:872
  (78 other events, 637.2 us)
Sparse Core Ops, SparseCore 0:
  18.8 75.9 all-gather.1
  173.3 27.5 reduce-scatter.1
